TPU v7x, 32 devices: a whole 2x2x4 slice. The times are simulated.
32 devices in a mesh: dp: 16 (over z, y, x), ep: 2 (over core).
Axes of the slice: x: 2, y: 2, z: 4, core: 2. Of those that a mesh axis runs over, the one named last changes fastest.
Arguments:
- residual: bfloat16 [256, 7168], P(('dp', 'ep')), may hold values from -6 to 6
- queries: bfloat16 [256, 36864], P('dp', 'ep'), may hold values from -57 to 57
- latent_cache: bfloat16 [256, 36864], P('dp'), may hold values from -6 to 6
- lengths: int32 [256], P('dp'), may hold values from 2 to 64, as said below
- destination: int32 [256], replicated, may hold values from 0 to 255, as said below
- w_uv: bfloat16 [64, 512, 128], P('ep'), may hold values from -0.25 to 0.25
- w_o: bfloat16 [8192, 7168], P('ep'), may hold values from -0.0625 to 0.0625
- norm_gain: float32 [7168], replicated, may hold values from 0.1 to 1.9
- experts: int32 [256, 8], P(('dp', 'ep')), may hold values from 0 to 15, all different within a row; in each aligned block of 8 rows (0 to 7, 8 to 15, ...) at most 8 rows name the same one
- gate_weights: float32 [256, 8], P(('dp', 'ep')), may hold values from 0.05 to 0.5
- w_gate: bfloat16 [16, 7168, 1024], P('dp', None, 'ep'), may hold values from -0.0625 to 0.0625
- w_up: bfloat16 [16, 7168, 1024], P('dp', None, 'ep'), may hold values from -0.0625 to 0.0625
- w_down: bfloat16 [16, 1024, 7168], P('dp', 'ep'), may hold values from -0.1875 to 0.1875
Outputs:
- layer_out: bfloat16 [256, 7168], P(('dp', 'ep'))
- arrivals: bfloat16 [64, 36864], P('dp')
Inputs may be any that keep to these rules, and one draw needn't show every extreme that they name: `destination`: A permutation. A slot whose entry differs from its index sends its request to a slot of another replica (block of 16 slots); the slots that are left are exactly the slots that are taken. At most 4 requests leave one replica, and in some replica exactly 4. `lengths`: every replica holds a request of length 64. Each row names 8 different experts. Among the rows of one device of dp+ep no expert is named more than 8 times, a bound that some block reaches.
All inputs are finite; a program needn't handle non-finite values.
Results may differ from a plain program's by a relative error of at most 0.0055.
Values may be sent and summed in bfloat16 or wider, within the bound.
No kernel may reach another device: no remote copies, remote signals or barrier semaphores. Data moves between devices by JAX's collectives and lax.ppermute only.
A program may use at most 192 MiB of HBM per device.

v0:
```python
import jax
import jax.numpy as jnp
from jax import lax
from jax.sharding import PartitionSpec as P

LAT = 512
KV = 576
V_DIM = 128
MOVE_MAX = 4
CTX = 64


score_scale = 192.0 ** (-0.5)
norm_eps = 1e-06


def one_hot_rows(wanted, row_count):
    return (wanted[:, None] == jnp.arange(row_count, dtype=jnp.int32)[None, :]).astype(jnp.bfloat16)


def expert_rows(flat_rows, w_gate, w_up, w_down):
    gate_part = jnp.dot(flat_rows, w_gate[0], preferred_element_type=jnp.float32)
    up_part = jnp.dot(flat_rows, w_up[0], preferred_element_type=jnp.float32)
    activated = (jax.nn.silu(gate_part) * up_part).astype(jnp.bfloat16)
    return jnp.dot(activated, w_down[0], preferred_element_type=jnp.float32)


def per_device(
    residual,
    queries,
    latent_cache,
    lengths,
    destination,
    w_uv,
    w_o,
    norm_gain,
    experts,
    gate_weights,
    w_gate,
    w_up,
    w_down,
):
    replica_rows = latent_cache.shape[0]
    all_slots = destination.shape[0]
    replicas = all_slots // replica_rows
    own_replica = lax.axis_index("dp")
    slot_ids = jnp.arange(all_slots, dtype=jnp.int32)
    anchor = jnp.zeros((all_slots,), jnp.int32).at[destination].set(slot_ids)
    leaving = destination // replica_rows != slot_ids // replica_rows
    leave_grid = leaving.reshape(replicas, replica_rows).astype(jnp.int32)
    leave_rank = (jnp.cumsum(leave_grid, axis=1) - 1).reshape(all_slots)
    outbox_slot = slot_ids // replica_rows * MOVE_MAX + leave_rank
    own_leave = lax.dynamic_slice_in_dim(leaving, own_replica * replica_rows, replica_rows)
    own_rank = lax.dynamic_slice_in_dim(leave_rank, own_replica * replica_rows, replica_rows)
    my_anchor = lax.dynamic_slice_in_dim(anchor, own_replica * replica_rows, replica_rows)
    box_ids = jnp.arange(MOVE_MAX, dtype=jnp.int32)
    hit_grid = (own_rank[None, :] == box_ids[:, None]) & own_leave[None, :]
    packing = hit_grid.astype(jnp.bfloat16)
    source_box = outbox_slot[my_anchor]
    wanted = jnp.sum(jnp.where(hit_grid, source_box[None, :], 0), axis=1) + jnp.where(
        jnp.any(hit_grid, axis=1), 0, -1
    )
    outbox = jnp.dot(packing, latent_cache, preferred_element_type=jnp.float32).astype(jnp.bfloat16)
    portion = lax.all_gather(outbox, "dp", axis=0, tiled=True)
    picker = one_hot_rows(wanted, portion.shape[0])
    landed = jnp.dot(picker, portion, preferred_element_type=jnp.float32)
    arrivals = landed.astype(jnp.bfloat16)
    spread = (own_leave[:, None] & (own_rank[:, None] == box_ids[None, :])).astype(jnp.bfloat16)
    fetched = jnp.dot(spread, arrivals, preferred_element_type=jnp.float32).astype(jnp.bfloat16)
    present = jnp.where(own_leave[:, None], fetched, latent_cache)
    heads_dev = w_uv.shape[0]
    latents = present.reshape(replica_rows, CTX, KV)
    query_rows = queries.reshape(replica_rows, heads_dev, KV)
    scores = (
        jnp.einsum("rhk,rtk->rht", query_rows, latents, preferred_element_type=jnp.float32)
        * score_scale
    )
    in_range = jnp.arange(CTX, dtype=jnp.int32)[None, None, :] < lengths[:, None, None]
    scores = jnp.where(in_range, scores, -jnp.inf)
    row_max = jnp.max(scores, axis=2, keepdims=True)
    weights = jnp.where(in_range, jnp.exp(scores - row_max), 0.0)
    prob_rows = (weights / jnp.sum(weights, axis=2, keepdims=True)).astype(jnp.bfloat16)
    context = jnp.einsum(
        "rht,rtl->rhl", prob_rows, latents[:, :, :LAT], preferred_element_type=jnp.float32
    ).astype(jnp.bfloat16)
    values = jnp.einsum("rhl,hlv->rhv", context, w_uv, preferred_element_type=jnp.float32).astype(
        jnp.bfloat16
    )
    values = values.reshape(replica_rows, heads_dev * V_DIM)
    tok_rows = residual.shape[0]
    width = residual.shape[1]
    attended = lax.psum_scatter(
        jnp.dot(values, w_o, preferred_element_type=jnp.float32),
        "ep",
        scatter_dimension=0,
        tiled=True,
    )
    hidden = residual.astype(jnp.float32) + attended
    normed = (
        hidden * lax.rsqrt(jnp.mean(hidden * hidden, axis=1, keepdims=True) + norm_eps) * norm_gain
    ).astype(jnp.bfloat16)
    expert_ids = jnp.arange(replicas, dtype=jnp.int32)
    matches = experts[:, :, None] == expert_ids[None, None, :]
    routed = jnp.any(matches, axis=1)
    gate_sum = jnp.sum(jnp.where(matches, gate_weights[:, :, None], 0.0), axis=1)
    place_rank = jnp.cumsum(routed.astype(jnp.int32), axis=0) - 1
    seat_ids = jnp.arange(tok_rows, dtype=jnp.int32)
    placement = jnp.transpose(routed)[:, None, :] & (
        jnp.transpose(place_rank)[:, None, :] == seat_ids[None, :, None]
    )
    outgoing = jnp.einsum(
        "ect,td->ecd", placement.astype(jnp.bfloat16), normed, preferred_element_type=jnp.float32
    ).astype(jnp.bfloat16)
    ep_count = lax.axis_size("ep")
    copies = jnp.broadcast_to(outgoing[:, None], (replicas, ep_count, tok_rows, width)).reshape(
        replicas * ep_count, tok_rows, width
    )
    received = lax.all_to_all(copies, ("dp", "ep"), split_axis=0, concat_axis=0, tiled=True)
    flat_rows = received.reshape(-1, received.shape[2])
    served_rows = expert_rows(flat_rows, w_gate, w_up, w_down).astype(jnp.bfloat16)
    served = served_rows.reshape(received.shape[0], received.shape[1], received.shape[2])
    returned = lax.all_to_all(served, ("dp", "ep"), split_axis=0, concat_axis=0, tiled=True)
    summed = jnp.sum(
        returned.reshape(replicas, ep_count, tok_rows, width).astype(jnp.float32), axis=1
    )
    expert_out = summed.astype(jnp.bfloat16)
    blended = jnp.where(placement, jnp.transpose(gate_sum)[:, None, :], 0.0)
    mixture = jnp.einsum(
        "ect,ecd->td", blended, expert_out.astype(jnp.float32), precision=lax.Precision.HIGHEST
    )
    layer_out = (hidden + mixture).astype(jnp.bfloat16)
    return (layer_out, arrivals)


def solution(mesh):
    in_specs = (
        P(("dp", "ep"), None),
        P("dp", "ep"),
        P("dp", None),
        P("dp"),
        P(),
        P("ep", None, None),
        P("ep", None),
        P(),
        P(("dp", "ep"), None),
        P(("dp", "ep"), None),
        P("dp", None, "ep"),
        P("dp", None, "ep"),
        P("dp", "ep", None),
    )
    out_specs = (P(("dp", "ep"), None), P("dp", None))
    return jax.shard_map(
        per_device, mesh=mesh, in_specs=in_specs, out_specs=out_specs, check_vma=False
    )
```

profile of v0, /device:TPU:0, one launch (start us, length us, event | category | flops | bytes accessed | tf_op | source)
XLA Modules:
  0.0 346.5 jit_solution(6635209056670955523)
XLA Ops:
  7.2 0.7 fusion.71
  8.0 0.2 reduce_window_sum.22
  8.4 2.3 fusion.2
  10.8 1.8 reshape.82
  12.6 0.7 add_select_fusion
  13.3 1.4 scatter_custom_fusion
  14.8 0.7 gather_fusion
  15.5 0.1 fusion.69
  15.6 0.1 select_reduce_fusion.1
  15.7 0.7 iota_compare_fusion.3
  16.4 78.1 %all-gather.3.cloned.1.call-done = bf16[16,4,36864]{2,1,0:T(4,128)(2,1)} async-done(((bf16[1,4,36864]{2,1,0:T(4,128)(2,1)}), bf16[16,4,36864]{2,1,0:T(4,128)(2,1)}) %all-gather.3.cloned.1.call-update) | async-done | bytes 4718608 | tf_op jit(solution)/shard_map/all_gather | solution.py:64
  94.6 7.4 %reshape.108 = bf16[64,36864]{1,0:T(8,128)(2,1)} reshape(bf16[16,4,36864]{2,1,0:T(4,128)(2,1)} %all-gather.3.cloned.1.call-done) | data formatting | bytes 9437184
  101.9 3.2 convolution_convert_fusion.1
  105.1 0.5 fusion.1
  105.7 1.6 reshape.81
  107.3 0.5 fusion.28
  107.9 0.2 fusion.73
  108.1 1.0 convolution_convert_fusion.5
  109.1 3.1 fusion.29
  112.2 20.8 %fusion.42 = f32[16,7168]{1,0:T(8,128)} fusion(bf16[4096,7168]{1,0:T(8,128)(2,1)} %param.19, bf16[32,2,8,128]{3,2,1,0:T(8,128)(2,1)S(1)} %fusion.29), kind=kOutput, calls=%fused_computation.46 | convolution fusion | flops 939524096 | bytes 59310080 | tf_op jit(solution)/shard_map/dot_general | solution.py:93
  133.3 6.4 %reduce-scatter.2.cloned.1.call-done = f32[8,7168]{1,0:T(8,128)} async-done(((f32[16,7168]{1,0:T(8,128)}), f32[8,7168]{1,0:T(8,128)}) %reduce-scatter.2.cloned.1.call-update) | async-done | bytes 229392 | tf_op jit(solution)/shard_map/reduce_scatter | solution.py:92
  139.7 1.1 multiply_reduce_fusion
  140.9 1.8 convolution_convert_fusion.4
  142.6 0.5 broadcast_in_dim.122
  143.1 88.5 %all_to_all.10 = bf16[32,8,7168]{2,1,0:T(8,128)(2,1)S(1)} all-to-all(bf16[32,8,7168]{2,1,0:T(8,128)(2,1)S(1)} %bitcast.64), channel_id=1, replica_groups=mesh['dp'=16,'ep'=2] {'dp','ep'}, dimensions={0} | all-to-all | bytes 7340032 | tf_op jit(solution)/shard_map/all_to_all | solution.py:118
  231.6 1.8 copy-done.1
  233.5 2.0 fusion.9
  235.5 12.1 %fusion.3 = bf16[32,8,7168]{2,1,0:T(8,128)(2,1)} fusion(bf16[1,512,7168]{2,1,0:T(8,128)(2,1)} %param.25, bf16[1,7168,512]{2,1,0:T(8,128)(2,1)} %param.24, bf16[32,8,7168]{2,1,0:T(8,128)(2,1)} %copy-done.1, f32[256,512]{1,0:T(8,128)S(1)} %fusion.9), kind=kOutput, calls=%fused_computation.9 | convolution fusion | flops 3760717824 | bytes 22544384 | tf_op jit(solution)/shard_map/dot_general | solution.py:25
  247.6 3.7 %all-to-all-start.1 = ((bf16[32,8,7168]{2,1,0:T(8,128)(2,1)}), bf16[32,8,7168]{2,1,0:T(8,128)(2,1)}, u32[]{:S(2)}, u32[]{:S(2)}) async-start(bf16[32,8,7168]{2,1,0:T(8,128)(2,1)} %fusion.3), calls=%async_computation.2 | async-start | bytes 7340032 | tf_op jit(solution)/shard_map/all_to_all | solution.py:122
  251.4 82.6 %all-to-all-done.1 = bf16[32,8,7168]{2,1,0:T(8,128)(2,1)} async-done(((bf16[32,8,7168]{2,1,0:T(8,128)(2,1)}), bf16[32,8,7168]{2,1,0:T(8,128)(2,1)}, u32[]{:S(2)}, u32[]{:S(2)}) %all-to-all-start.1) | async-done | bytes 3670048 | tf_op jit(solution)/shard_map/all_to_all | solution.py:122
  334.0 2.6 bitcast_reduce_fusion
  336.7 3.0 fusion.5
  (42 shorter events, 0.9 us)
Async XLA Ops:
  7.2 87.4 %all-gather.3.cloned.1.call-start = ((), (), s32[]{:S(2)}) async-start(), calls=%async_computation.4 | async-start | bytes 5013504 | tf_op jit(solution)/shard_map/all_gather | solution.py:64
  10.7 129.0 %reduce-scatter.2.cloned.1.call-start = ((), (), s32[]{:S(2)}) async-start(), calls=%async_computation.3 | async-start | bytes 688128 | tf_op jit(solution)/shard_map/reduce_scatter | solution.py:92
  101.9 3.2 copy-start
  105.1 2.7 copy-start.2
  112.2 20.9 %copy-start.6 = (s32[8,8]{1,0:T(8,128)S(1)}, s32[8,8]{1,0:T(8,128)}, u32[]{:S(2)}) copy-start(s32[8,8]{1,0:T(8,128)} %param.21) | copy-start | bytes 772
  112.2 27.5 %copy-start.4 = (bf16[8,7168]{1,0:T(8,128)(2,1)S(1)}, bf16[8,7168]{1,0:T(8,128)(2,1)}, u32[]{:S(2)}) copy-start(bf16[8,7168]{1,0:T(8,128)(2,1)} %param.13) | copy-start | bytes 344068
  112.2 28.6 %copy-start.5 = (f32[7168]{0:T(1024)S(1)}, f32[7168]{0:T(1024)}, u32[]{:S(2)}) copy-start(f32[7168]{0:T(1024)} %param.20) | copy-start | bytes 86020
  140.8 92.6 %slice-start = ((s8[7340032]{0:T(1024)(128)(4,1)}), s8[4194304]{0:T(1024)(128)(4,1)S(1)}, s32[]{:S(2)}) async-start(s8[7340032]{0:T(1024)(128)(4,1)} %bitcast.68), calls=%async_computation.5 | async-start | bytes 8388608
  142.6 90.8 %slice-start.1 = ((s8[7340032]{0:T(1024)(128)(4,1)}), s8[3145728]{0:T(1024)(128)(4,1)S(1)}, s32[]{:S(2)}) async-start(s8[7340032]{0:T(1024)(128)(4,1)} %bitcast.68), calls=%async_computation.6 | async-start | bytes 6291456
  231.6 1.8 copy-start.1
  247.6 3.7 %copy-start.7 = (f32[8,8]{1,0:T(8,128)S(1)}, f32[8,8]{1,0:T(8,128)}, u32[]{:S(2)}) copy-start(f32[8,8]{1,0:T(8,128)} %param.22) | copy-start | bytes 772
  247.6 86.4 %all-to-all-start.1 = ((bf16[32,8,7168]{2,1,0:T(8,128)(2,1)}), bf16[32,8,7168]{2,1,0:T(8,128)(2,1)}, u32[]{:S(2)}, u32[]{:S(2)}) async-start(bf16[32,8,7168]{2,1,0:T(8,128)(2,1)} %fusion.3), calls=%async_computation.2 | async-start | bytes 7340032 | tf_op jit(solution)/shard_map/all_to_all | solution.py:122
  251.3 85.4 %copy-start.3 = (f32[8,7168]{1,0:T(8,128)S(1)}, f32[8,7168]{1,0:T(8,128)}, u32[]{:S(2)}) copy-start(f32[8,7168]{1,0:T(8,128)} %reduce-scatter.2.cloned.1.call-done) | copy-start | bytes 688132
Sparse Core Ops, SparseCore 0:
  11.4 83.1 all-gather.2
  133.2 6.4 reduce-scatter.1
where the time goes:
time: 347 us
  waiting for transfers between devices  167 us (48%)
  blocking collectives  88.5 us (26%)
  matrix products  50.3 us (14%)
  local copies, waits for them, and re-layouts  15.6 us (4%)
  between operations  14.3 us (4%)
  other arithmetic  6.85 us (2%)
  starting transfers between devices  3.75 us (1%)
    all_to_all x1, blocking collectives, per_device(): lax.all_to_all(copies, ('dp', 'ep'), split_axis=0, concat_axis=0, tiled=T...  88.5 us
    all_to_all x1, waiting for transfers between devices, per_device(): lax.all_to_all(served, ('dp', 'ep'), split_axis=0, concat_axis=0, tiled=T...  82.6 us
    all_gather x1, waiting for transfers between devices, per_device(): portion = lax.all_gather(outbox, 'dp', axis=0, tiled=True)  78.1 us
    dot_general x1, matrix products, per_device(): jnp.dot(values, w_o, preferred_element_type=jnp.float32)  20.8 us
    dot_general x1, matrix products, expert_rows(): return jnp.dot(activated, w_down[0], preferred_element_type=jnp.float32)  12.1 us
    unnamed x21, local copies, waits for them, and re-layouts  9.24 us
  transfers between devices with their start and end apart: 3, of which 3 were waited for; matrix products, arithmetic and copies ran while one was open for 2% of the time, Pallas kernels for 0%

commit v1 on v0

v1 whole, which is shorter than its diff:
```python
import jax
import jax.numpy as jnp
from jax import lax
from jax.sharding import PartitionSpec as P

LAT = 512
KV = 576
V_DIM = 128
MOVE_MAX = 4
CTX = 64
GATE_COLS = 128


score_scale = 192.0 ** (-0.5)
norm_eps = 1e-06


def flip(x, axis, bit):
    pairs = [(i, i ^ bit) for i in range(lax.axis_size(axis))]
    return lax.ppermute(x, axis, pairs)


def bits_of(axis):
    size = lax.axis_size(axis)
    return [1 << b for b in range(size.bit_length() - 1)]


def expert_rows(flat_rows, w_gate, w_up, w_down):
    gate_part = jnp.dot(flat_rows, w_gate[0], preferred_element_type=jnp.float32)
    up_part = jnp.dot(flat_rows, w_up[0], preferred_element_type=jnp.float32)
    activated = (jax.nn.silu(gate_part) * up_part).astype(jnp.bfloat16)
    return jnp.dot(activated, w_down[0], preferred_element_type=jnp.float32)


def moves(destination, replica_rows):
    slots = destination.shape[0]
    replicas = slots // replica_rows
    ids = jnp.arange(slots, dtype=jnp.int32)
    home = ids // replica_rows
    leaving = destination // replica_rows != home
    earlier = (home[:, None] == home[None, :]) & (ids[:, None] < ids[None, :])
    rank = jnp.sum(jnp.where(earlier & leaving[:, None], 1, 0), axis=0)
    box = jnp.where(leaving, home * MOVE_MAX + rank, -1)
    boxes = jnp.arange(replicas * MOVE_MAX, dtype=jnp.int32)
    to_box = (boxes[:, None] == box[None, :]).astype(jnp.bfloat16)
    lands = (ids[:, None] == destination[None, :]).astype(jnp.bfloat16)
    target = jnp.dot(to_box, lands, preferred_element_type=jnp.float32).astype(jnp.bfloat16)
    picker = lax.dot_general(
        target, to_box, (((1,), (1,)), ((), ())), preferred_element_type=jnp.float32
    ).astype(jnp.bfloat16)
    return to_box, picker


def migrate(packing, picker, latent_cache):
    replicas = lax.axis_size("dp")
    ep_count = lax.axis_size("ep")
    width = latent_cache.shape[1] // ep_count
    share = width // replicas
    own = lax.dynamic_slice_in_dim(latent_cache, lax.axis_index("ep") * width, width, axis=1)
    outbox = jnp.dot(packing, own, preferred_element_type=jnp.float32).astype(jnp.bfloat16)
    outbox = outbox.reshape(MOVE_MAX, replicas, share).transpose(1, 0, 2)
    met = lax.all_to_all(outbox, "dp", split_axis=0, concat_axis=0)
    sorted_rows = jnp.dot(
        picker, met.reshape(replicas * MOVE_MAX, share), preferred_element_type=jnp.float32
    ).astype(jnp.bfloat16)
    taken = lax.all_to_all(
        sorted_rows.reshape(replicas, MOVE_MAX, share), "dp", split_axis=0, concat_axis=0
    )
    part = taken.transpose(1, 0, 2).reshape(MOVE_MAX, width)
    return lax.all_gather(part, "ep", axis=1, tiled=True)


def gather_rows(rows):
    bits = bits_of("dp")
    last = bits[:2]
    held = rows[None]
    for bit in bits[2:]:
        held = jnp.concatenate([held, flip(held, "dp", bit)], axis=0)
    half = rows.shape[1] // 2 // 128 * 128
    parts = [held[:, :, :half], held[:, :, half:]]
    orders = [last[::-1], last]
    for step in range(len(last)):
        parts = [
            jnp.concatenate([part, flip(part, "dp", order[step])], axis=0)
            for part, order in zip(parts, orders)
        ]
    blocks = parts[0].shape[0] // 4
    second = parts[1].reshape((2, 2, blocks) + parts[1].shape[1:])
    parts[1] = jnp.swapaxes(second, 0, 1).reshape(parts[1].shape)
    held = jnp.concatenate(parts, axis=2)
    for bit in bits_of("ep"):
        held = jnp.concatenate([held, flip(held, "ep", bit)], axis=0)
    return held


def add_up(kept, came):
    return (kept.astype(jnp.float32) + came.astype(jnp.float32)).astype(jnp.bfloat16)


def scatter_sums(blocks):
    for bit in bits_of("ep")[::-1]:
        near, far = jnp.split(blocks, 2, axis=0)
        blocks = add_up(near, flip(far, "ep", bit))
    bits = bits_of("dp")
    last = bits[:2]
    half = blocks.shape[2] // 2 // 128 * 128
    parts = [blocks[:, :, :half], blocks[:, :, half:]]
    size = parts[1].shape[0] // 4
    second = parts[1].reshape((2, 2, size) + parts[1].shape[1:])
    parts[1] = jnp.swapaxes(second, 0, 1).reshape(parts[1].shape)
    orders = [last, last[::-1]]
    for step in range(len(last)):
        split = [jnp.split(part, 2, axis=0) for part in parts]
        parts = [
            add_up(near, flip(far, "dp", order[step])) for (near, far), order in zip(split, orders)
        ]
    blocks = jnp.concatenate(parts, axis=2)
    rest = bits[2:]
    for bit in rest[:0:-1]:
        near, far = jnp.split(blocks, 2, axis=0)
        blocks = add_up(near, flip(far, "dp", bit))
    near, far = jnp.split(blocks, 2, axis=0)
    came = flip(far, "dp", rest[0])
    return near[0].astype(jnp.float32) + came[0].astype(jnp.float32)


def head_sums(part):
    if lax.axis_size("ep") != 2:
        return lax.psum_scatter(part, "ep", scatter_dimension=0, tiled=True)
    rows = part.shape[0] // 2
    own = lax.axis_index("ep")
    mine = lax.dynamic_slice_in_dim(part, own * rows, rows)
    other = lax.dynamic_slice_in_dim(part, (1 - own) * rows, rows)
    return mine + flip(other, "ep", 1)


def per_device(
    residual,
    queries,
    latent_cache,
    lengths,
    destination,
    w_uv,
    w_o,
    norm_gain,
    experts,
    gate_weights,
    w_gate,
    w_up,
    w_down,
):
    replica_rows = latent_cache.shape[0]
    replicas = destination.shape[0] // replica_rows
    own_replica = lax.axis_index("dp")
    to_box, picker = moves(destination, replica_rows)
    packing = lax.dynamic_slice(
        to_box, (own_replica * MOVE_MAX, own_replica * replica_rows), (MOVE_MAX, replica_rows)
    )
    arrivals = migrate(packing, picker, latent_cache)
    own_leave = jnp.sum(packing.astype(jnp.float32), axis=0) > 0
    fetched = lax.dot_general(
        packing, arrivals, (((0,), (0,)), ((), ())), preferred_element_type=jnp.float32
    ).astype(jnp.bfloat16)
    present = jnp.where(own_leave[:, None], fetched, latent_cache)
    heads_dev = w_uv.shape[0]
    latents = present.reshape(replica_rows, CTX, KV)
    query_rows = queries.reshape(replica_rows, heads_dev, KV)
    scores = (
        jnp.einsum("rhk,rtk->rht", query_rows, latents, preferred_element_type=jnp.float32)
        * score_scale
    )
    in_range = jnp.arange(CTX, dtype=jnp.int32)[None, None, :] < lengths[:, None, None]
    scores = jnp.where(in_range, scores, -jnp.inf)
    row_max = jnp.max(scores, axis=2, keepdims=True)
    weights = jnp.where(in_range, jnp.exp(scores - row_max), 0.0)
    prob_rows = (weights / jnp.sum(weights, axis=2, keepdims=True)).astype(jnp.bfloat16)
    context = jnp.einsum(
        "rht,rtl->rhl", prob_rows, latents[:, :, :LAT], preferred_element_type=jnp.float32
    ).astype(jnp.bfloat16)
    values = jnp.einsum("rhl,hlv->rhv", context, w_uv, preferred_element_type=jnp.float32).astype(
        jnp.bfloat16
    )
    values = values.reshape(replica_rows, heads_dev * V_DIM)
    width = residual.shape[1]
    attended = head_sums(jnp.dot(values, w_o, preferred_element_type=jnp.float32))
    hidden = residual.astype(jnp.float32) + attended
    normed = (
        hidden * lax.rsqrt(jnp.mean(hidden * hidden, axis=1, keepdims=True) + norm_eps) * norm_gain
    ).astype(jnp.bfloat16)
    expert_ids = jnp.arange(replicas, dtype=jnp.int32)
    matches = experts[:, :, None] == expert_ids[None, None, :]
    gate_sum = jnp.sum(jnp.where(matches, gate_weights[:, :, None], 0.0), axis=1)
    terms = []
    left = gate_sum
    for _ in range(3):
        term = lax.reduce_precision(left, 8, 7)
        terms.append(term.astype(jnp.bfloat16))
        left = left - term
    terms.append(jnp.zeros((gate_sum.shape[0], GATE_COLS - 3 * replicas), jnp.bfloat16))
    gathered = gather_rows(jnp.concatenate([normed] + terms, axis=1))
    flat = gathered.reshape(-1, width + GATE_COLS)
    chosen = (jnp.arange(GATE_COLS, dtype=jnp.int32) % replicas == own_replica).astype(jnp.float32)
    gates = jnp.sum(flat[:, width:].astype(jnp.float32) * chosen[None, :], axis=1)
    served = expert_rows(flat[:, :width], w_gate, w_up, w_down) * gates[:, None]
    mixture = scatter_sums(served.astype(jnp.bfloat16).reshape(gathered.shape[:2] + (width,)))
    layer_out = (hidden + mixture).astype(jnp.bfloat16)
    return (layer_out, arrivals)


def solution(mesh):
    in_specs = (
        P(("dp", "ep"), None),
        P("dp", "ep"),
        P("dp", None),
        P("dp"),
        P(),
        P("ep", None, None),
        P("ep", None),
        P(),
        P(("dp", "ep"), None),
        P(("dp", "ep"), None),
        P("dp", None, "ep"),
        P("dp", None, "ep"),
        P("dp", "ep", None),
    )
    out_specs = (P(("dp", "ep"), None), P("dp", None))
    return jax.shard_map(
        per_device, mesh=mesh, in_specs=in_specs, out_specs=out_specs, check_vma=False
    )
```

time: 347 us -> 171 us (0.49)
  blocking collectives: 88.5 us -> 2 us
  waiting for transfers between devices: 167 us -> 82.5 us
  starting transfers between devices: 3.75 us -> 22.7 us
  between operations: 14.3 us -> 1.03 us
  matrix products: 50.3 us -> 43.2 us
  local copies, waits for them, and re-layouts: 15.6 us -> 8.88 us
    all_to_all x1 -> x0, blocking collectives: 88.5 us -> none  [per_device(): lax.all_to_all(copies, ('dp', 'ep'), split_axis=0, concat_axis=0, tiled=T...]
    all_gather x1 -> x0, waiting for transfers between devices: 78.1 us -> none  [per_device(): portion = lax.all_gather(outbox, 'dp', axis=0, tiled=True)]
    all_to_all x1 -> x2, waiting for transfers between devices: 82.6 us -> 12.1 us  [the longest x1 6.89 us: migrate(): met = lax.all_to_all(outbox, 'dp', split_axis=0, concat_axis=0)]
    ppermute x0 -> x15, waiting for transfers between devices: none -> 70.3 us  [flip(): return lax.ppermute(x, axis, pairs)]
    ppermute x0 -> x15, starting transfers between devices: none -> 10.9 us  [flip(): return lax.ppermute(x, axis, pairs)]
    all_to_all x1 -> x2, starting transfers between devices: 3.67 us -> 11.8 us  [the longest x1 8.31 us: migrate(): met = lax.all_to_all(outbox, 'dp', split_axis=0, concat_axis=0)]
    dot_general x6 -> x5, matrix products: 12.8 us -> 5.73 us  [the longest x1 2.04 us: expert_rows(): up_part = jnp.dot(flat_rows, w_up[0], preferred_element_type=jnp.float32)]
    unnamed x21 -> x19, local copies, waits for them, and re-layouts: 9.24 us -> 2.45 us
  transfers between devices with their start and end apart: 3 -> 17, of which waited for: 3 -> 15; matrix products, arithmetic and copies ran while one was open for 2% -> 3% of each run, Pallas kernels for 0% -> 0%
where the time goes in v1:
time: 171 us
  waiting for transfers between devices  82.5 us (48%)
  matrix products  43.2 us (25%)
  starting transfers between devices  22.7 us (13%)
  other arithmetic  10.3 us (6%)
  local copies, waits for them, and re-layouts  8.88 us (5%)
  blocking collectives  2 us (1%)
    ppermute x15, waiting for transfers between devices, flip(): return lax.ppermute(x, axis, pairs)  70.3 us
    dot_general x1, matrix products, per_device(): jnp.dot(values, w_o, preferred_element_type=jnp.float32)  20.7 us
    dot_general x1, matrix products, expert_rows(): return jnp.dot(activated, w_down[0], preferred_element_type=jnp.float32)  12.2 us
    ppermute x15, starting transfers between devices, flip(): return lax.ppermute(x, axis, pairs)  10.9 us
    all_to_all x1, starting transfers between devices, migrate(): met = lax.all_to_all(outbox, 'dp', split_axis=0, concat_axis=0)  8.31 us
    all_to_all x1, waiting for transfers between devices, migrate(): met = lax.all_to_all(outbox, 'dp', split_axis=0, concat_axis=0)  6.89 us
    all_to_all x1, waiting for transfers between devices, migrate(): lax.all_to_all(sorted_rows.reshape(replicas, MOVE_MAX, share), 'dp', spli...  5.25 us
    reshape x1, other arithmetic, per_device(): flat = gathered.reshape(-1, width + GATE_COLS)  5.14 us
  transfers between devices with their start and end apart: 17, of which 15 were waited for; matrix products, arithmetic and copies ran while one was open for 3% of the time, Pallas kernels for 0%

profile of v1, /device:TPU:0, one launch (start us, length us, event | category | flops | bytes accessed | tf_op | source)
XLA Modules:
  0.0 170.6 jit_solution(10306701676882875231)
XLA Ops:
  2.4 1.9 %convolution_convert_fusion.1 = bf16[4,18432]{1,0:T(4,128)(2,1)} fusion(pred[4,16]{1,0:T(4,128)(4,1)S(1)} %get-tuple-element.5, bf16[16,36864]{1,0:T(8,128)(2,1)} %param.15, s32[]{:T(128)S(6)} %select_n.78), kind=kOutput, calls=%fused_computation.3 | convolution fusion | flops 2433024 | bytes 737348 | tf_op jit(solution)/shard_map/dot_general | solution.py:60
  4.4 8.3 %all-to-all-start = ((bf16[16,4,1152]{2,1,0:T(4,128)(2,1)}), bf16[16,4,1152]{2,1,0:T(4,128)(2,1)S(1)}, u32[]{:S(2)}, u32[]{:S(2)}) async-start(bf16[16,4,1152]{2,1,0:T(4,128)(2,1)} %bitcast.1), calls=%async_computation | async-start | bytes 294912 | tf_op jit(solution)/shard_map/all_to_all | solution.py:62
  13.6 6.9 %all-to-all-done = bf16[16,4,1152]{2,1,0:T(4,128)(2,1)S(1)} async-done(((bf16[16,4,1152]{2,1,0:T(4,128)(2,1)}), bf16[16,4,1152]{2,1,0:T(4,128)(2,1)S(1)}, u32[]{:S(2)}, u32[]{:S(2)}) %all-to-all-start) | async-done | bytes 147488 | tf_op jit(solution)/shard_map/all_to_all | solution.py:62
  21.5 3.5 %all-to-all-start.1 = ((bf16[16,4,1152]{2,1,0:T(4,128)(2,1)}), bf16[16,4,1152]{2,1,0:T(4,128)(2,1)S(1)}, u32[]{:S(2)}, u32[]{:S(2)}) async-start(bf16[16,4,1152]{2,1,0:T(4,128)(2,1)} %reshape.130), calls=%async_computation.1 | async-start | bytes 294912 | tf_op jit(solution)/shard_map/all_to_all | solution.py:66
  25.0 1.8 %reshape.133 = bf16[16,32,576]{2,1,0:T(8,128)(2,1)S(1)} reshape(bf16[16,18432]{1,0:T(8,128)(2,1)} %param.14) | data formatting | bytes 1179648 | tf_op jit(solution)/shard_map/reshape | solution.py:167
  27.6 5.2 %all-to-all-done.1 = bf16[16,4,1152]{2,1,0:T(4,128)(2,1)S(1)} async-done(((bf16[16,4,1152]{2,1,0:T(4,128)(2,1)}), bf16[16,4,1152]{2,1,0:T(4,128)(2,1)S(1)}, u32[]{:S(2)}, u32[]{:S(2)}) %all-to-all-start.1) | async-done | bytes 147488 | tf_op jit(solution)/shard_map/all_to_all | solution.py:66
  32.8 2.0 %all_gather.3 = bf16[4,36864]{1,0:T(4,128)(2,1)S(1)} all-gather(bf16[4,18432]{1,0:T(4,128)(2,1)S(1)} %bitcast.73), channel_id=1, replica_groups=mesh['dp'=16,'ep'=2] {'ep'}, dimensions={1}, use_global_device_ids=true | all-gather | bytes 442368 | tf_op jit(solution)/shard_map/all_gather | solution.py:70
  35.4 1.6 reshape.132
  38.9 3.1 %fusion.16 = bf16[32,2,8,128]{3,2,1,0:T(8,128)(2,1)S(1)} fusion(bf16[32,512,128]{2,1,0:T(8,128)(2,1)} %param.18, bf16[16,32,512]{2,1,0:T(8,128)(2,1)S(1)} %convolution_convert_fusion.3), kind=kOutput, calls=%fused_computation.28 | convolution fusion | flops 67174400 | bytes 4849664 | tf_op jit(solution)/shard_map/rhl,hlv->rhv/dot_general | solution.py:180
  42.0 20.7 %fusion.36 = f32[16,7168]{1,0:T(8,128)S(1)} fusion(bf16[4096,7168]{1,0:T(8,128)(2,1)} %param.19, bf16[32,2,8,128]{3,2,1,0:T(8,128)(2,1)S(1)} %fusion.16), kind=kOutput, calls=%fused_computation.66 | convolution fusion | flops 939524096 | bytes 59310080 | tf_op jit(solution)/shard_map/dot_general | solution.py:185
  63.1 1.2 collective-permute-done
  65.4 4.5 %collective-permute-done.1 = bf16[1,8,7296]{2,1,0:T(8,128)(2,1)S(1)} collective-permute-done((bf16[1,8,7296]{2,1,0:T(8,128)(2,1)S(1)}, bf16[1,8,7296]{2,1,0:T(8,128)(2,1)S(1)}, u32[]{:S(2)}, u32[]{:S(2)}) %collective-permute-start.1) | collective-permute-done | bytes 116768 | tf_op jit(solution)/shard_map/ppermute | solution.py:20
  70.0 1.0 collective-permute-start.2
  71.0 11.9 %collective-permute-done.2 = bf16[2,8,7296]{2,1,0:T(8,128)(2,1)S(1)} collective-permute-done((bf16[2,8,7296]{2,1,0:T(8,128)(2,1)S(1)}, bf16[2,8,7296]{2,1,0:T(8,128)(2,1)S(1)}, u32[]{:S(2)}, u32[]{:S(2)}) %collective-permute-start.2) | collective-permute-done | bytes 233504 | tf_op jit(solution)/shard_map/ppermute | solution.py:20
  82.9 1.1 collective-permute-start.5
  84.3 6.1 %collective-permute-done.5 = bf16[4,8,3712]{2,1,0:T(8,128)(2,1)S(1)} collective-permute-done((bf16[4,8,3712]{2,1,0:T(8,128)(2,1)S(1)}, bf16[4,8,3712]{2,1,0:T(8,128)(2,1)S(1)}, u32[]{:S(2)}, u32[]{:S(2)}) %collective-permute-start.5) | collective-permute-done | bytes 237600 | tf_op jit(solution)/shard_map/ppermute | solution.py:20
  92.2 10.1 %collective-permute-done.6 = bf16[8,8,3712]{2,1,0:T(8,128)(2,1)S(1)} collective-permute-done((bf16[8,8,3712]{2,1,0:T(8,128)(2,1)S(1)}, bf16[8,8,3712]{2,1,0:T(8,128)(2,1)S(1)}, u32[]{:S(2)}, u32[]{:S(2)}) %collective-permute-start.6) | collective-permute-done | bytes 475168 | tf_op jit(solution)/shard_map/ppermute | solution.py:20
  102.9 3.8 %collective-permute-done.7 = bf16[16,8,7296]{2,1,0:T(8,128)(2,1)S(1)} collective-permute-done((bf16[16,8,7296]{2,1,0:T(8,128)(2,1)S(1)}, bf16[16,8,7296]{2,1,0:T(8,128)(2,1)S(1)}, u32[]{:S(2)}, u32[]{:S(2)}) %collective-permute-start.7) | collective-permute-done | bytes 1867808 | tf_op jit(solution)/shard_map/ppermute | solution.py:20
  106.7 5.1 %maximum_bitcast_fusion = bf16[256,7296]{1,0:T(8,128)(2,1)S(1)} fusion(bf16[16,8,7296]{2,1,0:T(8,128)(2,1)S(1)} %collective-permute-done.7, bf16[16,8,3712]{2,1,0:T(8,128)(2,1)S(1)} %bitcast.65, bf16[8,8,3584]{2,1,0:T(8,128)(2,1)S(1)} %collective-permute-done.4, bf16[4,8,3584]{2,1,0:T(8,128)(2,1)S(1)} %collective-permute-done.3, ...), kind=kLoop, calls=%fused_computation.11 | loop fusion | flops 18677760 | bytes 7471104 | tf_op jit(solution)/shard_map/reshape | solution.py:201
  112.0 1.7 copy-done
  113.7 2.0 %fusion.4 = f32[256,512]{1,0:T(8,128)S(1)} fusion(bf16[1,7168,512]{2,1,0:T(8,128)(2,1)S(1)} %bitcast.76, bf16[256,7296]{1,0:T(8,128)(2,1)S(1)} %maximum_bitcast_fusion), kind=kOutput, calls=%fused_computation.7 | convolution fusion | flops 1879048192 | bytes 11534336 | tf_op jit(solution)/shard_map/dot_general | solution.py:30
  115.7 12.2 %fusion.2 = bf16[256,7168]{1,0:T(8,128)(2,1)} fusion(bf16[1,512,7168]{2,1,0:T(8,128)(2,1)} %param.25, f32[256]{0:T(256)S(1)} %multiply_reduce_fusion.1, f32[256,512]{1,0:T(8,128)S(1)} %fusion.4, bf16[1,7168,512]{2,1,0:T(8,128)(2,1)} %param.23, bf16[256,7296]{1,0:T(8,128)(2,1)} %copy-done), kind=kOutput, calls=%fused_computation.5 | convolution fusion | flops 3762552832 | bytes 22545408 | tf_op jit(solution)/shard_map/dot_general | solution.py:32
  127.9 1.8 %slice_bitcast_fusion = bf16[16,8,7168]{2,1,0:T(8,128)(2,1)S(1)} fusion(bf16[256,7168]{1,0:T(8,128)(2,1)} %fusion.2), kind=kLoop, calls=%fused_computation.18 | loop fusion | bytes 3670016 | tf_op jit(solution)/shard_map/split | solution.py:102
  129.9 3.6 %collective-permute-done.8 = bf16[16,8,7168]{2,1,0:T(8,128)(2,1)S(1)} collective-permute-done((bf16[16,8,7168]{2,1,0:T(8,128)(2,1)S(1)}, bf16[16,8,7168]{2,1,0:T(8,128)(2,1)S(1)}, u32[]{:S(2)}, u32[]{:S(2)}) %collective-permute-start.8) | collective-permute-done | bytes 1835040 | tf_op jit(solution)/shard_map/ppermute | solution.py:20
  134.1 1.3 collective-permute-start.9
  135.6 1.4 collective-permute-start.11
  136.9 9.8 %collective-permute-done.9 = bf16[8,8,3584]{2,1,0:T(8,128)(2,1)S(1)} collective-permute-done((bf16[8,8,3584]{2,1,0:T(8,128)(2,1)S(1)}, bf16[8,8,3584]{2,1,0:T(8,128)(2,1)S(1)}, u32[]{:S(2)}, u32[]{:S(2)}) %collective-permute-start.9) | collective-permute-done | bytes 458784 | tf_op jit(solution)/shard_map/ppermute | solution.py:20
  146.8 1.2 collective-permute-start.10
  148.2 1.5 collective-permute-start.12
  149.7 4.0 %collective-permute-done.10 = bf16[4,8,3584]{2,1,0:T(8,128)(2,1)S(1)} collective-permute-done((bf16[4,8,3584]{2,1,0:T(8,128)(2,1)S(1)}, bf16[4,8,3584]{2,1,0:T(8,128)(2,1)S(1)}, u32[]{:S(2)}, u32[]{:S(2)}) %collective-permute-start.10) | collective-permute-done | bytes 229408 | tf_op jit(solution)/shard_map/ppermute | solution.py:20
  155.0 9.2 %collective-permute-done.13 = bf16[2,8,7168]{2,1,0:T(8,128)(2,1)S(1)} collective-permute-done((bf16[2,8,7168]{2,1,0:T(8,128)(2,1)S(1)}, bf16[2,8,7168]{2,1,0:T(8,128)(2,1)S(1)}, u32[]{:S(2)}, u32[]{:S(2)}) %collective-permute-start.13) | collective-permute-done | bytes 229408 | tf_op jit(solution)/shard_map/ppermute | solution.py:20
  164.3 4.9 %collective-permute-done.14 = bf16[1,8,7168]{2,1,0:T(8,128)(2,1)S(1)} collective-permute-done((bf16[1,8,7168]{2,1,0:T(8,128)(2,1)S(1)}, bf16[1,8,7168]{2,1,0:T(8,128)(2,1)S(1)}, u32[]{:S(2)}, u32[]{:S(2)}) %collective-permute-start.14) | collective-permute-done | bytes 114720 | tf_op jit(solution)/shard_map/ppermute | solution.py:20
  (81 shorter events, 15.0 us)
Async XLA Ops:
  0.6 34.2 %copy-start.2 = (bf16[16,36864]{1,0:T(8,128)(2,1)S(1)}, bf16[16,36864]{1,0:T(8,128)(2,1)}, u32[]{:S(2)}) copy-start(bf16[16,36864]{1,0:T(8,128)(2,1)} %param.15) | copy-start | bytes 3538948
  4.4 16.2 %all-to-all-start = ((bf16[16,4,1152]{2,1,0:T(4,128)(2,1)}), bf16[16,4,1152]{2,1,0:T(4,128)(2,1)S(1)}, u32[]{:S(2)}, u32[]{:S(2)}) async-start(bf16[16,4,1152]{2,1,0:T(4,128)(2,1)} %bitcast.1), calls=%async_computation | async-start | bytes 294912 | tf_op jit(solution)/shard_map/all_to_all | solution.py:62
  21.5 11.4 %all-to-all-start.1 = ((bf16[16,4,1152]{2,1,0:T(4,128)(2,1)}), bf16[16,4,1152]{2,1,0:T(4,128)(2,1)S(1)}, u32[]{:S(2)}, u32[]{:S(2)}) async-start(bf16[16,4,1152]{2,1,0:T(4,128)(2,1)} %reshape.130), calls=%async_computation.1 | async-start | bytes 294912 | tf_op jit(solution)/shard_map/all_to_all | solution.py:66
  41.9 21.0 %copy-start.5 = (f32[8,8]{1,0:T(8,128)S(1)}, f32[8,8]{1,0:T(8,128)}, u32[]{:S(2)}) copy-start(f32[8,8]{1,0:T(8,128)} %param.22) | copy-start | bytes 772
  41.9 21.0 %copy-start.6 = (s32[8,8]{1,0:T(8,128)S(1)}, s32[8,8]{1,0:T(8,128)}, u32[]{:S(2)}) copy-start(s32[8,8]{1,0:T(8,128)} %param.21) | copy-start | bytes 772
  42.0 22.3 %copy-start.3 = (bf16[8,7168]{1,0:T(8,128)(2,1)S(1)}, bf16[8,7168]{1,0:T(8,128)(2,1)}, u32[]{:S(2)}) copy-start(bf16[8,7168]{1,0:T(8,128)(2,1)} %param.13) | copy-start | bytes 344068
  42.0 22.5 %copy-start.4 = (f32[7168]{0:T(1024)S(1)}, f32[7168]{0:T(1024)}, u32[]{:S(2)}) copy-start(f32[7168]{0:T(1024)} %param.20) | copy-start | bytes 86020
  62.7 1.6 collective-permute-start
  64.7 5.2 %collective-permute-start.1 = (bf16[1,8,7296]{2,1,0:T(8,128)(2,1)S(1)}, bf16[1,8,7296]{2,1,0:T(8,128)(2,1)S(1)}, u32[]{:S(2)}, u32[]{:S(2)}) collective-permute-start(bf16[1,8,7296]{2,1,0:T(8,128)(2,1)S(1)} %bitcast.69), channel_id=1, source_target_pairs={{0,8},{2,10},{4,12},{6,14},{8,0},{10,2},{12,4},{14,6},{16,24},{18,... | collective-permute-start | bytes 350216 | tf_op jit(solution)/shard_map/ppermute | solution.py:20
  70.0 12.9 %collective-permute-start.2 = (bf16[2,8,7296]{2,1,0:T(8,128)(2,1)S(1)}, bf16[2,8,7296]{2,1,0:T(8,128)(2,1)S(1)}, u32[]{:S(2)}, u32[]{:S(2)}) collective-permute-start(bf16[2,8,7296]{2,1,0:T(8,128)(2,1)S(1)} %pad_maximum_fusion.6), channel_id=1, source_target_pairs={{0,16},{2,18},{4,20},{6,22},{8,24},{10,26},{12,28},{14,30},{16,0},... | collective-permute-start | bytes 700424 | tf_op jit(solution)/shard_map/ppermute | solution.py:20
  82.9 7.6 %collective-permute-start.5 = (bf16[4,8,3712]{2,1,0:T(8,128)(2,1)S(1)}, bf16[4,8,3712]{2,1,0:T(8,128)(2,1)S(1)}, u32[]{:S(2)}, u32[]{:S(2)}) collective-permute-start(bf16[4,8,3712]{2,1,0:T(8,128)(2,1)S(1)} %pad_maximum_fusion.4), channel_id=1, source_target_pairs={{0,2},{2,0},{4,6},{6,4},{8,10},{10,8},{12,14},{14,12},{16,18},{18,... | collective-permute-start | bytes 712712 | tf_op jit(solution)/shard_map/ppermute | solution.py:20
  84.0 7.3 %collective-permute-start.3 = (bf16[4,8,3584]{2,1,0:T(8,128)(2,1)S(1)}, bf16[4,8,3584]{2,1,0:T(8,128)(2,1)S(1)}, u32[]{:S(2)}, u32[]{:S(2)}) collective-permute-start(bf16[4,8,3584]{2,1,0:T(8,128)(2,1)S(1)} %pad_maximum_fusion.8), channel_id=1, source_target_pairs={{0,4},{2,6},{4,0},{6,2},{8,12},{10,14},{12,8},{14,10},{16,20},{18,... | collective-permute-start | bytes 688136 | tf_op jit(solution)/shard_map/ppermute | solution.py:20
  90.5 11.8 %collective-permute-start.6 = (bf16[8,8,3712]{2,1,0:T(8,128)(2,1)S(1)}, bf16[8,8,3712]{2,1,0:T(8,128)(2,1)S(1)}, u32[]{:S(2)}, u32[]{:S(2)}) collective-permute-start(bf16[8,8,3712]{2,1,0:T(8,128)(2,1)S(1)} %pad_maximum_fusion.2), channel_id=1, source_target_pairs={{0,4},{2,6},{4,0},{6,2},{8,12},{10,14},{12,8},{14,10},{16,20},{18,... | collective-permute-start | bytes 1425416 | tf_op jit(solution)/shard_map/ppermute | solution.py:20
  91.3 11.3 %collective-permute-start.4 = (bf16[8,8,3584]{2,1,0:T(8,128)(2,1)S(1)}, bf16[8,8,3584]{2,1,0:T(8,128)(2,1)S(1)}, u32[]{:S(2)}, u32[]{:S(2)}) collective-permute-start(bf16[8,8,3584]{2,1,0:T(8,128)(2,1)S(1)} %pad_maximum_fusion.3), channel_id=1, source_target_pairs={{0,2},{2,0},{4,6},{6,4},{8,10},{10,8},{12,14},{14,12},{16,18},{18,... | collective-permute-start | bytes 1376264 | tf_op jit(solution)/shard_map/ppermute | solution.py:20
  102.3 11.4 %slice-start = ((s8[7340032]{0:T(1024)(128)(4,1)}), s8[4194304]{0:T(1024)(128)(4,1)S(1)}, s32[]{:S(2)}) async-start(s8[7340032]{0:T(1024)(128)(4,1)} %bitcast.75), calls=%async_computation.2 | async-start | bytes 8388608
  102.7 11.0 %slice-start.1 = ((s8[7340032]{0:T(1024)(128)(4,1)}), s8[3145728]{0:T(1024)(128)(4,1)S(1)}, s32[]{:S(2)}) async-start(s8[7340032]{0:T(1024)(128)(4,1)} %bitcast.75), calls=%async_computation.3 | async-start | bytes 6291456
  102.8 3.9 %collective-permute-start.7 = (bf16[16,8,7296]{2,1,0:T(8,128)(2,1)S(1)}, bf16[16,8,7296]{2,1,0:T(8,128)(2,1)S(1)}, u32[]{:S(2)}, u32[]{:S(2)}) collective-permute-start(bf16[16,8,7296]{2,1,0:T(8,128)(2,1)S(1)} %pad_maximum_fusion), channel_id=1, source_target_pairs={{0,1},{1,0},{2,3},{3,2},{4,5},{5,4},{6,7},{7,6},{8,9},{9,8},{10,11... | collective-permute-start | bytes 5603336 | tf_op jit(solution)/shard_map/ppermute | solution.py:20
  111.8 1.8 %copy-start = (bf16[256,7296]{1,0:T(8,128)(2,1)}, bf16[256,7296]{1,0:T(8,128)(2,1)S(1)}, u32[]{:S(2)}) copy-start(bf16[256,7296]{1,0:T(8,128)(2,1)S(1)} %maximum_bitcast_fusion) | copy-start | bytes 11206660
  127.9 5.6 %copy-start.1 = (bf16[256,7168]{1,0:T(8,128)(2,1)S(1)}, bf16[256,7168]{1,0:T(8,128)(2,1)}, u32[]{:S(2)}) copy-start(bf16[256,7168]{1,0:T(8,128)(2,1)} %fusion.2) | copy-start | bytes 11010052
  129.7 3.9 %collective-permute-start.8 = (bf16[16,8,7168]{2,1,0:T(8,128)(2,1)S(1)}, bf16[16,8,7168]{2,1,0:T(8,128)(2,1)S(1)}, u32[]{:S(2)}, u32[]{:S(2)}) collective-permute-start(bf16[16,8,7168]{2,1,0:T(8,128)(2,1)S(1)} %slice_bitcast_fusion), channel_id=1, source_target_pairs={{0,1},{1,0},{2,3},{3,2},{4,5},{5,4},{6,7},{7,6},{8,9},{9,8},{10,11... | collective-permute-start | bytes 5505032 | tf_op jit(solution)/shard_map/ppermute | solution.py:20
  134.1 12.6 %collective-permute-start.9 = (bf16[8,8,3584]{2,1,0:T(8,128)(2,1)S(1)}, bf16[8,8,3584]{2,1,0:T(8,128)(2,1)S(1)}, u32[]{:S(2)}, u32[]{:S(2)}) collective-permute-start(bf16[8,8,3584]{2,1,0:T(8,128)(2,1)S(1)} %split.65), channel_id=1, source_target_pairs={{0,2},{2,0},{4,6},{6,4},{8,10},{10,8},{12,14},{14,12},{16,18},{18,... | collective-permute-start | bytes 1376264 | tf_op jit(solution)/shard_map/ppermute | solution.py:20
  135.6 12.5 %collective-permute-start.11 = (bf16[8,8,3584]{2,1,0:T(8,128)(2,1)S(1)}, bf16[8,8,3584]{2,1,0:T(8,128)(2,1)S(1)}, u32[]{:S(2)}, u32[]{:S(2)}) collective-permute-start(bf16[8,8,3584]{2,1,0:T(8,128)(2,1)S(1)} %bitcast.74), channel_id=1, source_target_pairs={{0,4},{2,6},{4,0},{6,2},{8,12},{10,14},{12,8},{14,10},{16,20},{18,... | collective-permute-start | bytes 1376264 | tf_op jit(solution)/shard_map/ppermute | solution.py:20
  146.8 6.9 %collective-permute-start.10 = (bf16[4,8,3584]{2,1,0:T(8,128)(2,1)S(1)}, bf16[4,8,3584]{2,1,0:T(8,128)(2,1)S(1)}, u32[]{:S(2)}, u32[]{:S(2)}) collective-permute-start(bf16[4,8,3584]{2,1,0:T(8,128)(2,1)S(1)} %split.67), channel_id=1, source_target_pairs={{0,4},{2,6},{4,0},{6,2},{8,12},{10,14},{12,8},{14,10},{16,20},{18,... | collective-permute-start | bytes 688136 | tf_op jit(solution)/shard_map/ppermute | solution.py:20
  148.2 6.6 %collective-permute-start.12 = (bf16[4,8,3584]{2,1,0:T(8,128)(2,1)S(1)}, bf16[4,8,3584]{2,1,0:T(8,128)(2,1)S(1)}, u32[]{:S(2)}, u32[]{:S(2)}) collective-permute-start(bf16[4,8,3584]{2,1,0:T(8,128)(2,1)S(1)} %split.71), channel_id=1, source_target_pairs={{0,2},{2,0},{4,6},{6,4},{8,10},{10,8},{12,14},{14,12},{16,18},{18,... | collective-permute-start | bytes 688136 | tf_op jit(solution)/shard_map/ppermute | solution.py:20
  154.9 9.2 %collective-permute-start.13 = (bf16[2,8,7168]{2,1,0:T(8,128)(2,1)S(1)}, bf16[2,8,7168]{2,1,0:T(8,128)(2,1)S(1)}, u32[]{:S(2)}, u32[]{:S(2)}) collective-permute-start(bf16[2,8,7168]{2,1,0:T(8,128)(2,1)S(1)} %pad_maximum_fusion.7), channel_id=1, source_target_pairs={{0,16},{2,18},{4,20},{6,22},{8,24},{10,26},{12,28},{14,30},{16,0},... | collective-permute-start | bytes 688136 | tf_op jit(solution)/shard_map/ppermute | solution.py:20
  164.2 5.0 %collective-permute-start.14 = (bf16[1,8,7168]{2,1,0:T(8,128)(2,1)S(1)}, bf16[1,8,7168]{2,1,0:T(8,128)(2,1)S(1)}, u32[]{:S(2)}, u32[]{:S(2)}) collective-permute-start(bf16[1,8,7168]{2,1,0:T(8,128)(2,1)S(1)} %split.75), channel_id=1, source_target_pairs={{0,8},{2,10},{4,12},{6,14},{8,0},{10,2},{12,4},{14,6},{16,24},{18,... | collective-permute-start | bytes 344072 | tf_op jit(solution)/shard_map/ppermute | solution.py:20

commit v2 on v1

--- a/solution.py
+++ b/solution.py
@@ -1,6 +1,10 @@
+import functools
+
 import jax
 import jax.numpy as jnp
 from jax import lax
+from jax.experimental import pallas as pl
+from jax.experimental.pallas import tpu as pltpu
 from jax.sharding import PartitionSpec as P
 
 LAT = 512
@@ -25,11 +29,151 @@
     return [1 << b for b in range(size.bit_length() - 1)]
 
 
-def expert_rows(flat_rows, w_gate, w_up, w_down):
-    gate_part = jnp.dot(flat_rows, w_gate[0], preferred_element_type=jnp.float32)
-    up_part = jnp.dot(flat_rows, w_up[0], preferred_element_type=jnp.float32)
-    activated = (jax.nn.silu(gate_part) * up_part).astype(jnp.bfloat16)
-    return jnp.dot(activated, w_down[0], preferred_element_type=jnp.float32)
+CHUNKS = 4
+
+
+def read_rows(sets, width, half, at, size):
+    parts = []
+    for own, near_x, near_y, low, high in sets:
+        for ref in (own, near_x, near_y):
+            parts.append(ref[:, pl.ds(at, size)])
+        if half == 0:
+            parts.append(low[:, pl.ds(at, size)])
+        else:
+            parts.append(high[:, pl.ds(pl.multiple_of(at - width // 2, 128), size)])
+    return jnp.concatenate(parts, axis=0)
+
+
+def expert_kernel(set_count, *refs):
+    flat, refs = refs[: 5 * set_count], refs[5 * set_count :]
+    sets = [flat[5 * n : 5 * n + 5] for n in range(set_count)]
+    mask, w_gate, w_up, w_down, far, kept, gate_buf, up_buf, down_buf, gate_acc, up_acc, act, sems = refs
+    width = w_gate.shape[1]
+    size = width // CHUNKS
+    half_rows = far.shape[0]
+
+    def span(n):
+        return pl.ds(pl.multiple_of(n * size, size), size)
+
+    def copies_in(n):
+        return (
+            pltpu.make_async_copy(w_gate.at[0, span(n)], gate_buf.at[n], sems.at[0, n]),
+            pltpu.make_async_copy(w_up.at[0, span(n)], up_buf.at[n], sems.at[1, n]),
+        )
+
+    def copy_down(n):
+        return pltpu.make_async_copy(w_down.at[0, :, span(n)], down_buf.at[n], sems.at[2, n])
+
+    for n in range(CHUNKS):
+        for copy in copies_in(n):
+            copy.start()
+    for n in range(CHUNKS):
+        copy_down(n).start()
+    gate_acc[...] = jnp.zeros_like(gate_acc)
+    up_acc[...] = jnp.zeros_like(up_acc)
+    for half in range(2):
+
+        @pl.loop(half * CHUNKS // 2, (half + 1) * CHUNKS // 2)
+        def _(n):
+            for copy in copies_in(n):
+                copy.wait()
+            rows = read_rows(sets, width, half, pl.multiple_of(n * size, size), size)
+            gate_acc[...] += jnp.dot(rows, gate_buf[n], preferred_element_type=jnp.float32)
+            up_acc[...] += jnp.dot(rows, up_buf[n], preferred_element_type=jnp.float32)
+
+    tails = []
+    for own, near_x, near_y, low, high in sets:
+        tails += [ref[:, width:] for ref in (own, near_x, near_y)] + [high[:, width // 2 :]]
+    terms = jnp.concatenate(tails, axis=0).astype(jnp.float32)
+    gates = jnp.sum(terms * mask[...], axis=1, keepdims=True)
+    gated = gate_acc[...]
+    act[...] = (gated / (1.0 + jnp.exp(-gated)) * up_acc[...] * gates).astype(jnp.bfloat16)
+    kept[...] = act[:half_rows]
+
+    @pl.loop(0, CHUNKS)
+    def _(n):
+        copy_down(n).wait()
+        far[:, span(n)] = jnp.dot(
+            act[half_rows:], down_buf[n], preferred_element_type=jnp.float32
+        ).astype(jnp.bfloat16)
+
+
+def vmem_spec():
+    return pl.BlockSpec(memory_space=pltpu.VMEM)
+
+
+def experts_far(sets, mask, w_gate, w_up, w_down):
+    width, hidden_units = w_gate.shape[1:]
+    rows = sum(piece.shape[0] for pieces in sets for piece in pieces[:4])
+    size = width // CHUNKS
+    flat = [piece for pieces in sets for piece in pieces]
+    return pl.pallas_call(
+        functools.partial(expert_kernel, len(sets)),
+        out_shape=(
+            jax.ShapeDtypeStruct((rows // 2, width), jnp.bfloat16),
+            jax.ShapeDtypeStruct((rows // 2, hidden_units), jnp.bfloat16),
+        ),
+        in_specs=[vmem_spec()] * (len(flat) + 1) + [pl.BlockSpec(memory_space=pl.ANY)] * 3,
+        out_specs=(vmem_spec(), vmem_spec()),
+        scratch_shapes=[
+            pltpu.VMEM((CHUNKS, size, hidden_units), jnp.bfloat16),
+            pltpu.VMEM((CHUNKS, size, hidden_units), jnp.bfloat16),
+            pltpu.VMEM((CHUNKS, hidden_units, size), jnp.bfloat16),
+            pltpu.VMEM((rows, hidden_units), jnp.float32),
+            pltpu.VMEM((rows, hidden_units), jnp.float32),
+            pltpu.VMEM((rows, hidden_units), jnp.bfloat16),
+            pltpu.SemaphoreType.DMA((3, CHUNKS)),
+        ],
+        compiler_params=pltpu.CompilerParams(vmem_limit_bytes=48 << 20),
+        cost_estimate=pl.CostEstimate(
+            flops=5 * rows * width * hidden_units,
+            bytes_accessed=6 * width * hidden_units + 3 * rows * width,
+            transcendentals=rows * hidden_units,
+        ),
+        name="experts_far",
+    )(*flat, mask, w_gate, w_up, w_down)
+
+
+def down_kernel(kept, w_down, near, down_buf, sems):
+    size = down_buf.shape[2]
+
+    def copy(n):
+        columns = pl.ds(pl.multiple_of(n * size, size), size)
+        return pltpu.make_async_copy(w_down.at[0, :, columns], down_buf.at[n], sems.at[n])
+
+    for n in range(CHUNKS):
+        copy(n).start()
+
+    @pl.loop(0, CHUNKS)
+    def _(n):
+        copy(n).wait()
+        columns = pl.ds(pl.multiple_of(n * size, size), size)
+        near[:, columns] = jnp.dot(
+            kept[...], down_buf[n], preferred_element_type=jnp.float32
+        ).astype(jnp.bfloat16)
+
+
+def experts_near(kept, w_down):
+    rows, hidden_units = kept.shape
+    width = w_down.shape[2]
+    size = width // CHUNKS
+    return pl.pallas_call(
+        down_kernel,
+        out_shape=jax.ShapeDtypeStruct((rows, width), jnp.bfloat16),
+        in_specs=[vmem_spec(), pl.BlockSpec(memory_space=pl.ANY)],
+        out_specs=vmem_spec(),
+        scratch_shapes=[
+            pltpu.VMEM((CHUNKS, hidden_units, size), jnp.bfloat16),
+            pltpu.SemaphoreType.DMA((CHUNKS,)),
+        ],
+        compiler_params=pltpu.CompilerParams(vmem_limit_bytes=32 << 20),
+        cost_estimate=pl.CostEstimate(
+            flops=2 * rows * width * hidden_units,
+            bytes_accessed=2 * width * hidden_units + 2 * rows * width,
+            transcendentals=0,
+        ),
+        name="experts_near",
+    )(kept, w_down)
 
 
 def moves(destination, replica_rows):
@@ -71,57 +215,54 @@
 
 
 def gather_rows(rows):
-    bits = bits_of("dp")
-    last = bits[:2]
-    held = rows[None]
-    for bit in bits[2:]:
-        held = jnp.concatenate([held, flip(held, "dp", bit)], axis=0)
+    inner_x, inner_y, *outer = bits_of("dp")
+    for bit in outer:
+        rows = jnp.concatenate([rows, flip(rows, "dp", bit)], axis=0)
     half = rows.shape[1] // 2 // 128 * 128
-    parts = [held[:, :, :half], held[:, :, half:]]
-    orders = [last[::-1], last]
-    for step in range(len(last)):
-        parts = [
-            jnp.concatenate([part, flip(part, "dp", order[step])], axis=0)
-            for part, order in zip(parts, orders)
-        ]
-    blocks = parts[0].shape[0] // 4
-    second = parts[1].reshape((2, 2, blocks) + parts[1].shape[1:])
-    parts[1] = jnp.swapaxes(second, 0, 1).reshape(parts[1].shape)
-    held = jnp.concatenate(parts, axis=2)
+    near_x = flip(rows, "dp", inner_x)
+    near_y = flip(rows, "dp", inner_y)
+    low = flip(near_y[:, :half], "dp", inner_x)
+    high = flip(near_x[:, half:], "dp", inner_y)
+    sets = [(rows, near_x, near_y, low, high)]
     for bit in bits_of("ep"):
-        held = jnp.concatenate([held, flip(held, "ep", bit)], axis=0)
-    return held
-
-
-def add_up(kept, came):
-    return (kept.astype(jnp.float32) + came.astype(jnp.float32)).astype(jnp.bfloat16)
-
-
-def scatter_sums(blocks):
-    for bit in bits_of("ep")[::-1]:
-        near, far = jnp.split(blocks, 2, axis=0)
-        blocks = add_up(near, flip(far, "ep", bit))
-    bits = bits_of("dp")
-    last = bits[:2]
-    half = blocks.shape[2] // 2 // 128 * 128
-    parts = [blocks[:, :, :half], blocks[:, :, half:]]
-    size = parts[1].shape[0] // 4
-    second = parts[1].reshape((2, 2, size) + parts[1].shape[1:])
-    parts[1] = jnp.swapaxes(second, 0, 1).reshape(parts[1].shape)
-    orders = [last, last[::-1]]
-    for step in range(len(last)):
-        split = [jnp.split(part, 2, axis=0) for part in parts]
-        parts = [
-            add_up(near, flip(far, "dp", order[step])) for (near, far), order in zip(split, orders)
-        ]
-    blocks = jnp.concatenate(parts, axis=2)
-    rest = bits[2:]
-    for bit in rest[:0:-1]:
-        near, far = jnp.split(blocks, 2, axis=0)
-        blocks = add_up(near, flip(far, "dp", bit))
-    near, far = jnp.split(blocks, 2, axis=0)
-    came = flip(far, "dp", rest[0])
-    return near[0].astype(jnp.float32) + came[0].astype(jnp.float32)
+        sets = sets + [tuple(flip(piece, "ep", bit) for piece in pieces) for pieces in sets]
+    return sets
+
+
+def plus(*terms):
+    return sum(term.astype(jnp.float32) for term in terms)
+
+
+def narrow(x):
+    return x.astype(jnp.bfloat16)
+
+
+def scatter_sums(near, far):
+    bits = bits_of("ep")[::-1]
+    for bit in bits:
+        came = flip(far, "ep", bit)
+        if bit != bits[-1]:
+            both = narrow(plus(near, came))
+            near, far = jnp.split(both, 2, axis=0)
+    inner_x, inner_y, *outer = bits_of("dp")
+    width = near.shape[1]
+    half = width // 2
+    near = jnp.split(near, 4, axis=0)
+    came = jnp.split(came, 4, axis=0)
+    diagonal = narrow(plus(near[3], came[3]))
+    low = flip(diagonal[:, :half], "dp", inner_x)
+    high = flip(diagonal[:, half:], "dp", inner_y)
+    to_x = plus(near[1], came[1])
+    to_y = plus(near[2], came[2])
+    to_x = narrow(jnp.concatenate([to_x[:, :half], to_x[:, half:] + plus(high)], axis=1))
+    to_y = narrow(jnp.concatenate([to_y[:, :half] + plus(low), to_y[:, half:]], axis=1))
+    from_x = flip(to_x, "dp", inner_x)
+    from_y = flip(to_y, "dp", inner_y)
+    total = plus(near[0], came[0], from_x, from_y)
+    for bit in outer[::-1]:
+        mine, other = jnp.split(total, 2, axis=0)
+        total = mine + plus(flip(narrow(other), "dp", bit))
+    return total
 
 
 def head_sums(part):
@@ -197,12 +338,11 @@
         terms.append(term.astype(jnp.bfloat16))
         left = left - term
     terms.append(jnp.zeros((gate_sum.shape[0], GATE_COLS - 3 * replicas), jnp.bfloat16))
-    gathered = gather_rows(jnp.concatenate([normed] + terms, axis=1))
-    flat = gathered.reshape(-1, width + GATE_COLS)
-    chosen = (jnp.arange(GATE_COLS, dtype=jnp.int32) % replicas == own_replica).astype(jnp.float32)
-    gates = jnp.sum(flat[:, width:].astype(jnp.float32) * chosen[None, :], axis=1)
-    served = expert_rows(flat[:, :width], w_gate, w_up, w_down) * gates[:, None]
-    mixture = scatter_sums(served.astype(jnp.bfloat16).reshape(gathered.shape[:2] + (width,)))
+    sets = gather_rows(jnp.concatenate([normed] + terms, axis=1))
+    columns = jnp.arange(GATE_COLS, dtype=jnp.int32)[None, :]
+    chosen = (columns < 3 * replicas) & (columns % replicas == own_replica)
+    far, kept = experts_far(sets, chosen.astype(jnp.float32), w_gate, w_up, w_down)
+    mixture = scatter_sums(experts_near(kept, w_down), far)
     layer_out = (hidden + mixture).astype(jnp.bfloat16)
     return (layer_out, arrivals)
 

time: 171 us -> 156 us (0.912)
  matrix products: 43.2 us -> 29 us
  Pallas kernels: 0 us -> 11.2 us
  other arithmetic: 10.3 us -> 3.86 us
  local copies, waits for them, and re-layouts: 8.88 us -> 4.2 us
    dot_general x2 -> x0, matrix products: 14.2 us -> none  [the longest x1 12.2 us: expert_rows(): return jnp.dot(activated, w_down[0], preferred_element_type=jnp.float32)]
    pallas_call x0 -> x2, Pallas kernels: none -> 11.2 us  [the longest x1 8.51 us: experts_far(): pl.pallas_call(functools.partial(expert_kernel, len(sets)), out_shape=(ja...]
    reshape x1 -> x0, other arithmetic: 5.14 us -> none  [per_device(): flat = gathered.reshape(-1, width + GATE_COLS)]
    ppermute x15 -> x19, waiting for transfers between devices: 70.3 us -> 68.2 us  [flip(): return lax.ppermute(x, axis, pairs)]
    split x6 -> x2, local copies, waits for them, and re-layouts: 1.9 us -> 0.04 us  [scatter_sums(): mine, other = jnp.split(total, 2, axis=0)]
    ppermute x15 -> x19, starting transfers between devices: 10.9 us -> 10.8 us  [flip(): return lax.ppermute(x, axis, pairs)]
  transfers between devices with their start and end apart: 17 -> 21, of which waited for: 15 -> 16; matrix products, arithmetic and copies ran while one was open for 3% -> 1% of each run, Pallas kernels for 0% -> 2%
where the time goes in v2:
time: 156 us
  waiting for transfers between devices  82 us (53%)
  matrix products  29 us (19%)
  starting transfers between devices  22.7 us (15%)
  Pallas kernels  11.2 us (7%)
  local copies, waits for them, and re-layouts  4.2 us (3%)
  other arithmetic  3.86 us (2%)
  blocking collectives  2 us (1%)
    ppermute x19, waiting for transfers between devices, flip(): return lax.ppermute(x, axis, pairs)  68.2 us
    dot_general x1, matrix products, per_device(): jnp.dot(values, w_o, preferred_element_type=jnp.float32)  20.7 us
    ppermute x19, starting transfers between devices, flip(): return lax.ppermute(x, axis, pairs)  10.8 us
    pallas_call x1, Pallas kernels, experts_far(): pl.pallas_call(functools.partial(expert_kernel, len(sets)), out_shape=(ja...  8.51 us
    all_to_all x1, starting transfers between devices, migrate(): met = lax.all_to_all(outbox, 'dp', split_axis=0, concat_axis=0)  8.44 us
    all_to_all x1, waiting for transfers between devices, migrate(): lax.all_to_all(sorted_rows.reshape(replicas, MOVE_MAX, share), 'dp', spli...  6.93 us
    all_to_all x1, waiting for transfers between devices, migrate(): met = lax.all_to_all(outbox, 'dp', split_axis=0, concat_axis=0)  6.89 us
    all_to_all x1, starting transfers between devices, migrate(): lax.all_to_all(sorted_rows.reshape(replicas, MOVE_MAX, share), 'dp', spli...  3.52 us
  transfers between devices with their start and end apart: 21, of which 16 were waited for; matrix products, arithmetic and copies ran while one was open for 1% of the time, Pallas kernels for 2%

profile of v2, /device:TPU:0, one launch (start us, length us, event | category | flops | bytes accessed | tf_op | source)
XLA Modules:
  0.0 156.0 jit_solution(13599011508184337374)
XLA Ops:
  2.4 1.9 %convolution_convert_fusion.1 = bf16[4,18432]{1,0:T(4,128)(2,1)} fusion(pred[4,16]{1,0:T(4,128)(4,1)S(1)} %get-tuple-element.9, bf16[16,36864]{1,0:T(8,128)(2,1)} %param.15, s32[]{:T(128)S(6)} %select_n.82), kind=kOutput, calls=%fused_computation.3 | convolution fusion | flops 2433024 | bytes 737348 | tf_op jit(solution)/shard_map/dot_general | solution.py:204
  4.3 8.4 %all-to-all-start = ((bf16[16,4,1152]{2,1,0:T(4,128)(2,1)}), bf16[16,4,1152]{2,1,0:T(4,128)(2,1)S(1)}, u32[]{:S(2)}, u32[]{:S(2)}) async-start(bf16[16,4,1152]{2,1,0:T(4,128)(2,1)} %bitcast.1), calls=%async_computation | async-start | bytes 294912 | tf_op jit(solution)/shard_map/all_to_all | solution.py:206
  12.8 1.0 fusion.9
  13.8 6.9 %all-to-all-done = bf16[16,4,1152]{2,1,0:T(4,128)(2,1)S(1)} async-done(((bf16[16,4,1152]{2,1,0:T(4,128)(2,1)}), bf16[16,4,1152]{2,1,0:T(4,128)(2,1)S(1)}, u32[]{:S(2)}, u32[]{:S(2)}) %all-to-all-start) | async-done | bytes 147488 | tf_op jit(solution)/shard_map/all_to_all | solution.py:206
  21.6 3.5 %all-to-all-start.1 = ((bf16[16,4,1152]{2,1,0:T(4,128)(2,1)}), bf16[16,4,1152]{2,1,0:T(4,128)(2,1)S(1)}, u32[]{:S(2)}, u32[]{:S(2)}) async-start(bf16[16,4,1152]{2,1,0:T(4,128)(2,1)} %reshape.141), calls=%async_computation.1 | async-start | bytes 294912 | tf_op jit(solution)/shard_map/all_to_all | solution.py:210
  26.0 6.9 %all-to-all-done.1 = bf16[16,4,1152]{2,1,0:T(4,128)(2,1)S(1)} async-done(((bf16[16,4,1152]{2,1,0:T(4,128)(2,1)}), bf16[16,4,1152]{2,1,0:T(4,128)(2,1)S(1)}, u32[]{:S(2)}, u32[]{:S(2)}) %all-to-all-start.1) | async-done | bytes 147488 | tf_op jit(solution)/shard_map/all_to_all | solution.py:210
  32.9 2.0 %all_gather.3 = bf16[4,36864]{1,0:T(4,128)(2,1)S(1)} all-gather(bf16[4,18432]{1,0:T(4,128)(2,1)S(1)} %bitcast.27), channel_id=1, replica_groups=mesh['dp'=16,'ep'=2] {'ep'}, dimensions={1}, use_global_device_ids=true | all-gather | bytes 442368 | tf_op jit(solution)/shard_map/all_gather | solution.py:214
  35.5 1.6 %reshape.143 = bf16[16,64,576]{2,1,0:T(8,128)(2,1)S(1)} reshape(bf16[16,36864]{1,0:T(8,128)(2,1)S(1)} %fusion.1) | data formatting | bytes 2359296 | tf_op jit(solution)/shard_map/reshape | solution.py:307
  38.0 1.0 convolution_convert_fusion.3
  39.0 3.1 %fusion.7 = bf16[32,2,8,128]{3,2,1,0:T(8,128)(2,1)S(1)} fusion(bf16[32,512,128]{2,1,0:T(8,128)(2,1)} %param.18, bf16[16,32,512]{2,1,0:T(8,128)(2,1)S(1)} %convolution_convert_fusion.3), kind=kOutput, calls=%fused_computation.13 | convolution fusion | flops 67174400 | bytes 4849664 | tf_op jit(solution)/shard_map/rhl,hlv->rhv/dot_general | solution.py:321
  42.1 20.7 %fusion.19 = f32[16,7168]{1,0:T(8,128)S(1)} fusion(bf16[4096,7168]{1,0:T(8,128)(2,1)} %param.19, bf16[32,2,8,128]{3,2,1,0:T(8,128)(2,1)S(1)} %fusion.7), kind=kOutput, calls=%fused_computation.49 | convolution fusion | flops 939524096 | bytes 59310080 | tf_op jit(solution)/shard_map/dot_general | solution.py:326
  63.2 1.2 collective-permute-done
  65.6 4.5 %collective-permute-done.1 = bf16[8,7296]{1,0:T(8,128)(2,1)S(1)} collective-permute-done((bf16[8,7296]{1,0:T(8,128)(2,1)S(1)}, bf16[8,7296]{1,0:T(8,128)(2,1)S(1)}, u32[]{:S(2)}, u32[]{:S(2)}) %collective-permute-start.1) | collective-permute-done | bytes 116768 | tf_op jit(solution)/shard_map/ppermute | solution.py:24
  70.1 1.0 collective-permute-start.2
  71.1 11.9 %collective-permute-done.2 = bf16[16,7296]{1,0:T(8,128)(2,1)S(1)} collective-permute-done((bf16[16,7296]{1,0:T(8,128)(2,1)S(1)}, bf16[16,7296]{1,0:T(8,128)(2,1)S(1)}, u32[]{:S(2)}, u32[]{:S(2)}) %collective-permute-start.2) | collective-permute-done | bytes 233504 | tf_op jit(solution)/shard_map/ppermute | solution.py:24
  83.0 1.1 collective-permute-start.3
  84.4 11.1 %collective-permute-done.3.refs_1_ = bf16[32,7296]{1,0:T(8,128)(2,1)S(1)} collective-permute-done((bf16[32,7296]{1,0:T(8,128)(2,1)S(1)}, bf16[32,7296]{1,0:T(8,128)(2,1)S(1)}, u32[]{:S(2)}, u32[]{:S(2)}) %collective-permute-start.3) | collective-permute-done | bytes 466976 | tf_op jit(solution)/shard_map/ppermute | solution.py:24
  95.5 0.8 collective-permute-start.6
  97.5 4.6 %collective-permute-done.6.refs_4_ = bf16[32,3712]{1,0:T(8,128)(2,1)S(1)} collective-permute-done((bf16[32,3712]{1,0:T(8,128)(2,1)S(1)}, bf16[32,3712]{1,0:T(8,128)(2,1)S(1)}, u32[]{:S(2)}, u32[]{:S(2)}) %collective-permute-start.6) | collective-permute-done | bytes 237600 | tf_op jit(solution)/shard_map/ppermute | solution.py:24
  102.2 2.8 %collective-permute-done.5.refs_3_ = bf16[32,3584]{1,0:T(8,128)(2,1)S(1)} collective-permute-done((bf16[32,3584]{1,0:T(8,128)(2,1)S(1)}, bf16[32,3584]{1,0:T(8,128)(2,1)S(1)}, u32[]{:S(2)}, u32[]{:S(2)}) %collective-permute-start.5) | collective-permute-done | bytes 229408 | tf_op jit(solution)/shard_map/ppermute | solution.py:24
  105.0 1.5 collective-permute-done.10.refs_8_
  106.4 8.5 %experts_far.1 = (bf16[128,7168]{1,0:T(8,128)(2,1)S(1)}, bf16[128,512]{1,0:T(8,128)(2,1)S(1)}) custom-call(bf16[32,7296]{1,0:T(8,128)(2,1)S(1)} %pad_maximum_fusion.refs_0_, bf16[32,7296]{1,0:T(8,128)(2,1)S(1)} %collective-permute-done.3.refs_1_, bf16[32,7296]{1,0:T(8,128)(2,1)S(1)} %collective-permute-done.4.refs_2_, ...), custom_call_target="tpu_custom_call" | custom-call | flops 4697620480 | bytes 27525120 | tf_op jit(solution)/shard_map/experts_far/pallas_call | solution.py:110
  115.2 2.6 %experts_near.1 = bf16[128,7168]{1,0:T(8,128)(2,1)S(1)} custom-call(bf16[128,512]{1,0:T(8,128)(2,1)S(1)} %get-tuple-element.4.kept, bf16[1,512,7168]{2,1,0:T(8,128)(2,1)S(1)} %bitcast.26), custom_call_target="tpu_custom_call" | custom-call | flops 939524096 | bytes 9175040 | tf_op jit(solution)/shard_map/experts_near/pallas_call | solution.py:160
  117.8 1.0 collective-permute-done.12
  119.1 1.3 collective-permute-start.13
  120.5 1.3 collective-permute-start.15
  121.8 5.0 %collective-permute-done.13 = bf16[32,3584]{1,0:T(8,128)(2,1)S(1)} collective-permute-done((bf16[32,3584]{1,0:T(8,128)(2,1)S(1)}, bf16[32,3584]{1,0:T(8,128)(2,1)S(1)}, u32[]{:S(2)}, u32[]{:S(2)}) %collective-permute-start.13) | collective-permute-done | bytes 229408 | tf_op jit(solution)/shard_map/ppermute | solution.py:24
  128.0 1.6 %collective-permute-start.16 = (bf16[32,7168]{1,0:T(8,128)(2,1)S(1)}, bf16[32,7168]{1,0:T(8,128)(2,1)S(1)}, u32[]{:S(2)}, u32[]{:S(2)}) collective-permute-start(bf16[32,7168]{1,0:T(8,128)(2,1)S(1)} %pad_maximum_fusion.2), channel_id=1, source_target_pairs={{0,4},{2,6},{4,0},{6,2},{8,12},{10,14},{12,8},{14,10},{16,20},{18,... | collective-permute-start | bytes 1376264 | tf_op jit(solution)/shard_map/ppermute | solution.py:24
  129.6 9.1 %collective-permute-done.14 = bf16[32,7168]{1,0:T(8,128)(2,1)S(1)} collective-permute-done((bf16[32,7168]{1,0:T(8,128)(2,1)S(1)}, bf16[32,7168]{1,0:T(8,128)(2,1)S(1)}, u32[]{:S(2)}, u32[]{:S(2)}) %collective-permute-start.14) | collective-permute-done | bytes 458784 | tf_op jit(solution)/shard_map/ppermute | solution.py:24
  138.7 0.8 collective-permute-done.16
  139.9 9.5 %collective-permute-done.17 = bf16[16,7168]{1,0:T(8,128)(2,1)S(1)} collective-permute-done((bf16[16,7168]{1,0:T(8,128)(2,1)S(1)}, bf16[16,7168]{1,0:T(8,128)(2,1)S(1)}, u32[]{:S(2)}, u32[]{:S(2)}) %collective-permute-start.17) | collective-permute-done | bytes 229408 | tf_op jit(solution)/shard_map/ppermute | solution.py:24
  149.6 5.0 %collective-permute-done.18 = bf16[8,7168]{1,0:T(8,128)(2,1)S(1)} collective-permute-done((bf16[8,7168]{1,0:T(8,128)(2,1)S(1)}, bf16[8,7168]{1,0:T(8,128)(2,1)S(1)}, u32[]{:S(2)}, u32[]{:S(2)}) %collective-permute-start.18) | collective-permute-done | bytes 114720 | tf_op jit(solution)/shard_map/ppermute | solution.py:24
  (80 shorter events, 11.5 us)
Async XLA Ops:
  0.6 24.5 %copy-start.1 = (bf16[16,18432]{1,0:T(8,128)(2,1)S(1)}, bf16[16,18432]{1,0:T(8,128)(2,1)}, u32[]{:S(2)}) copy-start(bf16[16,18432]{1,0:T(8,128)(2,1)} %param.14) | copy-start | bytes 1769476
  0.7 25.2 %copy-start.6 = (s32[16]{0:T(128)S(1)}, s32[16]{0:T(128)}, u32[]{:S(2)}) copy-start(s32[16]{0:T(128)} %param.16) | copy-start | bytes 196
  4.3 30.6 %copy-start = (bf16[16,36864]{1,0:T(8,128)(2,1)S(1)}, bf16[16,36864]{1,0:T(8,128)(2,1)}, u32[]{:S(2)}) copy-start(bf16[16,36864]{1,0:T(8,128)(2,1)} %param.15) | copy-start | bytes 3538948
  4.3 16.3 %all-to-all-start = ((bf16[16,4,1152]{2,1,0:T(4,128)(2,1)}), bf16[16,4,1152]{2,1,0:T(4,128)(2,1)S(1)}, u32[]{:S(2)}, u32[]{:S(2)}) async-start(bf16[16,4,1152]{2,1,0:T(4,128)(2,1)} %bitcast.1), calls=%async_computation | async-start | bytes 294912 | tf_op jit(solution)/shard_map/all_to_all | solution.py:206
  21.6 11.4 %all-to-all-start.1 = ((bf16[16,4,1152]{2,1,0:T(4,128)(2,1)}), bf16[16,4,1152]{2,1,0:T(4,128)(2,1)S(1)}, u32[]{:S(2)}, u32[]{:S(2)}) async-start(bf16[16,4,1152]{2,1,0:T(4,128)(2,1)} %reshape.141), calls=%async_computation.1 | async-start | bytes 294912 | tf_op jit(solution)/shard_map/all_to_all | solution.py:210
  42.0 21.0 %copy-start.4 = (f32[8,8]{1,0:T(8,128)S(1)}, f32[8,8]{1,0:T(8,128)}, u32[]{:S(2)}) copy-start(f32[8,8]{1,0:T(8,128)} %param.22) | copy-start | bytes 772
  42.1 21.0 %copy-start.5 = (s32[8,8]{1,0:T(8,128)S(1)}, s32[8,8]{1,0:T(8,128)}, u32[]{:S(2)}) copy-start(s32[8,8]{1,0:T(8,128)} %param.21) | copy-start | bytes 772
  42.1 22.3 %copy-start.2 = (bf16[8,7168]{1,0:T(8,128)(2,1)S(1)}, bf16[8,7168]{1,0:T(8,128)(2,1)}, u32[]{:S(2)}) copy-start(bf16[8,7168]{1,0:T(8,128)(2,1)} %param.13) | copy-start | bytes 344068
  42.1 22.5 %copy-start.3 = (f32[7168]{0:T(1024)S(1)}, f32[7168]{0:T(1024)}, u32[]{:S(2)}) copy-start(f32[7168]{0:T(1024)} %param.20) | copy-start | bytes 86020
  62.8 1.6 collective-permute-start
  64.8 5.2 %collective-permute-start.1 = (bf16[8,7296]{1,0:T(8,128)(2,1)S(1)}, bf16[8,7296]{1,0:T(8,128)(2,1)S(1)}, u32[]{:S(2)}, u32[]{:S(2)}) collective-permute-start(bf16[8,7296]{1,0:T(8,128)(2,1)S(1)} %concatenate.18), channel_id=1, source_target_pairs={{0,8},{2,10},{4,12},{6,14},{8,0},{10,2},{12,4},{14,6},{16,24},{18,... | collective-permute-start | bytes 350216 | tf_op jit(solution)/shard_map/ppermute | solution.py:24
  70.1 12.9 %collective-permute-start.2 = (bf16[16,7296]{1,0:T(8,128)(2,1)S(1)}, bf16[16,7296]{1,0:T(8,128)(2,1)S(1)}, u32[]{:S(2)}, u32[]{:S(2)}) collective-permute-start(bf16[16,7296]{1,0:T(8,128)(2,1)S(1)} %pad_maximum_fusion.3), channel_id=1, source_target_pairs={{0,16},{2,18},{4,20},{6,22},{8,24},{10,26},{12,28},{14,30},{16,0},... | collective-permute-start | bytes 700424 | tf_op jit(solution)/shard_map/ppermute | solution.py:24
  82.9 32.2 %slice-start = ((s8[7340032]{0:T(1024)(128)(4,1)}), s8[4194304]{0:T(1024)(128)(4,1)S(1)}, s32[]{:S(2)}) async-start(s8[7340032]{0:T(1024)(128)(4,1)} %bitcast.25), calls=%async_computation.2 | async-start | bytes 8388608
  83.0 12.5 %collective-permute-start.3 = (bf16[32,7296]{1,0:T(8,128)(2,1)S(1)}, bf16[32,7296]{1,0:T(8,128)(2,1)S(1)}, u32[]{:S(2)}, u32[]{:S(2)}) collective-permute-start(bf16[32,7296]{1,0:T(8,128)(2,1)S(1)} %pad_maximum_fusion.refs_0_), channel_id=1, source_target_pairs={{0,2},{2,0},{4,6},{6,4},{8,10},{10,8},{12,14},{14,12},{16,18},{18,... | collective-permute-start | bytes 1400840 | tf_op jit(solution)/shard_map/ppermute | solution.py:24
  84.1 12.8 %collective-permute-start.4 = (bf16[32,7296]{1,0:T(8,128)(2,1)S(1)}, bf16[32,7296]{1,0:T(8,128)(2,1)S(1)}, u32[]{:S(2)}, u32[]{:S(2)}) collective-permute-start(bf16[32,7296]{1,0:T(8,128)(2,1)S(1)} %pad_maximum_fusion.refs_0_), channel_id=1, source_target_pairs={{0,4},{2,6},{4,0},{6,2},{8,12},{10,14},{12,8},{14,10},{16,20},{18,... | collective-permute-start | bytes 1400840 | tf_op jit(solution)/shard_map/ppermute | solution.py:24
  95.5 6.7 %collective-permute-start.6 = (bf16[32,3712]{1,0:T(8,128)(2,1)S(1)}, bf16[32,3712]{1,0:T(8,128)(2,1)S(1)}, u32[]{:S(2)}, u32[]{:S(2)}) collective-permute-start(bf16[32,3712]{1,0:T(8,128)(2,1)S(1)} %slice.40), channel_id=1, source_target_pairs={{0,4},{2,6},{4,0},{6,2},{8,12},{10,14},{12,8},{14,10},{16,20},{18,... | collective-permute-start | bytes 712712 | tf_op jit(solution)/shard_map/ppermute | solution.py:24
  96.3 8.6 %collective-permute-start.7 = (bf16[32,7296]{1,0:T(8,128)(2,1)S(1)}, bf16[32,7296]{1,0:T(8,128)(2,1)S(1)}, u32[]{:S(2)}, u32[]{:S(2)}) collective-permute-start(bf16[32,7296]{1,0:T(8,128)(2,1)S(1)} %pad_maximum_fusion.refs_0_), channel_id=1, source_target_pairs={{0,1},{1,0},{2,3},{3,2},{4,5},{5,4},{6,7},{7,6},{8,9},{9,8},{10,11... | collective-permute-start | bytes 1400840 | tf_op jit(solution)/shard_map/ppermute | solution.py:24
  96.3 10.1 %collective-permute-start.8 = (bf16[32,7296]{1,0:T(8,128)(2,1)S(1)}, bf16[32,7296]{1,0:T(8,128)(2,1)S(1)}, u32[]{:S(2)}, u32[]{:S(2)}) collective-permute-start(bf16[32,7296]{1,0:T(8,128)(2,1)S(1)} %collective-permute-done.3.refs_1_), channel_id=1, source_target_pairs={{0,1},{1,0},{2,3},{3,2},{4,5},{5,4},{6,7},{7,6},{8,9},{9,8},{10,11... | collective-permute-start | bytes 1400840 | tf_op jit(solution)/shard_map/ppermute | solution.py:24
  96.8 9.6 %collective-permute-start.9 = (bf16[32,7296]{1,0:T(8,128)(2,1)S(1)}, bf16[32,7296]{1,0:T(8,128)(2,1)S(1)}, u32[]{:S(2)}, u32[]{:S(2)}) collective-permute-start(bf16[32,7296]{1,0:T(8,128)(2,1)S(1)} %collective-permute-done.4.refs_2_), channel_id=1, source_target_pairs={{0,1},{1,0},{2,3},{3,2},{4,5},{5,4},{6,7},{7,6},{8,9},{9,8},{10,11... | collective-permute-start | bytes 1400840 | tf_op jit(solution)/shard_map/ppermute | solution.py:24
  96.8 8.1 %collective-permute-start.5 = (bf16[32,3584]{1,0:T(8,128)(2,1)S(1)}, bf16[32,3584]{1,0:T(8,128)(2,1)S(1)}, u32[]{:S(2)}, u32[]{:S(2)}) collective-permute-start(bf16[32,3584]{1,0:T(8,128)(2,1)S(1)} %slice.39), channel_id=1, source_target_pairs={{0,2},{2,0},{4,6},{6,4},{8,10},{10,8},{12,14},{14,12},{16,18},{18,... | collective-permute-start | bytes 688136 | tf_op jit(solution)/shard_map/ppermute | solution.py:24
  102.2 4.3 %collective-permute-start.11 = (bf16[32,3712]{1,0:T(8,128)(2,1)S(1)}, bf16[32,3712]{1,0:T(8,128)(2,1)S(1)}, u32[]{:S(2)}, u32[]{:S(2)}) collective-permute-start(bf16[32,3712]{1,0:T(8,128)(2,1)S(1)} %collective-permute-done.6.refs_4_), channel_id=1, source_target_pairs={{0,1},{1,0},{2,3},{3,2},{4,5},{5,4},{6,7},{7,6},{8,9},{9,8},{10,11... | collective-permute-start | bytes 712712 | tf_op jit(solution)/shard_map/ppermute | solution.py:24
  104.9 1.5 collective-permute-start.10
  104.9 10.2 %slice-start.1 = ((s8[7340032]{0:T(1024)(128)(4,1)}), s8[3145728]{0:T(1024)(128)(4,1)S(1)}, s32[]{:S(2)}) async-start(s8[7340032]{0:T(1024)(128)(4,1)} %bitcast.25), calls=%async_computation.3 | async-start | bytes 6291456
  114.9 3.9 %collective-permute-start.12 = (bf16[128,7168]{1,0:T(8,128)(2,1)S(1)}, bf16[128,7168]{1,0:T(8,128)(2,1)S(1)}, u32[]{:S(2)}, u32[]{:S(2)}) collective-permute-start(bf16[128,7168]{1,0:T(8,128)(2,1)S(1)} %get-tuple-element.5), channel_id=1, source_target_pairs={{0,1},{1,0},{2,3},{3,2},{4,5},{5,4},{6,7},{7,6},{8,9},{9,8},{10,11... | collective-permute-start | bytes 5505032 | tf_op jit(solution)/shard_map/ppermute | solution.py:24
  119.1 7.7 %collective-permute-start.13 = (bf16[32,3584]{1,0:T(8,128)(2,1)S(1)}, bf16[32,3584]{1,0:T(8,128)(2,1)S(1)}, u32[]{:S(2)}, u32[]{:S(2)}) collective-permute-start(bf16[32,3584]{1,0:T(8,128)(2,1)S(1)} %get-tuple-element.13), channel_id=1, source_target_pairs={{0,4},{2,6},{4,0},{6,2},{8,12},{10,14},{12,8},{14,10},{16,20},{18,... | collective-permute-start | bytes 688136 | tf_op jit(solution)/shard_map/ppermute | solution.py:24
  120.5 7.4 %collective-permute-start.15 = (bf16[32,3584]{1,0:T(8,128)(2,1)S(1)}, bf16[32,3584]{1,0:T(8,128)(2,1)S(1)}, u32[]{:S(2)}, u32[]{:S(2)}) collective-permute-start(bf16[32,3584]{1,0:T(8,128)(2,1)S(1)} %get-tuple-element.14), channel_id=1, source_target_pairs={{0,2},{2,0},{4,6},{6,4},{8,10},{10,8},{12,14},{14,12},{16,18},{18,... | collective-permute-start | bytes 688136 | tf_op jit(solution)/shard_map/ppermute | solution.py:24
  126.9 11.8 %collective-permute-start.14 = (bf16[32,7168]{1,0:T(8,128)(2,1)S(1)}, bf16[32,7168]{1,0:T(8,128)(2,1)S(1)}, u32[]{:S(2)}, u32[]{:S(2)}) collective-permute-start(bf16[32,7168]{1,0:T(8,128)(2,1)S(1)} %pad_maximum_fusion.1), channel_id=1, source_target_pairs={{0,2},{2,0},{4,6},{6,4},{8,10},{10,8},{12,14},{14,12},{16,18},{18,... | collective-permute-start | bytes 1376264 | tf_op jit(solution)/shard_map/ppermute | solution.py:24
  128.0 11.6 %collective-permute-start.16 = (bf16[32,7168]{1,0:T(8,128)(2,1)S(1)}, bf16[32,7168]{1,0:T(8,128)(2,1)S(1)}, u32[]{:S(2)}, u32[]{:S(2)}) collective-permute-start(bf16[32,7168]{1,0:T(8,128)(2,1)S(1)} %pad_maximum_fusion.2), channel_id=1, source_target_pairs={{0,4},{2,6},{4,0},{6,2},{8,12},{10,14},{12,8},{14,10},{16,20},{18,... | collective-permute-start | bytes 1376264 | tf_op jit(solution)/shard_map/ppermute | solution.py:24
  139.8 9.6 %collective-permute-start.17 = (bf16[16,7168]{1,0:T(8,128)(2,1)S(1)}, bf16[16,7168]{1,0:T(8,128)(2,1)S(1)}, u32[]{:S(2)}, u32[]{:S(2)}) collective-permute-start(bf16[16,7168]{1,0:T(8,128)(2,1)S(1)} %split.78), channel_id=1, source_target_pairs={{0,16},{2,18},{4,20},{6,22},{8,24},{10,26},{12,28},{14,30},{16,0},... | collective-permute-start | bytes 688136 | tf_op jit(solution)/shard_map/ppermute | solution.py:24
  149.5 5.1 %collective-permute-start.18 = (bf16[8,7168]{1,0:T(8,128)(2,1)S(1)}, bf16[8,7168]{1,0:T(8,128)(2,1)S(1)}, u32[]{:S(2)}, u32[]{:S(2)}) collective-permute-start(bf16[8,7168]{1,0:T(8,128)(2,1)S(1)} %split.79), channel_id=1, source_target_pairs={{0,8},{2,10},{4,12},{6,14},{8,0},{10,2},{12,4},{14,6},{16,24},{18,... | collective-permute-start | bytes 344072 | tf_op jit(solution)/shard_map/ppermute | solution.py:24

commit v3 on v2

--- a/solution.py
+++ b/solution.py
@@ -32,92 +32,246 @@
 CHUNKS = 4
 
 
-def read_rows(sets, width, half, at, size):
-    parts = []
-    for own, near_x, near_y, low, high in sets:
-        for ref in (own, near_x, near_y):
-            parts.append(ref[:, pl.ds(at, size)])
-        if half == 0:
-            parts.append(low[:, pl.ds(at, size)])
+def vmem_spec():
+    return pl.BlockSpec(memory_space=pltpu.VMEM)
+
+
+def any_spec():
+    return pl.BlockSpec(memory_space=pl.ANY)
+
+
+def span(n, size):
+    return pl.ds(pl.multiple_of(n * size, size), size)
+
+
+def values_kernel(context, w_uv, w_o, part, values, uv_buf, o_buf, uv_sems, o_sems):
+    heads, _, dim = w_uv.shape
+    groups = uv_sems.shape[0]
+    step = heads // groups
+    chunks, depth, width = o_buf.shape
+
+    def copy_uv(g):
+        own = pl.ds(g * step, step)
+        return pltpu.make_async_copy(w_uv.at[own], uv_buf.at[own], uv_sems.at[g])
+
+    def copy_o(n):
+        rows = pl.ds(n * depth, depth)
+        return pltpu.make_async_copy(w_o.at[rows, pl.ds(0, width)], o_buf.at[n], o_sems.at[n])
+
+    for g in range(groups):
+        copy_uv(g).start()
+    for n in range(chunks):
+        copy_o(n).start()
+    for g in range(groups):
+        copy_uv(g).wait()
+        for h in range(g * step, (g + 1) * step):
+            values[:, h * dim : (h + 1) * dim] = jnp.dot(
+                context[h], uv_buf[h], preferred_element_type=jnp.float32
+            ).astype(jnp.bfloat16)
+    for n in range(chunks):
+        copy_o(n).wait()
+        product = jnp.dot(
+            values[:, n * depth : (n + 1) * depth], o_buf[n], preferred_element_type=jnp.float32
+        )
+        if n == 0:
+            part[...] = product
         else:
-            parts.append(high[:, pl.ds(pl.multiple_of(at - width // 2, 128), size)])
-    return jnp.concatenate(parts, axis=0)
-
-
-def expert_kernel(set_count, *refs):
+            part[...] += product
+
+
+def values_and_first(context, w_uv, w_o, width):
+    heads, rows, latent = context.shape
+    depth = w_o.shape[0]
+    chunks = 8
+    groups = 4 if heads % 4 == 0 else 1
+    return pl.pallas_call(
+        values_kernel,
+        out_shape=(
+            jax.ShapeDtypeStruct((rows, width), jnp.float32),
+            jax.ShapeDtypeStruct((rows, depth), jnp.bfloat16),
+        ),
+        in_specs=[vmem_spec(), any_spec(), any_spec()],
+        out_specs=(vmem_spec(), vmem_spec()),
+        scratch_shapes=[
+            pltpu.VMEM(w_uv.shape, jnp.bfloat16),
+            pltpu.VMEM((chunks, depth // chunks, width), jnp.bfloat16),
+            pltpu.SemaphoreType.DMA((groups,)),
+            pltpu.SemaphoreType.DMA((chunks,)),
+        ],
+        compiler_params=pltpu.CompilerParams(vmem_limit_bytes=44 << 20),
+        cost_estimate=pl.CostEstimate(
+            flops=2 * rows * depth * (width + latent),
+            bytes_accessed=2 * depth * (width + latent),
+            transcendentals=0,
+        ),
+        name="values_and_first",
+    )(context, w_uv, w_o)
+
+
+def columns_kernel(start, values, w_o, part, o_buf, o_sems):
+    chunks, depth, width = o_buf.shape
+
+    def copy_o(n):
+        rows = pl.ds(n * depth, depth)
+        return pltpu.make_async_copy(w_o.at[rows, pl.ds(start, width)], o_buf.at[n], o_sems.at[n])
+
+    for n in range(chunks):
+        copy_o(n).start()
+    for n in range(chunks):
+        copy_o(n).wait()
+        product = jnp.dot(
+            values[:, n * depth : (n + 1) * depth], o_buf[n], preferred_element_type=jnp.float32
+        )
+        if n == 0:
+            part[...] = product
+        else:
+            part[...] += product
+
+
+def more_columns(values, w_o, start, width):
+    rows, depth = values.shape
+    chunks = 8
+    return pl.pallas_call(
+        functools.partial(columns_kernel, start),
+        out_shape=jax.ShapeDtypeStruct((rows, width), jnp.float32),
+        in_specs=[vmem_spec(), any_spec()],
+        out_specs=vmem_spec(),
+        scratch_shapes=[
+            pltpu.VMEM((chunks, depth // chunks, width), jnp.bfloat16),
+            pltpu.SemaphoreType.DMA((chunks,)),
+        ],
+        compiler_params=pltpu.CompilerParams(vmem_limit_bytes=24 << 20),
+        cost_estimate=pl.CostEstimate(
+            flops=2 * rows * depth * width, bytes_accessed=2 * depth * width, transcendentals=0
+        ),
+        name="more_columns",
+    )(values, w_o)
+
+
+def first_kernel(set_count, *refs):
+    flat, refs = refs[: 4 * set_count], refs[4 * set_count :]
+    w_gate, w_up, gate_acc, up_acc, gate_buf, up_buf, sems = refs
+    chunks, size, _ = gate_buf.shape
+
+    def copies_in(n):
+        return (
+            pltpu.make_async_copy(w_gate.at[0, span(n, size)], gate_buf.at[n], sems.at[0, n]),
+            pltpu.make_async_copy(w_up.at[0, span(n, size)], up_buf.at[n], sems.at[1, n]),
+        )
+
+    for n in range(chunks):
+        for copy in copies_in(n):
+            copy.start()
+    gate_acc[...] = jnp.zeros_like(gate_acc)
+    up_acc[...] = jnp.zeros_like(up_acc)
+
+    @pl.loop(0, chunks)
+    def _(n):
+        for copy in copies_in(n):
+            copy.wait()
+        rows = jnp.concatenate([ref[:, span(n, size)] for ref in flat], axis=0)
+        gate_acc[...] += jnp.dot(rows, gate_buf[n], preferred_element_type=jnp.float32)
+        up_acc[...] += jnp.dot(rows, up_buf[n], preferred_element_type=jnp.float32)
+
+
+def experts_first(sets, w_gate, w_up):
+    width, hidden_units = w_gate.shape[1:]
+    size = width // CHUNKS
+    flat = [piece for pieces in sets for piece in pieces]
+    rows = sum(piece.shape[0] for piece in flat)
+    sums = jax.ShapeDtypeStruct((rows, hidden_units), jnp.float32)
+    return pl.pallas_call(
+        functools.partial(first_kernel, len(sets)),
+        out_shape=(sums, sums),
+        in_specs=[vmem_spec()] * len(flat) + [any_spec()] * 2,
+        out_specs=(vmem_spec(), vmem_spec()),
+        scratch_shapes=[
+            pltpu.VMEM((CHUNKS // 2, size, hidden_units), jnp.bfloat16),
+            pltpu.VMEM((CHUNKS // 2, size, hidden_units), jnp.bfloat16),
+            pltpu.SemaphoreType.DMA((2, CHUNKS // 2)),
+        ],
+        compiler_params=pltpu.CompilerParams(vmem_limit_bytes=32 << 20),
+        cost_estimate=pl.CostEstimate(
+            flops=2 * rows * width * hidden_units,
+            bytes_accessed=2 * width * hidden_units + rows * width,
+            transcendentals=0,
+        ),
+        name="experts_first",
+    )(*flat, w_gate, w_up)
+
+
+def far_kernel(set_count, *refs):
     flat, refs = refs[: 5 * set_count], refs[5 * set_count :]
     sets = [flat[5 * n : 5 * n + 5] for n in range(set_count)]
-    mask, w_gate, w_up, w_down, far, kept, gate_buf, up_buf, down_buf, gate_acc, up_acc, act, sems = refs
-    width = w_gate.shape[1]
-    size = width // CHUNKS
+    mask, gate_first, up_first, w_gate, w_up, w_down, far, kept = refs[:8]
+    gate_buf, up_buf, down_buf, gate_acc, up_acc, act, sems = refs[8:]
+    chunks, size, _ = gate_buf.shape
+    half = w_gate.shape[1] // 2
     half_rows = far.shape[0]
 
-    def span(n):
-        return pl.ds(pl.multiple_of(n * size, size), size)
-
     def copies_in(n):
+        rows = pl.ds(half + n * size, size)
         return (
-            pltpu.make_async_copy(w_gate.at[0, span(n)], gate_buf.at[n], sems.at[0, n]),
-            pltpu.make_async_copy(w_up.at[0, span(n)], up_buf.at[n], sems.at[1, n]),
+            pltpu.make_async_copy(w_gate.at[0, rows], gate_buf.at[n], sems.at[0, n]),
+            pltpu.make_async_copy(w_up.at[0, rows], up_buf.at[n], sems.at[1, n]),
         )
 
     def copy_down(n):
-        return pltpu.make_async_copy(w_down.at[0, :, span(n)], down_buf.at[n], sems.at[2, n])
-
-    for n in range(CHUNKS):
+        return pltpu.make_async_copy(w_down.at[0, :, span(n, size)], down_buf.at[n], sems.at[2, n])
+
+    for n in range(chunks):
         for copy in copies_in(n):
             copy.start()
     for n in range(CHUNKS):
         copy_down(n).start()
-    gate_acc[...] = jnp.zeros_like(gate_acc)
-    up_acc[...] = jnp.zeros_like(up_acc)
-    for half in range(2):
-
-        @pl.loop(half * CHUNKS // 2, (half + 1) * CHUNKS // 2)
-        def _(n):
-            for copy in copies_in(n):
-                copy.wait()
-            rows = read_rows(sets, width, half, pl.multiple_of(n * size, size), size)
-            gate_acc[...] += jnp.dot(rows, gate_buf[n], preferred_element_type=jnp.float32)
-            up_acc[...] += jnp.dot(rows, up_buf[n], preferred_element_type=jnp.float32)
-
     tails = []
     for own, near_x, near_y, low, high in sets:
-        tails += [ref[:, width:] for ref in (own, near_x, near_y)] + [high[:, width // 2 :]]
+        tails += [ref[:, half:] for ref in (own, near_x, near_y)] + [high[:, size:]]
     terms = jnp.concatenate(tails, axis=0).astype(jnp.float32)
-    gates = jnp.sum(terms * mask[...], axis=1, keepdims=True)
-    gated = gate_acc[...]
-    act[...] = (gated / (1.0 + jnp.exp(-gated)) * up_acc[...] * gates).astype(jnp.bfloat16)
+    gates = jnp.sum(terms * mask[0:1], axis=1, keepdims=True)
+    factors = jnp.sum(terms * mask[1:2], axis=1, keepdims=True)
+    for n in range(chunks):
+        parts = []
+        for own, near_x, near_y, low, high in sets:
+            parts += [ref[:, n * size : (n + 1) * size] for ref in (own, near_x, near_y)]
+            parts.append((low, high)[n][:, :size])
+        rows = jnp.concatenate(parts, axis=0)
+        for copy in copies_in(n):
+            copy.wait()
+        before = (gate_first, up_first) if n == 0 else (gate_acc, up_acc)
+        gate_acc[...] = before[0][...] + jnp.dot(
+            rows, gate_buf[n], preferred_element_type=jnp.float32
+        )
+        up_acc[...] = before[1][...] + jnp.dot(rows, up_buf[n], preferred_element_type=jnp.float32)
+    gated = gate_acc[...] * factors
+    raised = up_acc[...] * factors
+    act[...] = (gated / (1.0 + jnp.exp(-gated)) * raised * gates).astype(jnp.bfloat16)
     kept[...] = act[:half_rows]
 
     @pl.loop(0, CHUNKS)
     def _(n):
         copy_down(n).wait()
-        far[:, span(n)] = jnp.dot(
+        far[:, span(n, size)] = jnp.dot(
             act[half_rows:], down_buf[n], preferred_element_type=jnp.float32
         ).astype(jnp.bfloat16)
 
 
-def vmem_spec():
-    return pl.BlockSpec(memory_space=pltpu.VMEM)
-
-
-def experts_far(sets, mask, w_gate, w_up, w_down):
+def experts_far(sets, mask, sums, w_gate, w_up, w_down):
     width, hidden_units = w_gate.shape[1:]
-    rows = sum(piece.shape[0] for pieces in sets for piece in pieces[:4])
+    rows = sums[0].shape[0]
     size = width // CHUNKS
     flat = [piece for pieces in sets for piece in pieces]
     return pl.pallas_call(
-        functools.partial(expert_kernel, len(sets)),
+        functools.partial(far_kernel, len(sets)),
         out_shape=(
             jax.ShapeDtypeStruct((rows // 2, width), jnp.bfloat16),
             jax.ShapeDtypeStruct((rows // 2, hidden_units), jnp.bfloat16),
         ),
-        in_specs=[vmem_spec()] * (len(flat) + 1) + [pl.BlockSpec(memory_space=pl.ANY)] * 3,
+        in_specs=[vmem_spec()] * (len(flat) + 3) + [any_spec()] * 3,
         out_specs=(vmem_spec(), vmem_spec()),
         scratch_shapes=[
-            pltpu.VMEM((CHUNKS, size, hidden_units), jnp.bfloat16),
-            pltpu.VMEM((CHUNKS, size, hidden_units), jnp.bfloat16),
+            pltpu.VMEM((CHUNKS // 2, size, hidden_units), jnp.bfloat16),
+            pltpu.VMEM((CHUNKS // 2, size, hidden_units), jnp.bfloat16),
             pltpu.VMEM((CHUNKS, hidden_units, size), jnp.bfloat16),
             pltpu.VMEM((rows, hidden_units), jnp.float32),
             pltpu.VMEM((rows, hidden_units), jnp.float32),
@@ -126,12 +280,12 @@
         ],
         compiler_params=pltpu.CompilerParams(vmem_limit_bytes=48 << 20),
         cost_estimate=pl.CostEstimate(
-            flops=5 * rows * width * hidden_units,
-            bytes_accessed=6 * width * hidden_units + 3 * rows * width,
+            flops=3 * rows * width * hidden_units,
+            bytes_accessed=4 * width * hidden_units + 3 * rows * width,
             transcendentals=rows * hidden_units,
         ),
         name="experts_far",
-    )(*flat, mask, w_gate, w_up, w_down)
+    )(*flat, mask, *sums, w_gate, w_up, w_down)
 
 
 def down_kernel(kept, w_down, near, down_buf, sems):
@@ -160,7 +314,7 @@
     return pl.pallas_call(
         down_kernel,
         out_shape=jax.ShapeDtypeStruct((rows, width), jnp.bfloat16),
-        in_specs=[vmem_spec(), pl.BlockSpec(memory_space=pl.ANY)],
+        in_specs=[vmem_spec(), any_spec()],
         out_specs=vmem_spec(),
         scratch_shapes=[
             pltpu.VMEM((CHUNKS, hidden_units, size), jnp.bfloat16),
@@ -214,18 +368,16 @@
     return lax.all_gather(part, "ep", axis=1, tiled=True)
 
 
-def gather_rows(rows):
-    inner_x, inner_y, *outer = bits_of("dp")
-    for bit in outer:
+def line_of(rows):
+    for bit in bits_of("dp")[2:]:
         rows = jnp.concatenate([rows, flip(rows, "dp", bit)], axis=0)
-    half = rows.shape[1] // 2 // 128 * 128
-    near_x = flip(rows, "dp", inner_x)
-    near_y = flip(rows, "dp", inner_y)
-    low = flip(near_y[:, :half], "dp", inner_x)
-    high = flip(near_x[:, half:], "dp", inner_y)
-    sets = [(rows, near_x, near_y, low, high)]
+    return rows
+
+
+def all_sets(pieces):
+    sets = [pieces]
     for bit in bits_of("ep"):
-        sets = sets + [tuple(flip(piece, "ep", bit) for piece in pieces) for pieces in sets]
+        sets = sets + [tuple(flip(piece, "ep", bit) for piece in one) for one in sets]
     return sets
 
 
@@ -275,6 +427,15 @@
     return mine + flip(other, "ep", 1)
 
 
+def three_terms(x):
+    terms = []
+    for _ in range(3):
+        term = lax.reduce_precision(x, 8, 7)
+        terms.append(narrow(term))
+        x = x - term
+    return terms
+
+
 def per_device(
     residual,
     queries,
@@ -315,34 +476,54 @@
     row_max = jnp.max(scores, axis=2, keepdims=True)
     weights = jnp.where(in_range, jnp.exp(scores - row_max), 0.0)
     prob_rows = (weights / jnp.sum(weights, axis=2, keepdims=True)).astype(jnp.bfloat16)
-    context = jnp.einsum(
-        "rht,rtl->rhl", prob_rows, latents[:, :, :LAT], preferred_element_type=jnp.float32
-    ).astype(jnp.bfloat16)
-    values = jnp.einsum("rhl,hlv->rhv", context, w_uv, preferred_element_type=jnp.float32).astype(
-        jnp.bfloat16
-    )
-    values = values.reshape(replica_rows, heads_dev * V_DIM)
+    context = narrow(
+        jnp.einsum("rht,rtl->rhl", prob_rows, latents[:, :, :LAT], preferred_element_type=jnp.float32)
+    )
     width = residual.shape[1]
-    attended = head_sums(jnp.dot(values, w_o, preferred_element_type=jnp.float32))
-    hidden = residual.astype(jnp.float32) + attended
-    normed = (
-        hidden * lax.rsqrt(jnp.mean(hidden * hidden, axis=1, keepdims=True) + norm_eps) * norm_gain
-    ).astype(jnp.bfloat16)
+    half, size = width // 2, width // CHUNKS
+    tokens = residual.astype(jnp.float32)
+
+    part, values = values_and_first(jnp.transpose(context, (1, 0, 2)), w_uv, w_o, half)
+    hidden_a = tokens[:, :half] + head_sums(part)
+    rows_a = narrow(hidden_a * norm_gain[None, :half])
+    values, rows_a = lax.optimization_barrier((values, rows_a))
+    inner_x, inner_y, *outer = bits_of("dp")
+    parts_b = [more_columns(values, w_o, half, size)]
+    came = flip(rows_a, "dp", outer[0])
+    held_a = jnp.concatenate([rows_a, came], axis=0)
+    values, held_a = lax.optimization_barrier((values, held_a))
+    parts_b.append(more_columns(values, w_o, half + size, size))
+    for bit in outer[1:]:
+        held_a = jnp.concatenate([held_a, flip(held_a, "dp", bit)], axis=0)
+    x_a = flip(held_a, "dp", inner_x)
+    y_a = flip(held_a, "dp", inner_y)
+
+    hidden_b = tokens[:, half:] + head_sums(jnp.concatenate(parts_b, axis=1))
+    squares = jnp.sum(hidden_a * hidden_a, axis=1, keepdims=True) + jnp.sum(
+        hidden_b * hidden_b, axis=1, keepdims=True
+    )
+    factor = lax.rsqrt(squares / width + norm_eps)
     expert_ids = jnp.arange(replicas, dtype=jnp.int32)
     matches = experts[:, :, None] == expert_ids[None, None, :]
     gate_sum = jnp.sum(jnp.where(matches, gate_weights[:, :, None], 0.0), axis=1)
-    terms = []
-    left = gate_sum
-    for _ in range(3):
-        term = lax.reduce_precision(left, 8, 7)
-        terms.append(term.astype(jnp.bfloat16))
-        left = left - term
-    terms.append(jnp.zeros((gate_sum.shape[0], GATE_COLS - 3 * replicas), jnp.bfloat16))
-    sets = gather_rows(jnp.concatenate([normed] + terms, axis=1))
-    columns = jnp.arange(GATE_COLS, dtype=jnp.int32)[None, :]
-    chosen = (columns < 3 * replicas) & (columns % replicas == own_replica)
-    far, kept = experts_far(sets, chosen.astype(jnp.float32), w_gate, w_up, w_down)
+    terms = three_terms(gate_sum) + three_terms(factor)
+    terms.append(jnp.zeros((tokens.shape[0], GATE_COLS - 3 * replicas - 3), jnp.bfloat16))
+    rows_b = jnp.concatenate([narrow(hidden_b * norm_gain[None, half:])] + terms, axis=1)
+    held_b = line_of(rows_b)
+    d_a = flip(y_a, "dp", inner_x)
+    sums = experts_first(all_sets((held_a, x_a, y_a, d_a)), w_gate, w_up)
+    x_b = flip(held_b, "dp", inner_x)
+    y_b = flip(held_b, "dp", inner_y)
+    low_b = flip(y_b[:, :size], "dp", inner_x)
+    high_b = flip(x_b[:, size:], "dp", inner_y)
+    columns = jnp.arange(GATE_COLS, dtype=jnp.int32)
+    gate_mask = (columns < 3 * replicas) & (columns % replicas == own_replica)
+    factor_mask = (columns >= 3 * replicas) & (columns < 3 * replicas + 3)
+    mask = jnp.stack([gate_mask, factor_mask]).astype(jnp.float32)
+    sets_b = all_sets((held_b, x_b, y_b, low_b, high_b))
+    far, kept = experts_far(sets_b, mask, sums, w_gate, w_up, w_down)
     mixture = scatter_sums(experts_near(kept, w_down), far)
+    hidden = jnp.concatenate([hidden_a, hidden_b], axis=1)
     layer_out = (hidden + mixture).astype(jnp.bfloat16)
     return (layer_out, arrivals)
 

time: 156 us -> 165 us (1.058)
  matrix products: 29 us -> 5.24 us
  Pallas kernels: 11.2 us -> 33.9 us
  local copies, waits for them, and re-layouts: 4.2 us -> 14.2 us
  waiting for transfers between devices: 82 us -> 73.3 us
  starting transfers between devices: 22.7 us -> 30.1 us
    dot_general x2 -> x0, matrix products: 23.8 us -> none  [the longest x1 20.7 us: per_device(): jnp.dot(values, w_o, preferred_element_type=jnp.float32)]
    pallas_call x1 -> x5, Pallas kernels: 8.51 us -> 31.2 us  [the longest x2 11.5 us: more_columns(): pl.pallas_call(functools.partial(columns_kernel, start), out_shape=jax.Sh...]
    unnamed x19 -> x28, local copies, waits for them, and re-layouts: 0.76 us -> 10.2 us
    ppermute x19 -> x29, waiting for transfers between devices: 68.2 us -> 60.2 us  [flip(): return lax.ppermute(x, axis, pairs)]
    ppermute x19 -> x29, starting transfers between devices: 10.8 us -> 18.1 us  [flip(): return lax.ppermute(x, axis, pairs)]
  transfers between devices with their start and end apart: 21 -> 31, of which waited for: 16 -> 19; matrix products, arithmetic and copies ran while one was open for 1% -> 2% of each run, Pallas kernels for 2% -> 7%
where the time goes in v3:
time: 165 us
  waiting for transfers between devices  73.3 us (44%)
  Pallas kernels  33.9 us (21%)
  starting transfers between devices  30.1 us (18%)
  local copies, waits for them, and re-layouts  14.2 us (9%)
  matrix products  5.24 us (3%)
  other arithmetic  4.71 us (3%)
  blocking collectives  2 us (1%)
    ppermute x29, waiting for transfers between devices, flip(): return lax.ppermute(x, axis, pairs)  60.2 us
    ppermute x29, starting transfers between devices, flip(): return lax.ppermute(x, axis, pairs)  18.1 us
    pallas_call x2, Pallas kernels, more_columns(): pl.pallas_call(functools.partial(columns_kernel, start), out_shape=jax.Sh...  11.5 us
    pallas_call x1, Pallas kernels, values_and_first(): pl.pallas_call(values_kernel, out_shape=(jax.ShapeDtypeStruct((rows, widt...  10.4 us
    unnamed x28, local copies, waits for them, and re-layouts  10.2 us
    all_to_all x1, starting transfers between devices, migrate(): met = lax.all_to_all(outbox, 'dp', split_axis=0, concat_axis=0)  8.44 us
    all_to_all x1, waiting for transfers between devices, migrate(): met = lax.all_to_all(outbox, 'dp', split_axis=0, concat_axis=0)  6.89 us
    pallas_call x1, Pallas kernels, experts_far(): pl.pallas_call(functools.partial(far_kernel, len(sets)), out_shape=(jax.S...  6.28 us
  transfers between devices with their start and end apart: 31, of which 19 were waited for; matrix products, arithmetic and copies ran while one was open for 2% of the time, Pallas kernels for 7%

profile of v3, /device:TPU:0, one launch (start us, length us, event | category | flops | bytes accessed | tf_op | source)
XLA Modules:
  0.0 164.5 jit_solution(8132648774334614843)
XLA Ops:
  2.4 2.0 %convolution_convert_fusion.1 = bf16[4,18432]{1,0:T(4,128)(2,1)} fusion(pred[4,16]{1,0:T(4,128)(4,1)S(1)} %get-tuple-element.27, bf16[16,36864]{1,0:T(8,128)(2,1)} %param.15, s32[]{:T(128)S(6)} %select_n.83), kind=kOutput, calls=%fused_computation.3 | convolution fusion | flops 2433024 | bytes 737348 | tf_op jit(solution)/shard_map/dot_general | solution.py:358
  4.4 8.4 %all-to-all-start = ((bf16[16,4,1152]{2,1,0:T(4,128)(2,1)}), bf16[16,4,1152]{2,1,0:T(4,128)(2,1)S(1)}, u32[]{:S(2)}, u32[]{:S(2)}) async-start(bf16[16,4,1152]{2,1,0:T(4,128)(2,1)} %bitcast.1), calls=%async_computation | async-start | bytes 294912 | tf_op jit(solution)/shard_map/all_to_all | solution.py:360
  13.8 6.9 %all-to-all-done = bf16[16,4,1152]{2,1,0:T(4,128)(2,1)S(1)} async-done(((bf16[16,4,1152]{2,1,0:T(4,128)(2,1)}), bf16[16,4,1152]{2,1,0:T(4,128)(2,1)S(1)}, u32[]{:S(2)}, u32[]{:S(2)}) %all-to-all-start) | async-done | bytes 147488 | tf_op jit(solution)/shard_map/all_to_all | solution.py:360
  21.6 3.5 %all-to-all-start.1 = ((bf16[16,4,1152]{2,1,0:T(4,128)(2,1)}), bf16[16,4,1152]{2,1,0:T(4,128)(2,1)S(1)}, u32[]{:S(2)}, u32[]{:S(2)}) async-start(bf16[16,4,1152]{2,1,0:T(4,128)(2,1)} %reshape.211), calls=%async_computation.1 | async-start | bytes 294912 | tf_op jit(solution)/shard_map/all_to_all | solution.py:364
  26.7 6.2 %all-to-all-done.1 = bf16[16,4,1152]{2,1,0:T(4,128)(2,1)S(1)} async-done(((bf16[16,4,1152]{2,1,0:T(4,128)(2,1)}), bf16[16,4,1152]{2,1,0:T(4,128)(2,1)S(1)}, u32[]{:S(2)}, u32[]{:S(2)}) %all-to-all-start.1) | async-done | bytes 147488 | tf_op jit(solution)/shard_map/all_to_all | solution.py:364
  32.9 2.0 %all_gather.3 = bf16[4,36864]{1,0:T(4,128)(2,1)S(1)} all-gather(bf16[4,18432]{1,0:T(4,128)(2,1)S(1)} %bitcast.25), channel_id=1, replica_groups=mesh['dp'=16,'ep'=2] {'ep'}, dimensions={1}, use_global_device_ids=true | all-gather | bytes 442368 | tf_op jit(solution)/shard_map/all_gather | solution.py:368
  35.5 1.8 %reshape.213 = bf16[16,64,576]{2,1,0:T(8,128)(2,1)S(1)} reshape(bf16[16,36864]{1,0:T(8,128)(2,1)S(1)} %fusion.1) | data formatting | bytes 2359296 | tf_op jit(solution)/shard_map/reshape | solution.py:468
  39.5 2.2 %copy-done.2 = bf16[32,512,128]{2,1,0:T(8,128)(2,1)S(1)} copy-done((bf16[32,512,128]{2,1,0:T(8,128)(2,1)S(1)}, bf16[32,512,128]{2,1,0:T(8,128)(2,1)}, u32[]{:S(2)}) %copy-start.2) | copy-done | bytes 4194328
  41.7 10.4 %values_and_first.1 = (f32[16,3584]{1,0:T(8,128)S(1)}, bf16[16,4096]{1,0:T(8,128)(2,1)S(1)}) custom-call(bf16[32,16,512]{2,1,0:T(8,128)(2,1)S(1)} %bitcast.24, bf16[32,512,128]{2,1,0:T(8,128)(2,1)S(1)} %copy-done.2, bf16[4096,7168]{1,0:T(8,128)(2,1)} %w_o.5), custom_call_target="tpu_custom_call" | custom-call | flops 536870912 | bytes 33554432 | tf_op jit(solution)/shard_map/values_and_first/pallas_call | solution.py:87
  54.6 5.7 %more_columns.2 = f32[16,1792]{1,0:T(8,128)S(1)} custom-call(bf16[16,4096]{1,0:T(8,128)(2,1)S(1)} %get-tuple-element.16.values, bf16[4096,7168]{1,0:T(8,128)(2,1)} %w_o.5), custom_call_target="tpu_custom_call" | custom-call | flops 234881024 | bytes 14680064 | tf_op jit(solution)/shard_map/more_columns/pallas_call | solution.py:134
  60.4 5.7 %more_columns.3 = f32[16,1792]{1,0:T(8,128)S(1)} custom-call(bf16[16,4096]{1,0:T(8,128)(2,1)S(1)} %get-tuple-element.16.values, bf16[4096,7168]{1,0:T(8,128)(2,1)} %w_o.5), custom_call_target="tpu_custom_call" | custom-call | flops 234881024 | bytes 14680064 | tf_op jit(solution)/shard_map/more_columns/pallas_call | solution.py:134
  70.3 1.9 %collective-permute-done.3 = bf16[8,3712]{1,0:T(8,128)(2,1)S(1)} collective-permute-done((bf16[8,3712]{1,0:T(8,128)(2,1)S(1)}, bf16[8,3712]{1,0:T(8,128)(2,1)S(1)}, u32[]{:S(2)}, u32[]{:S(2)}) %collective-permute-start.3) | collective-permute-done | bytes 59424 | tf_op jit(solution)/shard_map/ppermute | solution.py:24
  73.3 7.1 %collective-permute-done.14 = bf16[16,3584]{1,0:T(8,128)(2,1)S(1)} collective-permute-done((bf16[16,3584]{1,0:T(8,128)(2,1)S(1)}, bf16[16,3584]{1,0:T(8,128)(2,1)S(1)}, u32[]{:S(2)}, u32[]{:S(2)}) %collective-permute-start.14) | collective-permute-done | bytes 114720 | tf_op jit(solution)/shard_map/ppermute | solution.py:24
  81.2 1.4 collective-permute-done.4
  84.1 1.5 collective-permute-start.5
  85.5 3.5 %collective-permute-done.16.refs_2_ = bf16[32,3584]{1,0:T(8,128)(2,1)S(1)} collective-permute-done((bf16[32,3584]{1,0:T(8,128)(2,1)S(1)}, bf16[32,3584]{1,0:T(8,128)(2,1)S(1)}, u32[]{:S(2)}, u32[]{:S(2)}) %collective-permute-start.16) | collective-permute-done | bytes 229408 | tf_op jit(solution)/shard_map/ppermute | solution.py:24
  89.7 2.4 %collective-permute-done.15.refs_1_ = bf16[32,3584]{1,0:T(8,128)(2,1)S(1)} collective-permute-done((bf16[32,3584]{1,0:T(8,128)(2,1)S(1)}, bf16[32,3584]{1,0:T(8,128)(2,1)S(1)}, u32[]{:S(2)}, u32[]{:S(2)}) %collective-permute-start.15) | collective-permute-done | bytes 229408 | tf_op jit(solution)/shard_map/ppermute | solution.py:24
  92.6 7.9 %collective-permute-done.17.refs_3_ = bf16[32,3584]{1,0:T(8,128)(2,1)S(1)} collective-permute-done((bf16[32,3584]{1,0:T(8,128)(2,1)S(1)}, bf16[32,3584]{1,0:T(8,128)(2,1)S(1)}, u32[]{:S(2)}, u32[]{:S(2)}) %collective-permute-start.17) | collective-permute-done | bytes 229408 | tf_op jit(solution)/shard_map/ppermute | solution.py:24
  101.4 1.7 %collective-permute-start.8 = (bf16[32,1920]{1,0:T(8,128)(2,1)S(1)}, bf16[32,1920]{1,0:T(8,128)(2,1)S(1)}, u32[]{:S(2)}, u32[]{:S(2)}) collective-permute-start(bf16[32,1920]{1,0:T(8,128)(2,1)S(1)} %slice.58), channel_id=1, source_target_pairs={{0,4},{2,6},{4,0},{6,2},{8,12},{10,14},{12,8},{14,10},{16,20},{18,... | collective-permute-start | bytes 368648 | tf_op jit(solution)/shard_map/ppermute | solution.py:24
  103.7 2.5 %collective-permute-done.7.refs_3_ = bf16[32,1792]{1,0:T(8,128)(2,1)S(1)} collective-permute-done((bf16[32,1792]{1,0:T(8,128)(2,1)S(1)}, bf16[32,1792]{1,0:T(8,128)(2,1)S(1)}, u32[]{:S(2)}, u32[]{:S(2)}) %collective-permute-start.7) | collective-permute-done | bytes 114720 | tf_op jit(solution)/shard_map/ppermute | solution.py:24
  107.4 3.1 %copy-done = bf16[1,7168,512]{2,1,0:T(8,128)(2,1)S(1)} copy-done((bf16[1,7168,512]{2,1,0:T(8,128)(2,1)S(1)}, bf16[1,7168,512]{2,1,0:T(8,128)(2,1)}, u32[]{:S(2)}) %copy-start) | copy-done | bytes 7340056
  110.5 3.1 %copy-done.1 = bf16[1,7168,512]{2,1,0:T(8,128)(2,1)S(1)} copy-done((bf16[1,7168,512]{2,1,0:T(8,128)(2,1)S(1)}, bf16[1,7168,512]{2,1,0:T(8,128)(2,1)}, u32[]{:S(2)}) %copy-start.1) | copy-done | bytes 7340056
  113.6 3.1 %experts_first.1 = (f32[256,512]{1,0:T(8,128)S(1)}, f32[256,512]{1,0:T(8,128)S(1)}) custom-call(bf16[32,3584]{1,0:T(8,128)(2,1)S(1)} %constant_dynamic-update-slice_fusion.refs_0_, bf16[32,3584]{1,0:T(8,128)(2,1)S(1)} %collective-permute-done.15.refs_1_, bf16[32,3584]{1,0:T(8,128)(2,1)S(1)} %collective-permute-done.16.refs_2_, ...), custom_call_target="tpu_custom_call" | custom-call | flops 1879048192 | bytes 9175040 | tf_op jit(solution)/shard_map/experts_first/pallas_call | solution.py:183
  116.7 6.3 %experts_far.1 = (bf16[128,7168]{1,0:T(8,128)(2,1)S(1)}, bf16[128,512]{1,0:T(8,128)(2,1)S(1)}) custom-call(bf16[32,3712]{1,0:T(8,128)(2,1)S(1)} %pad_maximum_fusion.2.refs_0_, bf16[32,3712]{1,0:T(8,128)(2,1)S(1)} %collective-permute-done.5.refs_1_, bf16[32,3712]{1,0:T(8,128)(2,1)S(1)} %collective-permute-done.6.refs_2_, ...), custom_call_target="tpu_custom_call" | custom-call | flops 2818572288 | bytes 20185088 | tf_op jit(solution)/shard_map/experts_far/pallas_call | solution.py:264
  124.2 2.6 %experts_near.1 = bf16[128,7168]{1,0:T(8,128)(2,1)S(1)} custom-call(bf16[128,512]{1,0:T(8,128)(2,1)S(1)} %get-tuple-element.20.kept, bf16[1,512,7168]{2,1,0:T(8,128)(2,1)S(1)} %bitcast.23), custom_call_target="tpu_custom_call" | custom-call | flops 939524096 | bytes 9175040 | tf_op jit(solution)/shard_map/experts_near/pallas_call | solution.py:314
  127.2 1.7 %collective-permute-start.23 = (bf16[32,3584]{1,0:T(8,128)(2,1)S(1)}, bf16[32,3584]{1,0:T(8,128)(2,1)S(1)}, u32[]{:S(2)}, u32[]{:S(2)}) collective-permute-start(bf16[32,3584]{1,0:T(8,128)(2,1)S(1)} %get-tuple-element.31), channel_id=1, source_target_pairs={{0,4},{2,6},{4,0},{6,2},{8,12},{10,14},{12,8},{14,10},{16,20},{18,... | collective-permute-start | bytes 688136 | tf_op jit(solution)/shard_map/ppermute | solution.py:24
  130.0 4.9 %collective-permute-done.23 = bf16[32,3584]{1,0:T(8,128)(2,1)S(1)} collective-permute-done((bf16[32,3584]{1,0:T(8,128)(2,1)S(1)}, bf16[32,3584]{1,0:T(8,128)(2,1)S(1)}, u32[]{:S(2)}, u32[]{:S(2)}) %collective-permute-start.23) | collective-permute-done | bytes 229408 | tf_op jit(solution)/shard_map/ppermute | solution.py:24
  135.0 1.4 collective-permute-start.24
  136.5 1.3 collective-permute-start.26
  137.9 9.0 %collective-permute-done.24 = bf16[32,7168]{1,0:T(8,128)(2,1)S(1)} collective-permute-done((bf16[32,7168]{1,0:T(8,128)(2,1)S(1)}, bf16[32,7168]{1,0:T(8,128)(2,1)S(1)}, u32[]{:S(2)}, u32[]{:S(2)}) %collective-permute-start.24) | collective-permute-done | bytes 458784 | tf_op jit(solution)/shard_map/ppermute | solution.py:24
  148.4 9.6 %collective-permute-done.27 = bf16[16,7168]{1,0:T(8,128)(2,1)S(1)} collective-permute-done((bf16[16,7168]{1,0:T(8,128)(2,1)S(1)}, bf16[16,7168]{1,0:T(8,128)(2,1)S(1)}, u32[]{:S(2)}, u32[]{:S(2)}) %collective-permute-start.27) | collective-permute-done | bytes 229408 | tf_op jit(solution)/shard_map/ppermute | solution.py:24
  158.1 5.0 %collective-permute-done.28 = bf16[8,7168]{1,0:T(8,128)(2,1)S(1)} collective-permute-done((bf16[8,7168]{1,0:T(8,128)(2,1)S(1)}, bf16[8,7168]{1,0:T(8,128)(2,1)S(1)}, u32[]{:S(2)}, u32[]{:S(2)}) %collective-permute-start.28) | collective-permute-done | bytes 114720 | tf_op jit(solution)/shard_map/ppermute | solution.py:24
  (122 shorter events, 27.4 us)
Async XLA Ops:
  4.4 30.6 %copy-start.3 = (bf16[16,36864]{1,0:T(8,128)(2,1)S(1)}, bf16[16,36864]{1,0:T(8,128)(2,1)}, u32[]{:S(2)}) copy-start(bf16[16,36864]{1,0:T(8,128)(2,1)} %param.15) | copy-start | bytes 3538948
  4.4 16.3 %all-to-all-start = ((bf16[16,4,1152]{2,1,0:T(4,128)(2,1)}), bf16[16,4,1152]{2,1,0:T(4,128)(2,1)S(1)}, u32[]{:S(2)}, u32[]{:S(2)}) async-start(bf16[16,4,1152]{2,1,0:T(4,128)(2,1)} %bitcast.1), calls=%async_computation | async-start | bytes 294912 | tf_op jit(solution)/shard_map/all_to_all | solution.py:360
  21.6 11.4 %all-to-all-start.1 = ((bf16[16,4,1152]{2,1,0:T(4,128)(2,1)}), bf16[16,4,1152]{2,1,0:T(4,128)(2,1)S(1)}, u32[]{:S(2)}, u32[]{:S(2)}) async-start(bf16[16,4,1152]{2,1,0:T(4,128)(2,1)} %reshape.211), calls=%async_computation.1 | async-start | bytes 294912 | tf_op jit(solution)/shard_map/all_to_all | solution.py:364
  52.1 1.4 collective-permute-start
  53.7 6.7 %collective-permute-start.1 = (bf16[8,3584]{1,0:T(8,128)(2,1)S(1)}, bf16[8,3584]{1,0:T(8,128)(2,1)S(1)}, u32[]{:S(2)}, u32[]{:S(2)}) collective-permute-start(bf16[8,3584]{1,0:T(8,128)(2,1)S(1)} %multiply_convert_fusion.1), channel_id=1, source_target_pairs={{0,8},{2,10},{4,12},{6,14},{8,0},{10,2},{12,4},{14,6},{16,24},{18,... | collective-permute-start | bytes 172040 | tf_op jit(solution)/shard_map/ppermute | solution.py:24
  66.2 1.4 collective-permute-start.2
  68.0 4.2 %collective-permute-start.3 = (bf16[8,3712]{1,0:T(8,128)(2,1)S(1)}, bf16[8,3712]{1,0:T(8,128)(2,1)S(1)}, u32[]{:S(2)}, u32[]{:S(2)}) collective-permute-start(bf16[8,3712]{1,0:T(8,128)(2,1)S(1)} %concatenate.33), channel_id=1, source_target_pairs={{0,8},{2,10},{4,12},{6,14},{8,0},{10,2},{12,4},{14,6},{16,24},{18,... | collective-permute-start | bytes 178184 | tf_op jit(solution)/shard_map/ppermute | solution.py:24
  69.2 11.2 %collective-permute-start.14 = (bf16[16,3584]{1,0:T(8,128)(2,1)S(1)}, bf16[16,3584]{1,0:T(8,128)(2,1)S(1)}, u32[]{:S(2)}, u32[]{:S(2)}) collective-permute-start(bf16[16,3584]{1,0:T(8,128)(2,1)S(1)} %pad_maximum_fusion.4), channel_id=1, source_target_pairs={{0,16},{2,18},{4,20},{6,22},{8,24},{10,26},{12,28},{14,30},{16,0},... | collective-permute-start | bytes 344072 | tf_op jit(solution)/shard_map/ppermute | solution.py:24
  72.2 10.5 %collective-permute-start.4 = (bf16[16,3712]{1,0:T(8,128)(2,1)S(1)}, bf16[16,3712]{1,0:T(8,128)(2,1)S(1)}, u32[]{:S(2)}, u32[]{:S(2)}) collective-permute-start(bf16[16,3712]{1,0:T(8,128)(2,1)S(1)} %pad_maximum_fusion.3), channel_id=1, source_target_pairs={{0,16},{2,18},{4,20},{6,22},{8,24},{10,26},{12,28},{14,30},{16,0},... | collective-permute-start | bytes 356360 | tf_op jit(solution)/shard_map/ppermute | solution.py:24
  80.4 8.6 %collective-permute-start.16 = (bf16[32,3584]{1,0:T(8,128)(2,1)S(1)}, bf16[32,3584]{1,0:T(8,128)(2,1)S(1)}, u32[]{:S(2)}, u32[]{:S(2)}) collective-permute-start(bf16[32,3584]{1,0:T(8,128)(2,1)S(1)} %constant_dynamic-update-slice_fusion.refs_0_), channel_id=1, source_target_pairs={{0,4},{2,6},{4,0},{6,2},{8,12},{10,14},{12,8},{14,10},{16,20},{18,... | collective-permute-start | bytes 688136 | tf_op jit(solution)/shard_map/ppermute | solution.py:24
  82.7 9.9 %collective-permute-start.6 = (bf16[32,3712]{1,0:T(8,128)(2,1)S(1)}, bf16[32,3712]{1,0:T(8,128)(2,1)S(1)}, u32[]{:S(2)}, u32[]{:S(2)}) collective-permute-start(bf16[32,3712]{1,0:T(8,128)(2,1)S(1)} %pad_maximum_fusion.2.refs_0_), channel_id=1, source_target_pairs={{0,4},{2,6},{4,0},{6,2},{8,12},{10,14},{12,8},{14,10},{16,20},{18,... | collective-permute-start | bytes 712712 | tf_op jit(solution)/shard_map/ppermute | solution.py:24
  83.5 8.5 %collective-permute-start.15 = (bf16[32,3584]{1,0:T(8,128)(2,1)S(1)}, bf16[32,3584]{1,0:T(8,128)(2,1)S(1)}, u32[]{:S(2)}, u32[]{:S(2)}) collective-permute-start(bf16[32,3584]{1,0:T(8,128)(2,1)S(1)} %constant_dynamic-update-slice_fusion.refs_0_), channel_id=1, source_target_pairs={{0,2},{2,0},{4,6},{6,4},{8,10},{10,8},{12,14},{14,12},{16,18},{18,... | collective-permute-start | bytes 688136 | tf_op jit(solution)/shard_map/ppermute | solution.py:24
  84.1 16.5 %collective-permute-start.5 = (bf16[32,3712]{1,0:T(8,128)(2,1)S(1)}, bf16[32,3712]{1,0:T(8,128)(2,1)S(1)}, u32[]{:S(2)}, u32[]{:S(2)}) collective-permute-start(bf16[32,3712]{1,0:T(8,128)(2,1)S(1)} %pad_maximum_fusion.2.refs_0_), channel_id=1, source_target_pairs={{0,2},{2,0},{4,6},{6,4},{8,10},{10,8},{12,14},{14,12},{16,18},{18,... | collective-permute-start | bytes 712712 | tf_op jit(solution)/shard_map/ppermute | solution.py:24
  89.0 11.5 %collective-permute-start.17 = (bf16[32,3584]{1,0:T(8,128)(2,1)S(1)}, bf16[32,3584]{1,0:T(8,128)(2,1)S(1)}, u32[]{:S(2)}, u32[]{:S(2)}) collective-permute-start(bf16[32,3584]{1,0:T(8,128)(2,1)S(1)} %collective-permute-done.16.refs_2_), channel_id=1, source_target_pairs={{0,2},{2,0},{4,6},{6,4},{8,10},{10,8},{12,14},{14,12},{16,18},{18,... | collective-permute-start | bytes 688136 | tf_op jit(solution)/shard_map/ppermute | solution.py:24
  89.7 11.7 %collective-permute-start.18 = (bf16[32,3584]{1,0:T(8,128)(2,1)S(1)}, bf16[32,3584]{1,0:T(8,128)(2,1)S(1)}, u32[]{:S(2)}, u32[]{:S(2)}) collective-permute-start(bf16[32,3584]{1,0:T(8,128)(2,1)S(1)} %constant_dynamic-update-slice_fusion.refs_0_), channel_id=1, source_target_pairs={{0,1},{1,0},{2,3},{3,2},{4,5},{5,4},{6,7},{7,6},{8,9},{9,8},{10,11... | collective-permute-start | bytes 688136 | tf_op jit(solution)/shard_map/ppermute | solution.py:24
  92.0 11.1 %collective-permute-start.19 = (bf16[32,3584]{1,0:T(8,128)(2,1)S(1)}, bf16[32,3584]{1,0:T(8,128)(2,1)S(1)}, u32[]{:S(2)}, u32[]{:S(2)}) collective-permute-start(bf16[32,3584]{1,0:T(8,128)(2,1)S(1)} %collective-permute-done.15.refs_1_), channel_id=1, source_target_pairs={{0,1},{1,0},{2,3},{3,2},{4,5},{5,4},{6,7},{7,6},{8,9},{9,8},{10,11... | collective-permute-start | bytes 688136 | tf_op jit(solution)/shard_map/ppermute | solution.py:24
  92.6 10.6 %collective-permute-start.20 = (bf16[32,3584]{1,0:T(8,128)(2,1)S(1)}, bf16[32,3584]{1,0:T(8,128)(2,1)S(1)}, u32[]{:S(2)}, u32[]{:S(2)}) collective-permute-start(bf16[32,3584]{1,0:T(8,128)(2,1)S(1)} %collective-permute-done.16.refs_2_), channel_id=1, source_target_pairs={{0,1},{1,0},{2,3},{3,2},{4,5},{5,4},{6,7},{7,6},{8,9},{9,8},{10,11... | collective-permute-start | bytes 688136 | tf_op jit(solution)/shard_map/ppermute | solution.py:24
  100.6 6.3 %collective-permute-start.21 = (bf16[32,3584]{1,0:T(8,128)(2,1)S(1)}, bf16[32,3584]{1,0:T(8,128)(2,1)S(1)}, u32[]{:S(2)}, u32[]{:S(2)}) collective-permute-start(bf16[32,3584]{1,0:T(8,128)(2,1)S(1)} %collective-permute-done.17.refs_3_), channel_id=1, source_target_pairs={{0,1},{1,0},{2,3},{3,2},{4,5},{5,4},{6,7},{7,6},{8,9},{9,8},{10,11... | collective-permute-start | bytes 688136 | tf_op jit(solution)/shard_map/ppermute | solution.py:24
  100.6 5.6 %collective-permute-start.7 = (bf16[32,1792]{1,0:T(8,128)(2,1)S(1)}, bf16[32,1792]{1,0:T(8,128)(2,1)S(1)}, u32[]{:S(2)}, u32[]{:S(2)}) collective-permute-start(bf16[32,1792]{1,0:T(8,128)(2,1)S(1)} %slice.57), channel_id=1, source_target_pairs={{0,2},{2,0},{4,6},{6,4},{8,10},{10,8},{12,14},{14,12},{16,18},{18,... | collective-permute-start | bytes 344072 | tf_op jit(solution)/shard_map/ppermute | solution.py:24
  101.4 5.5 %collective-permute-start.8 = (bf16[32,1920]{1,0:T(8,128)(2,1)S(1)}, bf16[32,1920]{1,0:T(8,128)(2,1)S(1)}, u32[]{:S(2)}, u32[]{:S(2)}) collective-permute-start(bf16[32,1920]{1,0:T(8,128)(2,1)S(1)} %slice.58), channel_id=1, source_target_pairs={{0,4},{2,6},{4,0},{6,2},{8,12},{10,14},{12,8},{14,10},{16,20},{18,... | collective-permute-start | bytes 368648 | tf_op jit(solution)/shard_map/ppermute | solution.py:24
  103.1 13.5 %collective-permute-start.9 = (bf16[32,3712]{1,0:T(8,128)(2,1)S(1)}, bf16[32,3712]{1,0:T(8,128)(2,1)S(1)}, u32[]{:S(2)}, u32[]{:S(2)}) collective-permute-start(bf16[32,3712]{1,0:T(8,128)(2,1)S(1)} %pad_maximum_fusion.2.refs_0_), channel_id=1, source_target_pairs={{0,1},{1,0},{2,3},{3,2},{4,5},{5,4},{6,7},{7,6},{8,9},{9,8},{10,11... | collective-permute-start | bytes 712712 | tf_op jit(solution)/shard_map/ppermute | solution.py:24
  103.2 13.5 %collective-permute-start.10 = (bf16[32,3712]{1,0:T(8,128)(2,1)S(1)}, bf16[32,3712]{1,0:T(8,128)(2,1)S(1)}, u32[]{:S(2)}, u32[]{:S(2)}) collective-permute-start(bf16[32,3712]{1,0:T(8,128)(2,1)S(1)} %collective-permute-done.5.refs_1_), channel_id=1, source_target_pairs={{0,1},{1,0},{2,3},{3,2},{4,5},{5,4},{6,7},{7,6},{8,9},{9,8},{10,11... | collective-permute-start | bytes 712712 | tf_op jit(solution)/shard_map/ppermute | solution.py:24
  106.2 10.5 %collective-permute-start.11 = (bf16[32,3712]{1,0:T(8,128)(2,1)S(1)}, bf16[32,3712]{1,0:T(8,128)(2,1)S(1)}, u32[]{:S(2)}, u32[]{:S(2)}) collective-permute-start(bf16[32,3712]{1,0:T(8,128)(2,1)S(1)} %collective-permute-done.6.refs_2_), channel_id=1, source_target_pairs={{0,1},{1,0},{2,3},{3,2},{4,5},{5,4},{6,7},{7,6},{8,9},{9,8},{10,11... | collective-permute-start | bytes 712712 | tf_op jit(solution)/shard_map/ppermute | solution.py:24
  106.9 9.8 %collective-permute-start.12 = (bf16[32,1792]{1,0:T(8,128)(2,1)S(1)}, bf16[32,1792]{1,0:T(8,128)(2,1)S(1)}, u32[]{:S(2)}, u32[]{:S(2)}) collective-permute-start(bf16[32,1792]{1,0:T(8,128)(2,1)S(1)} %collective-permute-done.7.refs_3_), channel_id=1, source_target_pairs={{0,1},{1,0},{2,3},{3,2},{4,5},{5,4},{6,7},{7,6},{8,9},{9,8},{10,11... | collective-permute-start | bytes 344072 | tf_op jit(solution)/shard_map/ppermute | solution.py:24
  106.9 9.8 %collective-permute-start.13 = (bf16[32,1920]{1,0:T(8,128)(2,1)S(1)}, bf16[32,1920]{1,0:T(8,128)(2,1)S(1)}, u32[]{:S(2)}, u32[]{:S(2)}) collective-permute-start(bf16[32,1920]{1,0:T(8,128)(2,1)S(1)} %collective-permute-done.8.refs_4_), channel_id=1, source_target_pairs={{0,1},{1,0},{2,3},{3,2},{4,5},{5,4},{6,7},{7,6},{8,9},{9,8},{10,11... | collective-permute-start | bytes 368648 | tf_op jit(solution)/shard_map/ppermute | solution.py:24
  123.0 3.9 %collective-permute-start.22 = (bf16[128,7168]{1,0:T(8,128)(2,1)S(1)}, bf16[128,7168]{1,0:T(8,128)(2,1)S(1)}, u32[]{:S(2)}, u32[]{:S(2)}) collective-permute-start(bf16[128,7168]{1,0:T(8,128)(2,1)S(1)} %get-tuple-element.21), channel_id=1, source_target_pairs={{0,1},{1,0},{2,3},{3,2},{4,5},{5,4},{6,7},{7,6},{8,9},{9,8},{10,11... | collective-permute-start | bytes 5505032 | tf_op jit(solution)/shard_map/ppermute | solution.py:24
  127.2 7.7 %collective-permute-start.23 = (bf16[32,3584]{1,0:T(8,128)(2,1)S(1)}, bf16[32,3584]{1,0:T(8,128)(2,1)S(1)}, u32[]{:S(2)}, u32[]{:S(2)}) collective-permute-start(bf16[32,3584]{1,0:T(8,128)(2,1)S(1)} %get-tuple-element.31), channel_id=1, source_target_pairs={{0,4},{2,6},{4,0},{6,2},{8,12},{10,14},{12,8},{14,10},{16,20},{18,... | collective-permute-start | bytes 688136 | tf_op jit(solution)/shard_map/ppermute | solution.py:24
  129.0 7.4 %collective-permute-start.25 = (bf16[32,3584]{1,0:T(8,128)(2,1)S(1)}, bf16[32,3584]{1,0:T(8,128)(2,1)S(1)}, u32[]{:S(2)}, u32[]{:S(2)}) collective-permute-start(bf16[32,3584]{1,0:T(8,128)(2,1)S(1)} %get-tuple-element.32), channel_id=1, source_target_pairs={{0,2},{2,0},{4,6},{6,4},{8,10},{10,8},{12,14},{14,12},{16,18},{18,... | collective-permute-start | bytes 688136 | tf_op jit(solution)/shard_map/ppermute | solution.py:24
  135.0 11.8 %collective-permute-start.24 = (bf16[32,7168]{1,0:T(8,128)(2,1)S(1)}, bf16[32,7168]{1,0:T(8,128)(2,1)S(1)}, u32[]{:S(2)}, u32[]{:S(2)}) collective-permute-start(bf16[32,7168]{1,0:T(8,128)(2,1)S(1)} %pad_maximum_fusion), channel_id=1, source_target_pairs={{0,2},{2,0},{4,6},{6,4},{8,10},{10,8},{12,14},{14,12},{16,18},{18,... | collective-permute-start | bytes 1376264 | tf_op jit(solution)/shard_map/ppermute | solution.py:24
  136.5 11.5 %collective-permute-start.26 = (bf16[32,7168]{1,0:T(8,128)(2,1)S(1)}, bf16[32,7168]{1,0:T(8,128)(2,1)S(1)}, u32[]{:S(2)}, u32[]{:S(2)}) collective-permute-start(bf16[32,7168]{1,0:T(8,128)(2,1)S(1)} %pad_maximum_fusion.1), channel_id=1, source_target_pairs={{0,4},{2,6},{4,0},{6,2},{8,12},{10,14},{12,8},{14,10},{16,20},{18,... | collective-permute-start | bytes 1376264 | tf_op jit(solution)/shard_map/ppermute | solution.py:24
  148.3 9.6 %collective-permute-start.27 = (bf16[16,7168]{1,0:T(8,128)(2,1)S(1)}, bf16[16,7168]{1,0:T(8,128)(2,1)S(1)}, u32[]{:S(2)}, u32[]{:S(2)}) collective-permute-start(bf16[16,7168]{1,0:T(8,128)(2,1)S(1)} %split.78), channel_id=1, source_target_pairs={{0,16},{2,18},{4,20},{6,22},{8,24},{10,26},{12,28},{14,30},{16,0},... | collective-permute-start | bytes 688136 | tf_op jit(solution)/shard_map/ppermute | solution.py:24
  158.0 5.1 %collective-permute-start.28 = (bf16[8,7168]{1,0:T(8,128)(2,1)S(1)}, bf16[8,7168]{1,0:T(8,128)(2,1)S(1)}, u32[]{:S(2)}, u32[]{:S(2)}) collective-permute-start(bf16[8,7168]{1,0:T(8,128)(2,1)S(1)} %split.79), channel_id=1, source_target_pairs={{0,8},{2,10},{4,12},{6,14},{8,0},{10,2},{12,4},{14,6},{16,24},{18,... | collective-permute-start | bytes 344072 | tf_op jit(solution)/shard_map/ppermute | solution.py:24
  (12 other events, 144.5 us)

commit v4 on v3

--- a/solution.py
+++ b/solution.py
@@ -30,14 +30,15 @@
 
 
 CHUNKS = 4
+AHEAD = 3
 
 
 def vmem_spec():
     return pl.BlockSpec(memory_space=pltpu.VMEM)
 
 
-def any_spec():
-    return pl.BlockSpec(memory_space=pl.ANY)
+def hbm_spec():
+    return pl.BlockSpec(memory_space=pltpu.HBM)
 
 
 def span(n, size):
@@ -60,7 +61,7 @@
 
     for g in range(groups):
         copy_uv(g).start()
-    for n in range(chunks):
+    for n in range(AHEAD):
         copy_o(n).start()
     for g in range(groups):
         copy_uv(g).wait()
@@ -70,6 +71,8 @@
             ).astype(jnp.bfloat16)
     for n in range(chunks):
         copy_o(n).wait()
+        if n + AHEAD < chunks:
+            copy_o(n + AHEAD).start()
         product = jnp.dot(
             values[:, n * depth : (n + 1) * depth], o_buf[n], preferred_element_type=jnp.float32
         )
@@ -90,7 +93,7 @@
             jax.ShapeDtypeStruct((rows, width), jnp.float32),
             jax.ShapeDtypeStruct((rows, depth), jnp.bfloat16),
         ),
-        in_specs=[vmem_spec(), any_spec(), any_spec()],
+        in_specs=[vmem_spec(), hbm_spec(), hbm_spec()],
         out_specs=(vmem_spec(), vmem_spec()),
         scratch_shapes=[
             pltpu.VMEM(w_uv.shape, jnp.bfloat16),
@@ -115,10 +118,12 @@
         rows = pl.ds(n * depth, depth)
         return pltpu.make_async_copy(w_o.at[rows, pl.ds(start, width)], o_buf.at[n], o_sems.at[n])
 
-    for n in range(chunks):
+    for n in range(AHEAD):
         copy_o(n).start()
     for n in range(chunks):
         copy_o(n).wait()
+        if n + AHEAD < chunks:
+            copy_o(n + AHEAD).start()
         product = jnp.dot(
             values[:, n * depth : (n + 1) * depth], o_buf[n], preferred_element_type=jnp.float32
         )
@@ -134,7 +139,7 @@
     return pl.pallas_call(
         functools.partial(columns_kernel, start),
         out_shape=jax.ShapeDtypeStruct((rows, width), jnp.float32),
-        in_specs=[vmem_spec(), any_spec()],
+        in_specs=[vmem_spec(), hbm_spec()],
         out_specs=vmem_spec(),
         scratch_shapes=[
             pltpu.VMEM((chunks, depth // chunks, width), jnp.bfloat16),
@@ -149,7 +154,8 @@
 
 
 def first_kernel(set_count, *refs):
-    flat, refs = refs[: 4 * set_count], refs[4 * set_count :]
+    flat, refs = refs[: 5 * set_count], refs[5 * set_count :]
+    sets = [flat[5 * n : 5 * n + 5] for n in range(set_count)]
     w_gate, w_up, gate_acc, up_acc, gate_buf, up_buf, sems = refs
     chunks, size, _ = gate_buf.shape
 
@@ -162,28 +168,34 @@
     for n in range(chunks):
         for copy in copies_in(n):
             copy.start()
-    gate_acc[...] = jnp.zeros_like(gate_acc)
-    up_acc[...] = jnp.zeros_like(up_acc)
-
-    @pl.loop(0, chunks)
-    def _(n):
+    for n in range(chunks):
+        parts = []
+        for own, near_x, near_y, low, high in sets:
+            parts += [ref[:, n * size : (n + 1) * size] for ref in (own, near_x, near_y)]
+            parts.append((low, high)[n][...])
+        rows = jnp.concatenate(parts, axis=0)
         for copy in copies_in(n):
             copy.wait()
-        rows = jnp.concatenate([ref[:, span(n, size)] for ref in flat], axis=0)
-        gate_acc[...] += jnp.dot(rows, gate_buf[n], preferred_element_type=jnp.float32)
-        up_acc[...] += jnp.dot(rows, up_buf[n], preferred_element_type=jnp.float32)
+        gate_part = jnp.dot(rows, gate_buf[n], preferred_element_type=jnp.float32)
+        up_part = jnp.dot(rows, up_buf[n], preferred_element_type=jnp.float32)
+        if n == 0:
+            gate_acc[...] = gate_part
+            up_acc[...] = up_part
+        else:
+            gate_acc[...] += gate_part
+            up_acc[...] += up_part
 
 
 def experts_first(sets, w_gate, w_up):
     width, hidden_units = w_gate.shape[1:]
     size = width // CHUNKS
     flat = [piece for pieces in sets for piece in pieces]
-    rows = sum(piece.shape[0] for piece in flat)
+    rows = sum(piece.shape[0] for pieces in sets for piece in pieces[:4])
     sums = jax.ShapeDtypeStruct((rows, hidden_units), jnp.float32)
     return pl.pallas_call(
         functools.partial(first_kernel, len(sets)),
         out_shape=(sums, sums),
-        in_specs=[vmem_spec()] * len(flat) + [any_spec()] * 2,
+        in_specs=[vmem_spec()] * len(flat) + [hbm_spec()] * 2,
         out_specs=(vmem_spec(), vmem_spec()),
         scratch_shapes=[
             pltpu.VMEM((CHUNKS // 2, size, hidden_units), jnp.bfloat16),
@@ -267,7 +279,7 @@
             jax.ShapeDtypeStruct((rows // 2, width), jnp.bfloat16),
             jax.ShapeDtypeStruct((rows // 2, hidden_units), jnp.bfloat16),
         ),
-        in_specs=[vmem_spec()] * (len(flat) + 3) + [any_spec()] * 3,
+        in_specs=[vmem_spec()] * (len(flat) + 3) + [hbm_spec()] * 3,
         out_specs=(vmem_spec(), vmem_spec()),
         scratch_shapes=[
             pltpu.VMEM((CHUNKS // 2, size, hidden_units), jnp.bfloat16),
@@ -314,7 +326,7 @@
     return pl.pallas_call(
         down_kernel,
         out_shape=jax.ShapeDtypeStruct((rows, width), jnp.bfloat16),
-        in_specs=[vmem_spec(), any_spec()],
+        in_specs=[vmem_spec(), hbm_spec()],
         out_specs=vmem_spec(),
         scratch_shapes=[
             pltpu.VMEM((CHUNKS, hidden_units, size), jnp.bfloat16),
@@ -368,17 +380,16 @@
     return lax.all_gather(part, "ep", axis=1, tiled=True)
 
 
-def line_of(rows):
-    for bit in bits_of("dp")[2:]:
-        rows = jnp.concatenate([rows, flip(rows, "dp", bit)], axis=0)
-    return rows
-
-
 def all_sets(pieces):
     sets = [pieces]
     for bit in bits_of("ep"):
         sets = sets + [tuple(flip(piece, "ep", bit) for piece in one) for one in sets]
     return sets
+
+
+def dp_bits():
+    inner_x, inner_y, *outer = bits_of("dp")
+    return inner_x, inner_y, outer[::-1]
 
 
 def plus(*terms):
@@ -396,7 +407,7 @@
         if bit != bits[-1]:
             both = narrow(plus(near, came))
             near, far = jnp.split(both, 2, axis=0)
-    inner_x, inner_y, *outer = bits_of("dp")
+    inner_x, inner_y, outer = dp_bits()
     width = near.shape[1]
     half = width // 2
     near = jnp.split(near, 4, axis=0)
@@ -451,6 +462,9 @@
     w_up,
     w_down,
 ):
+    w_uv, w_o, w_gate, w_up, w_down = (
+        pltpu.with_memory_space_constraint(w, pltpu.HBM) for w in (w_uv, w_o, w_gate, w_up, w_down)
+    )
     replica_rows = latent_cache.shape[0]
     replicas = destination.shape[0] // replica_rows
     own_replica = lax.axis_index("dp")
@@ -487,14 +501,16 @@
     hidden_a = tokens[:, :half] + head_sums(part)
     rows_a = narrow(hidden_a * norm_gain[None, :half])
     values, rows_a = lax.optimization_barrier((values, rows_a))
-    inner_x, inner_y, *outer = bits_of("dp")
-    parts_b = [more_columns(values, w_o, half, size)]
-    came = flip(rows_a, "dp", outer[0])
+    inner_x, inner_y, outer = dp_bits()
+    early = half * 2 // 5 // 128 * 128
+    parts_b = [more_columns(values, w_o, half, early)]
+    came, parts_b = lax.optimization_barrier((flip(rows_a, "dp", outer[0]), parts_b))
     held_a = jnp.concatenate([rows_a, came], axis=0)
     values, held_a = lax.optimization_barrier((values, held_a))
-    parts_b.append(more_columns(values, w_o, half + size, size))
+    parts_b.append(more_columns(values, w_o, half + early, half - early))
     for bit in outer[1:]:
         held_a = jnp.concatenate([held_a, flip(held_a, "dp", bit)], axis=0)
+    parts_b, held_a = lax.optimization_barrier((parts_b, held_a))
     x_a = flip(held_a, "dp", inner_x)
     y_a = flip(held_a, "dp", inner_y)
 
@@ -509,13 +525,19 @@
     terms = three_terms(gate_sum) + three_terms(factor)
     terms.append(jnp.zeros((tokens.shape[0], GATE_COLS - 3 * replicas - 3), jnp.bfloat16))
     rows_b = jnp.concatenate([narrow(hidden_b * norm_gain[None, half:])] + terms, axis=1)
-    held_b = line_of(rows_b)
-    d_a = flip(y_a, "dp", inner_x)
-    sums = experts_first(all_sets((held_a, x_a, y_a, d_a)), w_gate, w_up)
+    held_b = jnp.concatenate([rows_b, flip(rows_b, "dp", outer[0])], axis=0)
+    held_b, x_a, y_a = lax.optimization_barrier((held_b, x_a, y_a))
+    low_a = flip(y_a[:, :size], "dp", inner_x)
+    high_a = flip(x_a[:, size:], "dp", inner_y)
+    for bit in outer[1:]:
+        held_b = jnp.concatenate([held_b, flip(held_b, "dp", bit)], axis=0)
+    held_b, low_a, high_a = lax.optimization_barrier((held_b, low_a, high_a))
     x_b = flip(held_b, "dp", inner_x)
     y_b = flip(held_b, "dp", inner_y)
+    sums = experts_first(all_sets((held_a, x_a, y_a, low_a, high_a)), w_gate, w_up)
     low_b = flip(y_b[:, :size], "dp", inner_x)
     high_b = flip(x_b[:, size:], "dp", inner_y)
+    low_b, high_b, sums = lax.optimization_barrier((low_b, high_b, sums))
     columns = jnp.arange(GATE_COLS, dtype=jnp.int32)
     gate_mask = (columns < 3 * replicas) & (columns % replicas == own_replica)
     factor_mask = (columns >= 3 * replicas) & (columns < 3 * replicas + 3)

time: 165 us -> 149 us (0.903)
  waiting for transfers between devices: 73.3 us -> 58.8 us
  local copies, waits for them, and re-layouts: 14.2 us -> 4.81 us
  Pallas kernels: 33.9 us -> 38.1 us
  starting transfers between devices: 30.1 us -> 33.3 us
    ppermute x29 -> x31, waiting for transfers between devices: 60.2 us -> 45.7 us  [flip(): return lax.ppermute(x, axis, pairs)]
    unnamed x28 -> x18, local copies, waits for them, and re-layouts: 10.2 us -> 0.76 us
    ppermute x29 -> x31, starting transfers between devices: 18.1 us -> 21.4 us  [flip(): return lax.ppermute(x, axis, pairs)]
  transfers between devices with their start and end apart: 31 -> 33, of which waited for: 19 -> 19; matrix products, arithmetic and copies ran while one was open for 2% -> 2% of each run, Pallas kernels for 7% -> 14%
where the time goes in v4:
time: 149 us; the launch traced here: 148 us
  waiting for transfers between devices  58.8 us (39%)
  Pallas kernels  38.1 us (26%)
  starting transfers between devices  33.3 us (22%)
  matrix products  5.24 us (4%)
  local copies, waits for them, and re-layouts  4.81 us (3%)
  other arithmetic  4.68 us (3%)
  blocking collectives  2 us (1%)
    ppermute x31, waiting for transfers between devices, flip(): return lax.ppermute(x, axis, pairs)  45.7 us
    ppermute x31, starting transfers between devices, flip(): return lax.ppermute(x, axis, pairs)  21.4 us
    pallas_call x2, Pallas kernels, more_columns(): pl.pallas_call(functools.partial(columns_kernel, start), out_shape=jax.Sh...  12.1 us
    pallas_call x1, Pallas kernels, values_and_first(): pl.pallas_call(values_kernel, out_shape=(jax.ShapeDtypeStruct((rows, widt...  11.7 us
    all_to_all x1, starting transfers between devices, migrate(): met = lax.all_to_all(outbox, 'dp', split_axis=0, concat_axis=0)  8.44 us
    all_to_all x1, waiting for transfers between devices, migrate(): met = lax.all_to_all(outbox, 'dp', split_axis=0, concat_axis=0)  6.89 us
    pallas_call x1, Pallas kernels, experts_far(): pl.pallas_call(functools.partial(far_kernel, len(sets)), out_shape=(jax.S...  6.36 us
    all_to_all x1, waiting for transfers between devices, migrate(): lax.all_to_all(sorted_rows.reshape(replicas, MOVE_MAX, share), 'dp', spli...  6.23 us
  transfers between devices with their start and end apart: 33, of which 19 were waited for; matrix products, arithmetic and copies ran while one was open for 2% of the time, Pallas kernels for 14%

profile of v4, /device:TPU:0, one launch (start us, length us, event | category | flops | bytes accessed | tf_op | source)
XLA Modules:
  0.0 148.1 jit_solution(3658368628399488151)
XLA Ops:
  2.4 2.0 %convolution_convert_fusion.1 = bf16[4,18432]{1,0:T(4,128)(2,1)} fusion(pred[4,16]{1,0:T(4,128)(4,1)S(1)} %get-tuple-element.57, bf16[16,36864]{1,0:T(8,128)(2,1)} %param.15, s32[]{:T(128)S(6)} %select_n.83), kind=kOutput, calls=%fused_computation.3 | convolution fusion | flops 2433024 | bytes 737348 | tf_op jit(solution)/shard_map/dot_general | solution.py:370
  4.4 8.4 %all-to-all-start = ((bf16[16,4,1152]{2,1,0:T(4,128)(2,1)}), bf16[16,4,1152]{2,1,0:T(4,128)(2,1)S(1)}, u32[]{:S(2)}, u32[]{:S(2)}) async-start(bf16[16,4,1152]{2,1,0:T(4,128)(2,1)} %bitcast.1), calls=%async_computation | async-start | bytes 294912 | tf_op jit(solution)/shard_map/all_to_all | solution.py:372
  13.8 6.9 %all-to-all-done = bf16[16,4,1152]{2,1,0:T(4,128)(2,1)S(1)} async-done(((bf16[16,4,1152]{2,1,0:T(4,128)(2,1)}), bf16[16,4,1152]{2,1,0:T(4,128)(2,1)S(1)}, u32[]{:S(2)}, u32[]{:S(2)}) %all-to-all-start) | async-done | bytes 147488 | tf_op jit(solution)/shard_map/all_to_all | solution.py:372
  21.6 3.5 %all-to-all-start.1 = ((bf16[16,4,1152]{2,1,0:T(4,128)(2,1)}), bf16[16,4,1152]{2,1,0:T(4,128)(2,1)S(1)}, u32[]{:S(2)}, u32[]{:S(2)}) async-start(bf16[16,4,1152]{2,1,0:T(4,128)(2,1)} %reshape.211), calls=%async_computation.1 | async-start | bytes 294912 | tf_op jit(solution)/shard_map/all_to_all | solution.py:376
  26.7 6.2 %all-to-all-done.1 = bf16[16,4,1152]{2,1,0:T(4,128)(2,1)S(1)} async-done(((bf16[16,4,1152]{2,1,0:T(4,128)(2,1)}), bf16[16,4,1152]{2,1,0:T(4,128)(2,1)S(1)}, u32[]{:S(2)}, u32[]{:S(2)}) %all-to-all-start.1) | async-done | bytes 147488 | tf_op jit(solution)/shard_map/all_to_all | solution.py:376
  32.9 2.0 %all_gather.3 = bf16[4,36864]{1,0:T(4,128)(2,1)S(1)} all-gather(bf16[4,18432]{1,0:T(4,128)(2,1)S(1)} %bitcast.23), channel_id=1, replica_groups=mesh['dp'=16,'ep'=2] {'ep'}, dimensions={1}, use_global_device_ids=true | all-gather | bytes 442368 | tf_op jit(solution)/shard_map/all_gather | solution.py:380
  35.6 1.8 %reshape.213 = bf16[16,64,576]{2,1,0:T(8,128)(2,1)S(1)} reshape(bf16[16,36864]{1,0:T(8,128)(2,1)S(1)} %fusion.1) | data formatting | bytes 2359296 | tf_op jit(solution)/shard_map/reshape | solution.py:482
  39.5 11.7 %values_and_first.1 = (f32[16,3584]{1,0:T(8,128)S(1)}, bf16[16,4096]{1,0:T(8,128)(2,1)S(1)}) custom-call(bf16[32,16,512]{2,1,0:T(8,128)(2,1)S(1)} %bitcast.22, bf16[32,512,128]{2,1,0:T(8,128)(2,1)} %w_uv.1, bf16[4096,7168]{1,0:T(8,128)(2,1)} %w_o.5), custom_call_target="tpu_custom_call" | custom-call | flops 536870912 | bytes 33554432 | tf_op jit(solution)/shard_map/values_and_first/pallas_call | solution.py:90
  51.5 1.2 collective-permute-done
  53.9 5.3 %more_columns.2 = f32[16,1408]{1,0:T(8,128)S(1)} custom-call(bf16[16,4096]{1,0:T(8,128)(2,1)S(1)} %get-tuple-element.33.values, bf16[4096,7168]{1,0:T(8,128)(2,1)} %w_o.5), custom_call_target="tpu_custom_call" | custom-call | flops 184549376 | bytes 11534336 | tf_op jit(solution)/shard_map/more_columns/pallas_call | solution.py:139
  60.3 6.9 %more_columns.3 = f32[16,2176]{1,0:T(8,128)S(1)} custom-call(bf16[16,4096]{1,0:T(8,128)(2,1)S(1)} %get-tuple-element.33.values, bf16[4096,7168]{1,0:T(8,128)(2,1)} %w_o.5), custom_call_target="tpu_custom_call" | custom-call | flops 285212672 | bytes 17825792 | tf_op jit(solution)/shard_map/more_columns/pallas_call | solution.py:139
  67.3 1.3 collective-permute-done.3
  69.0 1.8 %collective-permute-start.4 = (bf16[8,3712]{1,0:T(8,128)(2,1)S(1)}, bf16[8,3712]{1,0:T(8,128)(2,1)S(1)}, u32[]{:S(2)}, u32[]{:S(2)}) collective-permute-start(bf16[8,3712]{1,0:T(8,128)(2,1)S(1)} %concatenate.33), channel_id=1, source_target_pairs={{0,16},{2,18},{4,20},{6,22},{8,24},{10,26},{12,28},{14,30},{16,0},... | collective-permute-start | bytes 178184 | tf_op jit(solution)/shard_map/ppermute | solution.py:24
  72.2 3.1 %collective-permute-done.4 = bf16[8,3712]{1,0:T(8,128)(2,1)S(1)} collective-permute-done((bf16[8,3712]{1,0:T(8,128)(2,1)S(1)}, bf16[8,3712]{1,0:T(8,128)(2,1)S(1)}, u32[]{:S(2)}, u32[]{:S(2)}) %collective-permute-start.4) | collective-permute-done | bytes 59424 | tf_op jit(solution)/shard_map/ppermute | solution.py:24
  75.2 3.0 %collective-permute-done.5.refs_1_ = bf16[32,3584]{1,0:T(8,128)(2,1)S(1)} collective-permute-done((bf16[32,3584]{1,0:T(8,128)(2,1)S(1)}, bf16[32,3584]{1,0:T(8,128)(2,1)S(1)}, u32[]{:S(2)}, u32[]{:S(2)}) %collective-permute-start.5) | collective-permute-done | bytes 229408 | tf_op jit(solution)/shard_map/ppermute | solution.py:24
  78.5 1.9 %collective-permute-start.7 = (bf16[16,3712]{1,0:T(8,128)(2,1)S(1)}, bf16[16,3712]{1,0:T(8,128)(2,1)S(1)}, u32[]{:S(2)}, u32[]{:S(2)}) collective-permute-start(bf16[16,3712]{1,0:T(8,128)(2,1)S(1)} %pad_maximum_fusion.4), channel_id=1, source_target_pairs={{0,8},{2,10},{4,12},{6,14},{8,0},{10,2},{12,4},{14,6},{16,24},{18,... | collective-permute-start | bytes 356360 | tf_op jit(solution)/shard_map/ppermute | solution.py:24
  82.1 1.2 collective-permute-done.7
  83.4 1.9 %collective-permute-done.8.refs_3_ = bf16[32,1792]{1,0:T(8,128)(2,1)S(1)} collective-permute-done((bf16[32,1792]{1,0:T(8,128)(2,1)S(1)}, bf16[32,1792]{1,0:T(8,128)(2,1)S(1)}, u32[]{:S(2)}, u32[]{:S(2)}) %collective-permute-start.8) | collective-permute-done | bytes 114720 | tf_op jit(solution)/shard_map/ppermute | solution.py:24
  86.2 1.2 collective-permute-start.10
  88.1 4.2 %collective-permute-done.10.refs_1_ = bf16[32,3712]{1,0:T(8,128)(2,1)S(1)} collective-permute-done((bf16[32,3712]{1,0:T(8,128)(2,1)S(1)}, bf16[32,3712]{1,0:T(8,128)(2,1)S(1)}, u32[]{:S(2)}, u32[]{:S(2)}) %collective-permute-start.10) | collective-permute-done | bytes 237600 | tf_op jit(solution)/shard_map/ppermute | solution.py:24
  92.3 1.1 collective-permute-done.11.refs_2_
  94.4 1.3 collective-permute-start.12
  96.2 4.3 %experts_first.1 = (f32[256,512]{1,0:T(8,128)S(1)}, f32[256,512]{1,0:T(8,128)S(1)}) custom-call(bf16[32,3584]{1,0:T(8,128)(2,1)S(1)} %pad_maximum_fusion.3.refs_0_, bf16[32,3584]{1,0:T(8,128)(2,1)S(1)} %collective-permute-done.5.refs_1_, bf16[32,3584]{1,0:T(8,128)(2,1)S(1)} %collective-permute-done.6.refs_2_, ...), custom_call_target="tpu_custom_call" | custom-call | flops 1879048192 | bytes 9175040 | tf_op jit(solution)/shard_map/experts_first/pallas_call | solution.py:195
  102.1 6.4 %experts_far.1 = (bf16[128,7168]{1,0:T(8,128)(2,1)S(1)}, bf16[128,512]{1,0:T(8,128)(2,1)S(1)}) custom-call(bf16[32,3712]{1,0:T(8,128)(2,1)S(1)} %pad_maximum_fusion.2.refs_0_, bf16[32,3712]{1,0:T(8,128)(2,1)S(1)} %collective-permute-done.10.refs_1_, bf16[32,3712]{1,0:T(8,128)(2,1)S(1)} %collective-permute-done.11.refs_2_, ...), custom_call_target="tpu_custom_call" | custom-call | flops 2818572288 | bytes 20185088 | tf_op jit(solution)/shard_map/experts_far/pallas_call | solution.py:276
  108.9 3.6 %experts_near.1 = bf16[128,7168]{1,0:T(8,128)(2,1)S(1)} custom-call(bf16[128,512]{1,0:T(8,128)(2,1)S(1)} %get-tuple-element.50.kept, bf16[1,512,7168]{2,1,0:T(8,128)(2,1)} %w_down.1), custom_call_target="tpu_custom_call" | custom-call | flops 939524096 | bytes 9175040 | tf_op jit(solution)/shard_map/experts_near/pallas_call | solution.py:326
  112.9 1.3 collective-permute-start.25
  114.3 1.2 collective-permute-start.27
  115.5 5.1 %collective-permute-done.25 = bf16[32,3584]{1,0:T(8,128)(2,1)S(1)} collective-permute-done((bf16[32,3584]{1,0:T(8,128)(2,1)S(1)}, bf16[32,3584]{1,0:T(8,128)(2,1)S(1)}, u32[]{:S(2)}, u32[]{:S(2)}) %collective-permute-start.25) | collective-permute-done | bytes 229408 | tf_op jit(solution)/shard_map/ppermute | solution.py:24
  121.8 1.6 %collective-permute-start.28 = (bf16[32,7168]{1,0:T(8,128)(2,1)S(1)}, bf16[32,7168]{1,0:T(8,128)(2,1)S(1)}, u32[]{:S(2)}, u32[]{:S(2)}) collective-permute-start(bf16[32,7168]{1,0:T(8,128)(2,1)S(1)} %pad_maximum_fusion.1), channel_id=1, source_target_pairs={{0,4},{2,6},{4,0},{6,2},{8,12},{10,14},{12,8},{14,10},{16,20},{18,... | collective-permute-start | bytes 1376264 | tf_op jit(solution)/shard_map/ppermute | solution.py:24
  123.4 9.2 %collective-permute-done.26 = bf16[32,7168]{1,0:T(8,128)(2,1)S(1)} collective-permute-done((bf16[32,7168]{1,0:T(8,128)(2,1)S(1)}, bf16[32,7168]{1,0:T(8,128)(2,1)S(1)}, u32[]{:S(2)}, u32[]{:S(2)}) %collective-permute-start.26) | collective-permute-done | bytes 458784 | tf_op jit(solution)/shard_map/ppermute | solution.py:24
  134.4 5.2 %collective-permute-done.29 = bf16[16,7168]{1,0:T(8,128)(2,1)S(1)} collective-permute-done((bf16[16,7168]{1,0:T(8,128)(2,1)S(1)}, bf16[16,7168]{1,0:T(8,128)(2,1)S(1)}, u32[]{:S(2)}, u32[]{:S(2)}) %collective-permute-start.29) | collective-permute-done | bytes 229408 | tf_op jit(solution)/shard_map/ppermute | solution.py:24
  140.8 6.0 %collective-permute-done.30 = bf16[8,7168]{1,0:T(8,128)(2,1)S(1)} collective-permute-done((bf16[8,7168]{1,0:T(8,128)(2,1)S(1)}, bf16[8,7168]{1,0:T(8,128)(2,1)S(1)}, u32[]{:S(2)}, u32[]{:S(2)}) %collective-permute-start.30) | collective-permute-done | bytes 114720 | tf_op jit(solution)/shard_map/ppermute | solution.py:24
  (118 shorter events, 25.3 us)
Async XLA Ops:
  4.4 16.3 %all-to-all-start = ((bf16[16,4,1152]{2,1,0:T(4,128)(2,1)}), bf16[16,4,1152]{2,1,0:T(4,128)(2,1)S(1)}, u32[]{:S(2)}, u32[]{:S(2)}) async-start(bf16[16,4,1152]{2,1,0:T(4,128)(2,1)} %bitcast.1), calls=%async_computation | async-start | bytes 294912 | tf_op jit(solution)/shard_map/all_to_all | solution.py:372
  21.6 11.4 %all-to-all-start.1 = ((bf16[16,4,1152]{2,1,0:T(4,128)(2,1)}), bf16[16,4,1152]{2,1,0:T(4,128)(2,1)S(1)}, u32[]{:S(2)}, u32[]{:S(2)}) async-start(bf16[16,4,1152]{2,1,0:T(4,128)(2,1)} %reshape.211), calls=%async_computation.1 | async-start | bytes 294912 | tf_op jit(solution)/shard_map/all_to_all | solution.py:376
  51.3 1.4 collective-permute-start
  52.9 6.3 %collective-permute-start.1 = (bf16[8,3584]{1,0:T(8,128)(2,1)S(1)}, bf16[8,3584]{1,0:T(8,128)(2,1)S(1)}, u32[]{:S(2)}, u32[]{:S(2)}) collective-permute-start(bf16[8,3584]{1,0:T(8,128)(2,1)S(1)} %multiply_convert_fusion.1), channel_id=1, source_target_pairs={{0,16},{2,18},{4,20},{6,22},{8,24},{10,26},{12,28},{14,30},{16,0},... | collective-permute-start | bytes 172040 | tf_op jit(solution)/shard_map/ppermute | solution.py:24
  59.2 7.9 %collective-permute-start.2 = (bf16[16,3584]{1,0:T(8,128)(2,1)S(1)}, bf16[16,3584]{1,0:T(8,128)(2,1)S(1)}, u32[]{:S(2)}, u32[]{:S(2)}) collective-permute-start(bf16[16,3584]{1,0:T(8,128)(2,1)S(1)} %pad_maximum_fusion.5), channel_id=1, source_target_pairs={{0,8},{2,10},{4,12},{6,14},{8,0},{10,2},{12,4},{14,6},{16,24},{18,... | collective-permute-start | bytes 344072 | tf_op jit(solution)/shard_map/ppermute | solution.py:24
  69.0 6.2 %collective-permute-start.4 = (bf16[8,3712]{1,0:T(8,128)(2,1)S(1)}, bf16[8,3712]{1,0:T(8,128)(2,1)S(1)}, u32[]{:S(2)}, u32[]{:S(2)}) collective-permute-start(bf16[8,3712]{1,0:T(8,128)(2,1)S(1)} %concatenate.33), channel_id=1, source_target_pairs={{0,16},{2,18},{4,20},{6,22},{8,24},{10,26},{12,28},{14,30},{16,0},... | collective-permute-start | bytes 178184 | tf_op jit(solution)/shard_map/ppermute | solution.py:24
  70.9 7.4 %collective-permute-start.5 = (bf16[32,3584]{1,0:T(8,128)(2,1)S(1)}, bf16[32,3584]{1,0:T(8,128)(2,1)S(1)}, u32[]{:S(2)}, u32[]{:S(2)}) collective-permute-start(bf16[32,3584]{1,0:T(8,128)(2,1)S(1)} %pad_maximum_fusion.3.refs_0_), channel_id=1, source_target_pairs={{0,2},{2,0},{4,6},{6,4},{8,10},{10,8},{12,14},{14,12},{16,18},{18,... | collective-permute-start | bytes 688136 | tf_op jit(solution)/shard_map/ppermute | solution.py:24
  71.4 7.1 %collective-permute-start.6 = (bf16[32,3584]{1,0:T(8,128)(2,1)S(1)}, bf16[32,3584]{1,0:T(8,128)(2,1)S(1)}, u32[]{:S(2)}, u32[]{:S(2)}) collective-permute-start(bf16[32,3584]{1,0:T(8,128)(2,1)S(1)} %pad_maximum_fusion.3.refs_0_), channel_id=1, source_target_pairs={{0,4},{2,6},{4,0},{6,2},{8,12},{10,14},{12,8},{14,10},{16,20},{18,... | collective-permute-start | bytes 688136 | tf_op jit(solution)/shard_map/ppermute | solution.py:24
  78.5 4.8 %collective-permute-start.7 = (bf16[16,3712]{1,0:T(8,128)(2,1)S(1)}, bf16[16,3712]{1,0:T(8,128)(2,1)S(1)}, u32[]{:S(2)}, u32[]{:S(2)}) collective-permute-start(bf16[16,3712]{1,0:T(8,128)(2,1)S(1)} %pad_maximum_fusion.4), channel_id=1, source_target_pairs={{0,8},{2,10},{4,12},{6,14},{8,0},{10,2},{12,4},{14,6},{16,24},{18,... | collective-permute-start | bytes 356360 | tf_op jit(solution)/shard_map/ppermute | solution.py:24
  80.4 4.9 %collective-permute-start.8 = (bf16[32,1792]{1,0:T(8,128)(2,1)S(1)}, bf16[32,1792]{1,0:T(8,128)(2,1)S(1)}, u32[]{:S(2)}, u32[]{:S(2)}) collective-permute-start(bf16[32,1792]{1,0:T(8,128)(2,1)S(1)} %slice.52), channel_id=1, source_target_pairs={{0,2},{2,0},{4,6},{6,4},{8,10},{10,8},{12,14},{14,12},{16,18},{18,... | collective-permute-start | bytes 344072 | tf_op jit(solution)/shard_map/ppermute | solution.py:24
  81.3 4.9 %collective-permute-start.9 = (bf16[32,1792]{1,0:T(8,128)(2,1)S(1)}, bf16[32,1792]{1,0:T(8,128)(2,1)S(1)}, u32[]{:S(2)}, u32[]{:S(2)}) collective-permute-start(bf16[32,1792]{1,0:T(8,128)(2,1)S(1)} %slice.53), channel_id=1, source_target_pairs={{0,4},{2,6},{4,0},{6,2},{8,12},{10,14},{12,8},{14,10},{16,20},{18,... | collective-permute-start | bytes 344072 | tf_op jit(solution)/shard_map/ppermute | solution.py:24
  86.2 6.1 %collective-permute-start.10 = (bf16[32,3712]{1,0:T(8,128)(2,1)S(1)}, bf16[32,3712]{1,0:T(8,128)(2,1)S(1)}, u32[]{:S(2)}, u32[]{:S(2)}) collective-permute-start(bf16[32,3712]{1,0:T(8,128)(2,1)S(1)} %pad_maximum_fusion.2.refs_0_), channel_id=1, source_target_pairs={{0,2},{2,0},{4,6},{6,4},{8,10},{10,8},{12,14},{14,12},{16,18},{18,... | collective-permute-start | bytes 712712 | tf_op jit(solution)/shard_map/ppermute | solution.py:24
  87.3 6.1 %collective-permute-start.11 = (bf16[32,3712]{1,0:T(8,128)(2,1)S(1)}, bf16[32,3712]{1,0:T(8,128)(2,1)S(1)}, u32[]{:S(2)}, u32[]{:S(2)}) collective-permute-start(bf16[32,3712]{1,0:T(8,128)(2,1)S(1)} %pad_maximum_fusion.2.refs_0_), channel_id=1, source_target_pairs={{0,4},{2,6},{4,0},{6,2},{8,12},{10,14},{12,8},{14,10},{16,20},{18,... | collective-permute-start | bytes 712712 | tf_op jit(solution)/shard_map/ppermute | solution.py:24
  87.6 5.9 %collective-permute-start.14 = (bf16[32,3584]{1,0:T(8,128)(2,1)S(1)}, bf16[32,3584]{1,0:T(8,128)(2,1)S(1)}, u32[]{:S(2)}, u32[]{:S(2)}) collective-permute-start(bf16[32,3584]{1,0:T(8,128)(2,1)S(1)} %pad_maximum_fusion.3.refs_0_), channel_id=1, source_target_pairs={{0,1},{1,0},{2,3},{3,2},{4,5},{5,4},{6,7},{7,6},{8,9},{9,8},{10,11... | collective-permute-start | bytes 688136 | tf_op jit(solution)/shard_map/ppermute | solution.py:24
  87.6 6.4 %collective-permute-start.15 = (bf16[32,3584]{1,0:T(8,128)(2,1)S(1)}, bf16[32,3584]{1,0:T(8,128)(2,1)S(1)}, u32[]{:S(2)}, u32[]{:S(2)}) collective-permute-start(bf16[32,3584]{1,0:T(8,128)(2,1)S(1)} %collective-permute-done.5.refs_1_), channel_id=1, source_target_pairs={{0,1},{1,0},{2,3},{3,2},{4,5},{5,4},{6,7},{7,6},{8,9},{9,8},{10,11... | collective-permute-start | bytes 688136 | tf_op jit(solution)/shard_map/ppermute | solution.py:24
  88.1 6.2 %collective-permute-start.16 = (bf16[32,3584]{1,0:T(8,128)(2,1)S(1)}, bf16[32,3584]{1,0:T(8,128)(2,1)S(1)}, u32[]{:S(2)}, u32[]{:S(2)}) collective-permute-start(bf16[32,3584]{1,0:T(8,128)(2,1)S(1)} %collective-permute-done.6.refs_2_), channel_id=1, source_target_pairs={{0,1},{1,0},{2,3},{3,2},{4,5},{5,4},{6,7},{7,6},{8,9},{9,8},{10,11... | collective-permute-start | bytes 688136 | tf_op jit(solution)/shard_map/ppermute | solution.py:24
  92.3 3.4 %collective-permute-start.17 = (bf16[32,1792]{1,0:T(8,128)(2,1)S(1)}, bf16[32,1792]{1,0:T(8,128)(2,1)S(1)}, u32[]{:S(2)}, u32[]{:S(2)}) collective-permute-start(bf16[32,1792]{1,0:T(8,128)(2,1)S(1)} %collective-permute-done.8.refs_3_), channel_id=1, source_target_pairs={{0,1},{1,0},{2,3},{3,2},{4,5},{5,4},{6,7},{7,6},{8,9},{9,8},{10,11... | collective-permute-start | bytes 344072 | tf_op jit(solution)/shard_map/ppermute | solution.py:24
  93.5 2.3 %collective-permute-start.18 = (bf16[32,1792]{1,0:T(8,128)(2,1)S(1)}, bf16[32,1792]{1,0:T(8,128)(2,1)S(1)}, u32[]{:S(2)}, u32[]{:S(2)}) collective-permute-start(bf16[32,1792]{1,0:T(8,128)(2,1)S(1)} %collective-permute-done.9.refs_4_), channel_id=1, source_target_pairs={{0,1},{1,0},{2,3},{3,2},{4,5},{5,4},{6,7},{7,6},{8,9},{9,8},{10,11... | collective-permute-start | bytes 344072 | tf_op jit(solution)/shard_map/ppermute | solution.py:24
  93.5 7.6 %collective-permute-start.19 = (bf16[32,3712]{1,0:T(8,128)(2,1)S(1)}, bf16[32,3712]{1,0:T(8,128)(2,1)S(1)}, u32[]{:S(2)}, u32[]{:S(2)}) collective-permute-start(bf16[32,3712]{1,0:T(8,128)(2,1)S(1)} %pad_maximum_fusion.2.refs_0_), channel_id=1, source_target_pairs={{0,1},{1,0},{2,3},{3,2},{4,5},{5,4},{6,7},{7,6},{8,9},{9,8},{10,11... | collective-permute-start | bytes 712712 | tf_op jit(solution)/shard_map/ppermute | solution.py:24
  94.1 6.5 %collective-permute-start.13 = (bf16[32,1920]{1,0:T(8,128)(2,1)S(1)}, bf16[32,1920]{1,0:T(8,128)(2,1)S(1)}, u32[]{:S(2)}, u32[]{:S(2)}) collective-permute-start(bf16[32,1920]{1,0:T(8,128)(2,1)S(1)} %slice.66), channel_id=1, source_target_pairs={{0,4},{2,6},{4,0},{6,2},{8,12},{10,14},{12,8},{14,10},{16,20},{18,... | collective-permute-start | bytes 368648 | tf_op jit(solution)/shard_map/ppermute | solution.py:24
  94.4 6.2 %collective-permute-start.12 = (bf16[32,1792]{1,0:T(8,128)(2,1)S(1)}, bf16[32,1792]{1,0:T(8,128)(2,1)S(1)}, u32[]{:S(2)}, u32[]{:S(2)}) collective-permute-start(bf16[32,1792]{1,0:T(8,128)(2,1)S(1)} %slice.65), channel_id=1, source_target_pairs={{0,2},{2,0},{4,6},{6,4},{8,10},{10,8},{12,14},{14,12},{16,18},{18,... | collective-permute-start | bytes 344072 | tf_op jit(solution)/shard_map/ppermute | solution.py:24
  95.7 6.4 %collective-permute-start.20 = (bf16[32,3712]{1,0:T(8,128)(2,1)S(1)}, bf16[32,3712]{1,0:T(8,128)(2,1)S(1)}, u32[]{:S(2)}, u32[]{:S(2)}) collective-permute-start(bf16[32,3712]{1,0:T(8,128)(2,1)S(1)} %collective-permute-done.10.refs_1_), channel_id=1, source_target_pairs={{0,1},{1,0},{2,3},{3,2},{4,5},{5,4},{6,7},{7,6},{8,9},{9,8},{10,11... | collective-permute-start | bytes 712712 | tf_op jit(solution)/shard_map/ppermute | solution.py:24
  95.7 6.4 %collective-permute-start.21 = (bf16[32,3712]{1,0:T(8,128)(2,1)S(1)}, bf16[32,3712]{1,0:T(8,128)(2,1)S(1)}, u32[]{:S(2)}, u32[]{:S(2)}) collective-permute-start(bf16[32,3712]{1,0:T(8,128)(2,1)S(1)} %collective-permute-done.11.refs_2_), channel_id=1, source_target_pairs={{0,1},{1,0},{2,3},{3,2},{4,5},{5,4},{6,7},{7,6},{8,9},{9,8},{10,11... | collective-permute-start | bytes 712712 | tf_op jit(solution)/shard_map/ppermute | solution.py:24
  100.5 1.6 %collective-permute-start.23 = (bf16[32,1920]{1,0:T(8,128)(2,1)S(1)}, bf16[32,1920]{1,0:T(8,128)(2,1)S(1)}, u32[]{:S(2)}, u32[]{:S(2)}) collective-permute-start(bf16[32,1920]{1,0:T(8,128)(2,1)S(1)} %collective-permute-done.13.refs_4_), channel_id=1, source_target_pairs={{0,1},{1,0},{2,3},{3,2},{4,5},{5,4},{6,7},{7,6},{8,9},{9,8},{10,11... | collective-permute-start | bytes 368648 | tf_op jit(solution)/shard_map/ppermute | solution.py:24
  100.7 1.4 collective-permute-start.22
  108.5 4.0 %collective-permute-start.24 = (bf16[128,7168]{1,0:T(8,128)(2,1)S(1)}, bf16[128,7168]{1,0:T(8,128)(2,1)S(1)}, u32[]{:S(2)}, u32[]{:S(2)}) collective-permute-start(bf16[128,7168]{1,0:T(8,128)(2,1)S(1)} %get-tuple-element.51), channel_id=1, source_target_pairs={{0,1},{1,0},{2,3},{3,2},{4,5},{5,4},{6,7},{7,6},{8,9},{9,8},{10,11... | collective-permute-start | bytes 5505032 | tf_op jit(solution)/shard_map/ppermute | solution.py:24
  112.9 7.7 %collective-permute-start.25 = (bf16[32,3584]{1,0:T(8,128)(2,1)S(1)}, bf16[32,3584]{1,0:T(8,128)(2,1)S(1)}, u32[]{:S(2)}, u32[]{:S(2)}) collective-permute-start(bf16[32,3584]{1,0:T(8,128)(2,1)S(1)} %get-tuple-element.61), channel_id=1, source_target_pairs={{0,4},{2,6},{4,0},{6,2},{8,12},{10,14},{12,8},{14,10},{16,20},{18,... | collective-permute-start | bytes 688136 | tf_op jit(solution)/shard_map/ppermute | solution.py:24
  114.3 7.5 %collective-permute-start.27 = (bf16[32,3584]{1,0:T(8,128)(2,1)S(1)}, bf16[32,3584]{1,0:T(8,128)(2,1)S(1)}, u32[]{:S(2)}, u32[]{:S(2)}) collective-permute-start(bf16[32,3584]{1,0:T(8,128)(2,1)S(1)} %get-tuple-element.62), channel_id=1, source_target_pairs={{0,2},{2,0},{4,6},{6,4},{8,10},{10,8},{12,14},{14,12},{16,18},{18,... | collective-permute-start | bytes 688136 | tf_op jit(solution)/shard_map/ppermute | solution.py:24
  120.7 11.8 %collective-permute-start.26 = (bf16[32,7168]{1,0:T(8,128)(2,1)S(1)}, bf16[32,7168]{1,0:T(8,128)(2,1)S(1)}, u32[]{:S(2)}, u32[]{:S(2)}) collective-permute-start(bf16[32,7168]{1,0:T(8,128)(2,1)S(1)} %pad_maximum_fusion), channel_id=1, source_target_pairs={{0,2},{2,0},{4,6},{6,4},{8,10},{10,8},{12,14},{14,12},{16,18},{18,... | collective-permute-start | bytes 1376264 | tf_op jit(solution)/shard_map/ppermute | solution.py:24
  121.8 11.5 %collective-permute-start.28 = (bf16[32,7168]{1,0:T(8,128)(2,1)S(1)}, bf16[32,7168]{1,0:T(8,128)(2,1)S(1)}, u32[]{:S(2)}, u32[]{:S(2)}) collective-permute-start(bf16[32,7168]{1,0:T(8,128)(2,1)S(1)} %pad_maximum_fusion.1), channel_id=1, source_target_pairs={{0,4},{2,6},{4,0},{6,2},{8,12},{10,14},{12,8},{14,10},{16,20},{18,... | collective-permute-start | bytes 1376264 | tf_op jit(solution)/shard_map/ppermute | solution.py:24
  133.6 6.1 %collective-permute-start.29 = (bf16[16,7168]{1,0:T(8,128)(2,1)S(1)}, bf16[16,7168]{1,0:T(8,128)(2,1)S(1)}, u32[]{:S(2)}, u32[]{:S(2)}) collective-permute-start(bf16[16,7168]{1,0:T(8,128)(2,1)S(1)} %split.78), channel_id=1, source_target_pairs={{0,8},{2,10},{4,12},{6,14},{8,0},{10,2},{12,4},{14,6},{16,24},{18,... | collective-permute-start | bytes 688136 | tf_op jit(solution)/shard_map/ppermute | solution.py:24
  139.8 7.0 %collective-permute-start.30 = (bf16[8,7168]{1,0:T(8,128)(2,1)S(1)}, bf16[8,7168]{1,0:T(8,128)(2,1)S(1)}, u32[]{:S(2)}, u32[]{:S(2)}) collective-permute-start(bf16[8,7168]{1,0:T(8,128)(2,1)S(1)} %split.79), channel_id=1, source_target_pairs={{0,16},{2,18},{4,20},{6,22},{8,24},{10,26},{12,28},{14,30},{16,0},... | collective-permute-start | bytes 344072 | tf_op jit(solution)/shard_map/ppermute | solution.py:24
  (9 other events, 145.8 us)

commit v5 on v4

--- a/solution.py
+++ b/solution.py
@@ -30,7 +30,7 @@
 
 
 CHUNKS = 4
-AHEAD = 3
+IN_FLIGHT = 10 << 20
 
 
 def vmem_spec():
@@ -45,8 +45,12 @@
     return pl.ds(pl.multiple_of(n * size, size), size)
 
 
-def values_kernel(context, w_uv, w_o, part, values, uv_buf, o_buf, uv_sems, o_sems):
-    heads, _, dim = w_uv.shape
+def attention_kernel(
+    moved, lengths, queries, cached, arrived, w_uv, w_o, part, values,
+    keys, context, uv_buf, o_buf, uv_sems, o_sems,
+):
+    requests, heads, _ = queries.shape
+    latent, dim = w_uv.shape[1:]
     groups = uv_sems.shape[0]
     step = heads // groups
     chunks, depth, width = o_buf.shape
@@ -61,18 +65,41 @@
 
     for g in range(groups):
         copy_uv(g).start()
-    for n in range(AHEAD):
+    ahead = min(chunks, max(2, 2 * IN_FLIGHT // (2 * depth * width)))
+    for n in range(ahead):
         copy_o(n).start()
+    for i in range(requests):
+        row = moved[i]
+        keys[i] = jnp.where(row >= 0, arrived[jnp.maximum(row, 0)], cached[i])
+    scores, limits = [], []
+    for i in range(requests):
+        score = lax.dot_general(
+            queries[i], keys[i], (((1,), (1,)), ((), ())), preferred_element_type=jnp.float32
+        )
+        scores.append(score)
+        limits.append(jnp.full(score.shape, lengths[i], jnp.int32))
+    scores = jnp.concatenate(scores, axis=0) * score_scale
+    in_range = lax.broadcasted_iota(jnp.int32, scores.shape, 1) < jnp.concatenate(limits, axis=0)
+    scores = jnp.where(in_range, scores, -jnp.inf)
+    row_max = jnp.max(scores, axis=1, keepdims=True)
+    weights = jnp.where(in_range, jnp.exp(scores - row_max), 0.0)
+    probs = (weights / jnp.sum(weights, axis=1, keepdims=True)).astype(jnp.bfloat16)
+    for i in range(requests):
+        context[:, i, :] = jnp.dot(
+            probs[i * heads : (i + 1) * heads],
+            keys[i, :, :latent],
+            preferred_element_type=jnp.float32,
+        )
     for g in range(groups):
         copy_uv(g).wait()
         for h in range(g * step, (g + 1) * step):
             values[:, h * dim : (h + 1) * dim] = jnp.dot(
-                context[h], uv_buf[h], preferred_element_type=jnp.float32
+                context[h].astype(jnp.bfloat16), uv_buf[h], preferred_element_type=jnp.float32
             ).astype(jnp.bfloat16)
     for n in range(chunks):
         copy_o(n).wait()
-        if n + AHEAD < chunks:
-            copy_o(n + AHEAD).start()
+        if n + ahead < chunks:
+            copy_o(n + ahead).start()
         product = jnp.dot(
             values[:, n * depth : (n + 1) * depth], o_buf[n], preferred_element_type=jnp.float32
         )
@@ -82,33 +109,37 @@
             part[...] += product
 
 
-def values_and_first(context, w_uv, w_o, width):
-    heads, rows, latent = context.shape
+def attention_and_first(moved, lengths, queries, cached, arrived, w_uv, w_o, width):
+    requests, heads, key_width = queries.shape
+    latent = w_uv.shape[1]
     depth = w_o.shape[0]
     chunks = 8
     groups = 4 if heads % 4 == 0 else 1
+    smem = pl.BlockSpec(memory_space=pltpu.SMEM)
     return pl.pallas_call(
-        values_kernel,
+        attention_kernel,
         out_shape=(
-            jax.ShapeDtypeStruct((rows, width), jnp.float32),
-            jax.ShapeDtypeStruct((rows, depth), jnp.bfloat16),
-        ),
-        in_specs=[vmem_spec(), hbm_spec(), hbm_spec()],
+            jax.ShapeDtypeStruct((requests, width), jnp.float32),
+            jax.ShapeDtypeStruct((requests, depth), jnp.bfloat16),
+        ),
+        in_specs=[smem, smem] + [vmem_spec()] * 3 + [hbm_spec()] * 2,
         out_specs=(vmem_spec(), vmem_spec()),
         scratch_shapes=[
+            pltpu.VMEM(cached.shape, jnp.bfloat16),
+            pltpu.VMEM((heads, requests, latent), jnp.float32),
             pltpu.VMEM(w_uv.shape, jnp.bfloat16),
             pltpu.VMEM((chunks, depth // chunks, width), jnp.bfloat16),
             pltpu.SemaphoreType.DMA((groups,)),
             pltpu.SemaphoreType.DMA((chunks,)),
         ],
-        compiler_params=pltpu.CompilerParams(vmem_limit_bytes=44 << 20),
+        compiler_params=pltpu.CompilerParams(vmem_limit_bytes=48 << 20),
         cost_estimate=pl.CostEstimate(
-            flops=2 * rows * depth * (width + latent),
+            flops=2 * requests * depth * (width + latent),
             bytes_accessed=2 * depth * (width + latent),
-            transcendentals=0,
-        ),
-        name="values_and_first",
-    )(context, w_uv, w_o)
+            transcendentals=requests * heads * CTX,
+        ),
+        name="attention_and_first",
+    )(moved, lengths, queries, cached, arrived, w_uv, w_o)
 
 
 def columns_kernel(start, values, w_o, part, o_buf, o_sems):
@@ -118,12 +149,13 @@
         rows = pl.ds(n * depth, depth)
         return pltpu.make_async_copy(w_o.at[rows, pl.ds(start, width)], o_buf.at[n], o_sems.at[n])
 
-    for n in range(AHEAD):
+    ahead = min(chunks, max(2, IN_FLIGHT // (2 * depth * width)))
+    for n in range(ahead):
         copy_o(n).start()
     for n in range(chunks):
         copy_o(n).wait()
-        if n + AHEAD < chunks:
-            copy_o(n + AHEAD).start()
+        if n + ahead < chunks:
+            copy_o(n + ahead).start()
         product = jnp.dot(
             values[:, n * depth : (n + 1) * depth], o_buf[n], preferred_element_type=jnp.float32
         )
@@ -212,134 +244,158 @@
     )(*flat, w_gate, w_up)
 
 
-def far_kernel(set_count, *refs):
+def hold_kernel(after, w_gate, w_up, w_down, gate, up, down, done, sems):
+    half = gate.shape[0]
+    parts = sems.shape[1]
+
+    def copies(n):
+        size = half // parts
+        rows = pl.ds(n * size, size)
+        later = pl.ds(half + n * size, size)
+        units = pl.ds(n * (down.shape[0] // parts), down.shape[0] // parts)
+        return (
+            pltpu.make_async_copy(w_gate.at[0, later], gate.at[rows], sems.at[0, n]),
+            pltpu.make_async_copy(w_up.at[0, later], up.at[rows], sems.at[1, n]),
+            pltpu.make_async_copy(w_down.at[0, units], down.at[units], sems.at[2, n]),
+        )
+
+    for n in range(parts):
+        for copy in copies(n):
+            copy.start()
+    done[...] = after[...]
+    for n in range(parts):
+        for copy in copies(n):
+            copy.wait()
+
+
+def hold_weights(after, w_gate, w_up, w_down):
+    width, hidden_units = w_gate.shape[1:]
+    half = width // 2
+    return pl.pallas_call(
+        hold_kernel,
+        out_shape=(
+            pltpu.VMEM((half, hidden_units), jnp.bfloat16),
+            pltpu.VMEM((half, hidden_units), jnp.bfloat16),
+            pltpu.VMEM((hidden_units, width), jnp.bfloat16),
+            jax.ShapeDtypeStruct(after.shape, after.dtype),
+        ),
+        in_specs=[vmem_spec()] + [hbm_spec()] * 3,
+        out_specs=(vmem_spec(),) * 4,
+        scratch_shapes=[pltpu.SemaphoreType.DMA((3, 2))],
+        compiler_params=pltpu.CompilerParams(vmem_limit_bytes=4 << 20),
+        cost_estimate=pl.CostEstimate(
+            flops=0, bytes_accessed=4 * width * hidden_units, transcendentals=0
+        ),
+        name="hold_weights",
+    )(after, w_gate, w_up, w_down)
+
+
+def held(array):
+    return pltpu.with_memory_space_constraint(array, pltpu.VMEM)
+
+
+def second_kernel(set_count, *refs):
     flat, refs = refs[: 5 * set_count], refs[5 * set_count :]
     sets = [flat[5 * n : 5 * n + 5] for n in range(set_count)]
-    mask, gate_first, up_first, w_gate, w_up, w_down, far, kept = refs[:8]
-    gate_buf, up_buf, down_buf, gate_acc, up_acc, act, sems = refs[8:]
-    chunks, size, _ = gate_buf.shape
-    half = w_gate.shape[1] // 2
-    half_rows = far.shape[0]
-
-    def copies_in(n):
-        rows = pl.ds(half + n * size, size)
-        return (
-            pltpu.make_async_copy(w_gate.at[0, rows], gate_buf.at[n], sems.at[0, n]),
-            pltpu.make_async_copy(w_up.at[0, rows], up_buf.at[n], sems.at[1, n]),
-        )
-
-    def copy_down(n):
-        return pltpu.make_async_copy(w_down.at[0, :, span(n, size)], down_buf.at[n], sems.at[2, n])
-
-    for n in range(chunks):
-        for copy in copies_in(n):
-            copy.start()
-    for n in range(CHUNKS):
-        copy_down(n).start()
+    mask, gate_first, up_first, w_gate, w_up, w_down = refs[:6]
+    near, far, rest, gate_acc, up_acc, act = refs[6:]
+    half = w_gate.shape[0]
+    size = half // 2
+    line = near.shape[0] * 2 // set_count
     tails = []
     for own, near_x, near_y, low, high in sets:
         tails += [ref[:, half:] for ref in (own, near_x, near_y)] + [high[:, size:]]
     terms = jnp.concatenate(tails, axis=0).astype(jnp.float32)
     gates = jnp.sum(terms * mask[0:1], axis=1, keepdims=True)
     factors = jnp.sum(terms * mask[1:2], axis=1, keepdims=True)
-    for n in range(chunks):
+    for n in range(2):
         parts = []
         for own, near_x, near_y, low, high in sets:
             parts += [ref[:, n * size : (n + 1) * size] for ref in (own, near_x, near_y)]
             parts.append((low, high)[n][:, :size])
         rows = jnp.concatenate(parts, axis=0)
-        for copy in copies_in(n):
-            copy.wait()
         before = (gate_first, up_first) if n == 0 else (gate_acc, up_acc)
+        depth = slice(n * size, (n + 1) * size)
         gate_acc[...] = before[0][...] + jnp.dot(
-            rows, gate_buf[n], preferred_element_type=jnp.float32
-        )
-        up_acc[...] = before[1][...] + jnp.dot(rows, up_buf[n], preferred_element_type=jnp.float32)
+            rows, w_gate[depth], preferred_element_type=jnp.float32
+        )
+        up_acc[...] = before[1][...] + jnp.dot(
+            rows, w_up[depth], preferred_element_type=jnp.float32
+        )
     gated = gate_acc[...] * factors
     raised = up_acc[...] * factors
     act[...] = (gated / (1.0 + jnp.exp(-gated)) * raised * gates).astype(jnp.bfloat16)
-    kept[...] = act[:half_rows]
+    corners = []
+    for n in range(set_count):
+        rest[n * 3 * line : (n + 1) * 3 * line] = act[n * 4 * line : (n * 4 + 3) * line]
+        corners.append(act[(n * 4 + 3) * line : (n + 1) * 4 * line])
+    corner = jnp.concatenate(corners, axis=0)
+    mine = near.shape[0]
 
     @pl.loop(0, CHUNKS)
     def _(n):
-        copy_down(n).wait()
-        far[:, span(n, size)] = jnp.dot(
-            act[half_rows:], down_buf[n], preferred_element_type=jnp.float32
-        ).astype(jnp.bfloat16)
-
-
-def experts_far(sets, mask, sums, w_gate, w_up, w_down):
-    width, hidden_units = w_gate.shape[1:]
+        columns = span(n, size)
+        product = jnp.dot(corner, w_down[:, columns], preferred_element_type=jnp.float32)
+        near[:, columns] = product[:mine].astype(jnp.bfloat16)
+        far[:, columns] = product[mine:].astype(jnp.bfloat16)
+
+
+def experts_second(sets, mask, sums, w_gate, w_up, w_down):
+    hidden_units, width = w_down.shape
     rows = sums[0].shape[0]
-    size = width // CHUNKS
     flat = [piece for pieces in sets for piece in pieces]
+    corner = jax.ShapeDtypeStruct((rows // 8, width), jnp.bfloat16)
     return pl.pallas_call(
-        functools.partial(far_kernel, len(sets)),
+        functools.partial(second_kernel, len(sets)),
         out_shape=(
-            jax.ShapeDtypeStruct((rows // 2, width), jnp.bfloat16),
-            jax.ShapeDtypeStruct((rows // 2, hidden_units), jnp.bfloat16),
-        ),
-        in_specs=[vmem_spec()] * (len(flat) + 3) + [hbm_spec()] * 3,
-        out_specs=(vmem_spec(), vmem_spec()),
+            corner,
+            corner,
+            jax.ShapeDtypeStruct((rows // 4 * 3, hidden_units), jnp.bfloat16),
+        ),
+        in_specs=[vmem_spec()] * (len(flat) + 6),
+        out_specs=(vmem_spec(),) * 3,
         scratch_shapes=[
-            pltpu.VMEM((CHUNKS // 2, size, hidden_units), jnp.bfloat16),
-            pltpu.VMEM((CHUNKS // 2, size, hidden_units), jnp.bfloat16),
-            pltpu.VMEM((CHUNKS, hidden_units, size), jnp.bfloat16),
             pltpu.VMEM((rows, hidden_units), jnp.float32),
             pltpu.VMEM((rows, hidden_units), jnp.float32),
             pltpu.VMEM((rows, hidden_units), jnp.bfloat16),
-            pltpu.SemaphoreType.DMA((3, CHUNKS)),
         ],
-        compiler_params=pltpu.CompilerParams(vmem_limit_bytes=48 << 20),
+        compiler_params=pltpu.CompilerParams(vmem_limit_bytes=24 << 20),
         cost_estimate=pl.CostEstimate(
             flops=3 * rows * width * hidden_units,
-            bytes_accessed=4 * width * hidden_units + 3 * rows * width,
+            bytes_accessed=2 * rows * width,
             transcendentals=rows * hidden_units,
         ),
-        name="experts_far",
-    )(*flat, mask, *sums, w_gate, w_up, w_down)
-
-
-def down_kernel(kept, w_down, near, down_buf, sems):
-    size = down_buf.shape[2]
-
-    def copy(n):
-        columns = pl.ds(pl.multiple_of(n * size, size), size)
-        return pltpu.make_async_copy(w_down.at[0, :, columns], down_buf.at[n], sems.at[n])
-
-    for n in range(CHUNKS):
-        copy(n).start()
+        name="experts_second",
+    )(*flat, mask, *sums, held(w_gate), held(w_up), held(w_down))
+
+
+def rest_kernel(rest, w_down, near, far):
+    size = w_down.shape[1] // CHUNKS
+    mine = near.shape[0]
 
     @pl.loop(0, CHUNKS)
     def _(n):
-        copy(n).wait()
-        columns = pl.ds(pl.multiple_of(n * size, size), size)
-        near[:, columns] = jnp.dot(
-            kept[...], down_buf[n], preferred_element_type=jnp.float32
-        ).astype(jnp.bfloat16)
-
-
-def experts_near(kept, w_down):
-    rows, hidden_units = kept.shape
-    width = w_down.shape[2]
-    size = width // CHUNKS
+        columns = span(n, size)
+        product = jnp.dot(rest[...], w_down[:, columns], preferred_element_type=jnp.float32)
+        near[:, columns] = product[:mine].astype(jnp.bfloat16)
+        far[:, columns] = product[mine:].astype(jnp.bfloat16)
+
+
+def experts_rest(rest, w_down):
+    rows, hidden_units = rest.shape
+    width = w_down.shape[1]
+    outs = jax.ShapeDtypeStruct((rows // 2, width), jnp.bfloat16)
     return pl.pallas_call(
-        down_kernel,
-        out_shape=jax.ShapeDtypeStruct((rows, width), jnp.bfloat16),
-        in_specs=[vmem_spec(), hbm_spec()],
-        out_specs=vmem_spec(),
-        scratch_shapes=[
-            pltpu.VMEM((CHUNKS, hidden_units, size), jnp.bfloat16),
-            pltpu.SemaphoreType.DMA((CHUNKS,)),
-        ],
-        compiler_params=pltpu.CompilerParams(vmem_limit_bytes=32 << 20),
+        rest_kernel,
+        out_shape=(outs, outs),
+        in_specs=[vmem_spec()] * 2,
+        out_specs=(vmem_spec(),) * 2,
+        compiler_params=pltpu.CompilerParams(vmem_limit_bytes=24 << 20),
         cost_estimate=pl.CostEstimate(
-            flops=2 * rows * width * hidden_units,
-            bytes_accessed=2 * width * hidden_units + 2 * rows * width,
-            transcendentals=0,
-        ),
-        name="experts_near",
-    )(kept, w_down)
+            flops=2 * rows * width * hidden_units, bytes_accessed=2 * rows * width, transcendentals=0
+        ),
+        name="experts_rest",
+    )(rest, held(w_down))
 
 
 def moves(destination, replica_rows):
@@ -400,28 +456,28 @@
     return x.astype(jnp.bfloat16)
 
 
-def scatter_sums(near, far):
+def ep_sums(near, far):
     bits = bits_of("ep")[::-1]
     for bit in bits:
         came = flip(far, "ep", bit)
         if bit != bits[-1]:
-            both = narrow(plus(near, came))
-            near, far = jnp.split(both, 2, axis=0)
+            near, far = jnp.split(narrow(plus(near, came)), 2, axis=0)
+    return near, came
+
+
+def scatter_sums(corner, rest):
     inner_x, inner_y, outer = dp_bits()
-    width = near.shape[1]
-    half = width // 2
-    near = jnp.split(near, 4, axis=0)
-    came = jnp.split(came, 4, axis=0)
-    diagonal = narrow(plus(near[3], came[3]))
+    half = corner[0].shape[1] // 2
+    diagonal = narrow(plus(*ep_sums(*corner)))
     low = flip(diagonal[:, :half], "dp", inner_x)
     high = flip(diagonal[:, half:], "dp", inner_y)
-    to_x = plus(near[1], came[1])
-    to_y = plus(near[2], came[2])
+    own, to_x, to_y = zip(*(jnp.split(term, 3, axis=0) for term in ep_sums(*rest)))
+    to_x, to_y = plus(*to_x), plus(*to_y)
     to_x = narrow(jnp.concatenate([to_x[:, :half], to_x[:, half:] + plus(high)], axis=1))
     to_y = narrow(jnp.concatenate([to_y[:, :half] + plus(low), to_y[:, half:]], axis=1))
     from_x = flip(to_x, "dp", inner_x)
     from_y = flip(to_y, "dp", inner_y)
-    total = plus(near[0], came[0], from_x, from_y)
+    total = plus(*own, from_x, from_y)
     for bit in outer[::-1]:
         mine, other = jnp.split(total, 2, axis=0)
         total = mine + plus(flip(narrow(other), "dp", bit))
@@ -473,31 +529,19 @@
         to_box, (own_replica * MOVE_MAX, own_replica * replica_rows), (MOVE_MAX, replica_rows)
     )
     arrivals = migrate(packing, picker, latent_cache)
-    own_leave = jnp.sum(packing.astype(jnp.float32), axis=0) > 0
-    fetched = lax.dot_general(
-        packing, arrivals, (((0,), (0,)), ((), ())), preferred_element_type=jnp.float32
-    ).astype(jnp.bfloat16)
-    present = jnp.where(own_leave[:, None], fetched, latent_cache)
+    boxes = jnp.arange(1, MOVE_MAX + 1, dtype=jnp.float32)[:, None]
+    moved = jnp.sum(packing.astype(jnp.float32) * boxes, axis=0).astype(jnp.int32) - 1
     heads_dev = w_uv.shape[0]
-    latents = present.reshape(replica_rows, CTX, KV)
     query_rows = queries.reshape(replica_rows, heads_dev, KV)
-    scores = (
-        jnp.einsum("rhk,rtk->rht", query_rows, latents, preferred_element_type=jnp.float32)
-        * score_scale
-    )
-    in_range = jnp.arange(CTX, dtype=jnp.int32)[None, None, :] < lengths[:, None, None]
-    scores = jnp.where(in_range, scores, -jnp.inf)
-    row_max = jnp.max(scores, axis=2, keepdims=True)
-    weights = jnp.where(in_range, jnp.exp(scores - row_max), 0.0)
-    prob_rows = (weights / jnp.sum(weights, axis=2, keepdims=True)).astype(jnp.bfloat16)
-    context = narrow(
-        jnp.einsum("rht,rtl->rhl", prob_rows, latents[:, :, :LAT], preferred_element_type=jnp.float32)
-    )
+    cached = latent_cache.reshape(replica_rows, CTX, KV)
+    arrived = arrivals.reshape(MOVE_MAX, CTX, KV)
     width = residual.shape[1]
     half, size = width // 2, width // CHUNKS
     tokens = residual.astype(jnp.float32)
 
-    part, values = values_and_first(jnp.transpose(context, (1, 0, 2)), w_uv, w_o, half)
+    part, values = attention_and_first(
+        moved, lengths, query_rows, cached, arrived, w_uv, w_o, half
+    )
     hidden_a = tokens[:, :half] + head_sums(part)
     rows_a = narrow(hidden_a * norm_gain[None, :half])
     values, rows_a = lax.optimization_barrier((values, rows_a))
@@ -531,20 +575,24 @@
     high_a = flip(x_a[:, size:], "dp", inner_y)
     for bit in outer[1:]:
         held_b = jnp.concatenate([held_b, flip(held_b, "dp", bit)], axis=0)
-    held_b, low_a, high_a = lax.optimization_barrier((held_b, low_a, high_a))
-    x_b = flip(held_b, "dp", inner_x)
-    y_b = flip(held_b, "dp", inner_y)
-    sums = experts_first(all_sets((held_a, x_a, y_a, low_a, high_a)), w_gate, w_up)
-    low_b = flip(y_b[:, :size], "dp", inner_x)
-    high_b = flip(x_b[:, size:], "dp", inner_y)
-    low_b, high_b, sums = lax.optimization_barrier((low_b, high_b, sums))
     columns = jnp.arange(GATE_COLS, dtype=jnp.int32)
     gate_mask = (columns < 3 * replicas) & (columns % replicas == own_replica)
     factor_mask = (columns >= 3 * replicas) & (columns < 3 * replicas + 3)
     mask = jnp.stack([gate_mask, factor_mask]).astype(jnp.float32)
+    held_b, low_a, high_a, mask = lax.optimization_barrier((held_b, low_a, high_a, mask))
+    x_b = flip(held_b, "dp", inner_x)
+    y_b = flip(held_b, "dp", inner_y)
+    gate_held, up_held, down_held, mask = hold_weights(mask, w_gate, w_up, w_down)
+    low_a, high_a, mask = lax.optimization_barrier((low_a, high_a, mask))
+    sets_a = all_sets((held_a, x_a, y_a, low_a, high_a))
+    x_b, y_b, sets_a = lax.optimization_barrier((x_b, y_b, sets_a))
+    low_b = flip(y_b[:, :size], "dp", inner_x)
+    high_b = flip(x_b[:, size:], "dp", inner_y)
+    sums = experts_first(sets_a, w_gate, w_up)
+    low_b, high_b, sums = lax.optimization_barrier((low_b, high_b, sums))
     sets_b = all_sets((held_b, x_b, y_b, low_b, high_b))
-    far, kept = experts_far(sets_b, mask, sums, w_gate, w_up, w_down)
-    mixture = scatter_sums(experts_near(kept, w_down), far)
+    near, far, rest = experts_second(sets_b, mask, sums, gate_held, up_held, down_held)
+    mixture = scatter_sums((near, far), experts_rest(rest, down_held))
     hidden = jnp.concatenate([hidden_a, hidden_b], axis=1)
     layer_out = (hidden + mixture).astype(jnp.bfloat16)
     return (layer_out, arrivals)

time: 149 us -> 144 us (0.966)
  waiting for transfers between devices: 58.8 us -> 53.1 us
  matrix products: 5.24 us -> 3.16 us
  starting transfers between devices: 33.3 us -> 35.1 us
  Pallas kernels: 38.1 us -> 39.8 us
    ppermute x31 -> x32, waiting for transfers between devices: 45.7 us -> 42.1 us  [flip(): return lax.ppermute(x, axis, pairs)]
    dot_general x3 -> x0, matrix products: 2.15 us -> none  [the longest x1 1.02 us: per_device(): jnp.einsum('rht,rtl->rhl', prob_rows, latents[:, :, :LAT], preferred_elem...]
    pallas_call x3 -> x4, Pallas kernels: 21.7 us -> 23.8 us  [the longest x1 12.4 us: attention_and_first(): pl.pallas_call(attention_kernel, out_shape=(jax.ShapeDtypeStruct((request...]
    all_to_all x1, waiting for transfers between devices: 6.23 us -> 4.19 us  [migrate(): lax.all_to_all(sorted_rows.reshape(replicas, MOVE_MAX, share), 'dp', spli...]
    ppermute x31 -> x32, starting transfers between devices: 21.4 us -> 23.1 us  [flip(): return lax.ppermute(x, axis, pairs)]
  transfers between devices with their start and end apart: 33 -> 34, of which waited for: 19 -> 20; matrix products, arithmetic and copies ran while one was open for 2% -> 4% of each run, Pallas kernels for 14% -> 16%
where the time goes in v5:
time: 144 us
  waiting for transfers between devices  53.1 us (37%)
  Pallas kernels  39.8 us (28%)
  starting transfers between devices  35.1 us (24%)
  local copies, waits for them, and re-layouts  5.72 us (4%)
  other arithmetic  3.71 us (3%)
  matrix products  3.16 us (2%)
  blocking collectives  2.19 us (2%)
    ppermute x32, waiting for transfers between devices, flip(): return lax.ppermute(x, axis, pairs)  42.1 us
    ppermute x32, starting transfers between devices, flip(): return lax.ppermute(x, axis, pairs)  23.1 us
    pallas_call x1, Pallas kernels, attention_and_first(): pl.pallas_call(attention_kernel, out_shape=(jax.ShapeDtypeStruct((request...  12.4 us
    pallas_call x2, Pallas kernels, more_columns(): pl.pallas_call(functools.partial(columns_kernel, start), out_shape=jax.Sh...  11.8 us
    all_to_all x1, starting transfers between devices, migrate(): met = lax.all_to_all(outbox, 'dp', split_axis=0, concat_axis=0)  8.31 us
    all_to_all x1, waiting for transfers between devices, migrate(): met = lax.all_to_all(outbox, 'dp', split_axis=0, concat_axis=0)  6.88 us
    pallas_call x1, Pallas kernels, hold_weights(): pl.pallas_call(hold_kernel, out_shape=(pltpu.VMEM((half, hidden_units), j...  5.29 us
    pallas_call x1, Pallas kernels, experts_first(): pl.pallas_call(functools.partial(first_kernel, len(sets)), out_shape=(sum...  4.3 us
  transfers between devices with their start and end apart: 34, of which 20 were waited for; matrix products, arithmetic and copies ran while one was open for 4% of the time, Pallas kernels for 16%

profile of v5, /device:TPU:0, one launch (start us, length us, event | category | flops | bytes accessed | tf_op | source)
XLA Modules:
  0.0 144.0 jit_solution(17504442267160261639)
XLA Ops:
  2.3 2.0 %convolution_convert_fusion = bf16[4,18432]{1,0:T(4,128)(2,1)} fusion(bf16[16,36864]{1,0:T(8,128)(2,1)} %param.15, s32[]{:T(128)S(6)} %select_n.69, pred[64,256]{1,0:T(8,128)(4,1)S(1)} %iota_compare_fusion.4, s32[]{:T(128)S(6)} %select_n.67, s32[]{:T(128)S(6)} %select_n.68), kind=kOutput, calls=%fused_computation | convolution fusion | flops 2433024 | bytes 737804 | tf_op jit(solution)/shard_map/dot_general | solution.py:426
  4.3 8.3 %all-to-all-start = ((bf16[16,4,1152]{2,1,0:T(4,128)(2,1)}), bf16[16,4,1152]{2,1,0:T(4,128)(2,1)S(1)}, u32[]{:S(2)}, u32[]{:S(2)}) async-start(bf16[16,4,1152]{2,1,0:T(4,128)(2,1)} %bitcast.1), calls=%async_computation | async-start | bytes 294912 | tf_op jit(solution)/shard_map/all_to_all | solution.py:428
  13.6 6.9 %all-to-all-done = bf16[16,4,1152]{2,1,0:T(4,128)(2,1)S(1)} async-done(((bf16[16,4,1152]{2,1,0:T(4,128)(2,1)}), bf16[16,4,1152]{2,1,0:T(4,128)(2,1)S(1)}, u32[]{:S(2)}, u32[]{:S(2)}) %all-to-all-start) | async-done | bytes 147488 | tf_op jit(solution)/shard_map/all_to_all | solution.py:428
  21.4 3.6 %all-to-all-start.1 = ((bf16[16,4,1152]{2,1,0:T(4,128)(2,1)}), bf16[16,4,1152]{2,1,0:T(4,128)(2,1)S(1)}, u32[]{:S(2)}, u32[]{:S(2)}) async-start(bf16[16,4,1152]{2,1,0:T(4,128)(2,1)} %reshape.194), calls=%async_computation.1 | async-start | bytes 294912 | tf_op jit(solution)/shard_map/all_to_all | solution.py:432
  25.2 1.6 %reshape.191.cached = bf16[16,64,576]{2,1,0:T(8,128)(2,1)S(1)} reshape(bf16[16,36864]{1,0:T(8,128)(2,1)S(1)} %copy-done.1) | data formatting | bytes 2359296 | tf_op jit(solution)/shard_map/reshape | solution.py:536
  26.9 1.8 %reshape.190.queries = bf16[16,32,576]{2,1,0:T(8,128)(2,1)S(1)} reshape(bf16[16,18432]{1,0:T(8,128)(2,1)} %param.14) | data formatting | bytes 1179648 | tf_op jit(solution)/shard_map/reshape | solution.py:535
  28.7 4.2 %all-to-all-done.1 = bf16[16,4,1152]{2,1,0:T(4,128)(2,1)S(1)} async-done(((bf16[16,4,1152]{2,1,0:T(4,128)(2,1)}), bf16[16,4,1152]{2,1,0:T(4,128)(2,1)S(1)}, u32[]{:S(2)}, u32[]{:S(2)}) %all-to-all-start.1) | async-done | bytes 147488 | tf_op jit(solution)/shard_map/all_to_all | solution.py:432
  32.9 2.2 %all_gather.3 = bf16[4,36864]{1,0:T(4,128)(2,1)S(1)} all-gather(bf16[4,18432]{1,0:T(4,128)(2,1)S(1)} %bitcast.10), channel_id=1, replica_groups=mesh['dp'=16,'ep'=2] {'ep'}, dimensions={1}, use_global_device_ids=true | all-gather | bytes 442368 | tf_op jit(solution)/shard_map/all_gather | solution.py:436
  35.5 12.4 %attention_and_first.1 = (f32[16,3584]{1,0:T(8,128)S(1)}, bf16[16,4096]{1,0:T(8,128)(2,1)S(1)}) custom-call(s32[16]{0:T(128)S(1)} %convert_add_fusion.3.moved, s32[16]{0:T(128)S(1)} %copy-done, bf16[16,32,576]{2,1,0:T(8,128)(2,1)S(1)} %reshape.190.queries, bf16[16,64,576]{2,1,0:T(8,128)(2,1)S(1)} %reshape.191.cached, ...), custom_call_target="tpu_custom_call" | custom-call | flops 536870912 | bytes 33554432 | tf_op jit(solution)/shard_map/attention_and_first/pallas_call | solution.py:119
  48.2 1.2 collective-permute-done
  50.6 5.0 %more_columns.2 = f32[16,1408]{1,0:T(8,128)S(1)} custom-call(bf16[16,4096]{1,0:T(8,128)(2,1)S(1)} %get-tuple-element.56.values, bf16[4096,7168]{1,0:T(8,128)(2,1)} %w_o.5), custom_call_target="tpu_custom_call" | custom-call | flops 184549376 | bytes 11534336 | tf_op jit(solution)/shard_map/more_columns/pallas_call | solution.py:171
  56.6 6.8 %more_columns.3 = f32[16,2176]{1,0:T(8,128)S(1)} custom-call(bf16[16,4096]{1,0:T(8,128)(2,1)S(1)} %get-tuple-element.56.values, bf16[4096,7168]{1,0:T(8,128)(2,1)} %w_o.5), custom_call_target="tpu_custom_call" | custom-call | flops 285212672 | bytes 17825792 | tf_op jit(solution)/shard_map/more_columns/pallas_call | solution.py:171
  63.7 1.3 collective-permute-done.3
  65.4 1.8 %collective-permute-start.4 = (bf16[8,3712]{1,0:T(8,128)(2,1)S(1)}, bf16[8,3712]{1,0:T(8,128)(2,1)S(1)}, u32[]{:S(2)}, u32[]{:S(2)}) collective-permute-start(bf16[8,3712]{1,0:T(8,128)(2,1)S(1)} %concatenate.33), channel_id=1, source_target_pairs={{0,16},{2,18},{4,20},{6,22},{8,24},{10,26},{12,28},{14,30},{16,0},... | collective-permute-start | bytes 178184 | tf_op jit(solution)/shard_map/ppermute | solution.py:24
  68.5 3.1 %collective-permute-done.4 = bf16[8,3712]{1,0:T(8,128)(2,1)S(1)} collective-permute-done((bf16[8,3712]{1,0:T(8,128)(2,1)S(1)}, bf16[8,3712]{1,0:T(8,128)(2,1)S(1)}, u32[]{:S(2)}, u32[]{:S(2)}) %collective-permute-start.4) | collective-permute-done | bytes 59424 | tf_op jit(solution)/shard_map/ppermute | solution.py:24
  71.6 2.9 %collective-permute-done.6.refs_2_ = bf16[32,3584]{1,0:T(8,128)(2,1)S(1)} collective-permute-done((bf16[32,3584]{1,0:T(8,128)(2,1)S(1)}, bf16[32,3584]{1,0:T(8,128)(2,1)S(1)}, u32[]{:S(2)}, u32[]{:S(2)}) %collective-permute-start.6) | collective-permute-done | bytes 229408 | tf_op jit(solution)/shard_map/ppermute | solution.py:24
  75.0 1.3 collective-permute-start.7
  77.0 1.3 collective-permute-start.9
  79.9 2.2 %collective-permute-done.9.refs_4_ = bf16[32,1792]{1,0:T(8,128)(2,1)S(1)} collective-permute-done((bf16[32,1792]{1,0:T(8,128)(2,1)S(1)}, bf16[32,1792]{1,0:T(8,128)(2,1)S(1)}, u32[]{:S(2)}, u32[]{:S(2)}) %collective-permute-start.9) | collective-permute-done | bytes 114720 | tf_op jit(solution)/shard_map/ppermute | solution.py:24
  84.6 5.3 %hold_weights.1 = (bf16[3584,512]{1,0:T(8,128)(2,1)S(1)}, bf16[3584,512]{1,0:T(8,128)(2,1)S(1)}, bf16[512,7168]{1,0:T(8,128)(2,1)S(1)}, f32[2,128]{1,0:T(2,128)S(1)}) custom-call(f32[2,128]{1,0:T(2,128)S(1)} %add_convert_fusion.1.after, bf16[1,7168,512]{2,1,0:T(8,128)(2,1)} %refs_10_.1, bf16[1,7168,512]{2,1,0:T(8,128)(2,1)} %refs_11_.1, ...), custom_call_target="tpu_custom_call" | custom-call | bytes 14680064 | tf_op jit(solution)/shard_map/hold_weights/pallas_call | solution.py:274
  92.5 1.3 collective-permute-start.17
  93.8 1.3 collective-permute-start.18
  95.1 4.3 %experts_first.1 = (f32[256,512]{1,0:T(8,128)S(1)}, f32[256,512]{1,0:T(8,128)S(1)}) custom-call(bf16[32,3584]{1,0:T(8,128)(2,1)S(1)} %pad_maximum_fusion.3.refs_0_, bf16[32,3584]{1,0:T(8,128)(2,1)S(1)} %collective-permute-done.5.refs_1_, bf16[32,3584]{1,0:T(8,128)(2,1)S(1)} %collective-permute-done.6.refs_2_, ...), custom_call_target="tpu_custom_call" | custom-call | flops 1879048192 | bytes 9175040 | tf_op jit(solution)/shard_map/experts_first/pallas_call | solution.py:227
  101.0 3.9 %experts_second.1 = (bf16[32,7168]{1,0:T(8,128)(2,1)S(1)}, bf16[32,7168]{1,0:T(8,128)(2,1)S(1)}, bf16[192,512]{1,0:T(8,128)(2,1)S(1)}) custom-call(bf16[32,3712]{1,0:T(8,128)(2,1)S(1)} %pad_maximum_fusion.2.refs_0_, bf16[32,3712]{1,0:T(8,128)(2,1)S(1)} %collective-permute-done.10.refs_1_, bf16[32,3712]{1,0:T(8,128)(2,1)S(1)} %collective-permute-done.11.refs_2_, ...), custom_call_target="tpu_custom_call" | custom-call | flops 2818572288 | bytes 3670016 | tf_op jit(solution)/shard_map/experts_second/pallas_call | solution.py:348
  105.2 2.2 %experts_rest.1 = (bf16[96,7168]{1,0:T(8,128)(2,1)S(1)}, bf16[96,7168]{1,0:T(8,128)(2,1)S(1)}) custom-call(bf16[192,512]{1,0:T(8,128)(2,1)S(1)} %get-tuple-element.93.rest, bf16[512,7168]{1,0:T(8,128)(2,1)S(1)} %get-tuple-element.92.refs_15_.w_down), custom_call_target="tpu_custom_call" | custom-call | flops 1409286144 | bytes 2752512 | tf_op jit(solution)/shard_map/experts_rest/pallas_call | solution.py:388
  110.8 5.4 %collective-permute-done.28 = bf16[32,3584]{1,0:T(8,128)(2,1)S(1)} collective-permute-done((bf16[32,3584]{1,0:T(8,128)(2,1)S(1)}, bf16[32,3584]{1,0:T(8,128)(2,1)S(1)}, u32[]{:S(2)}, u32[]{:S(2)}) %collective-permute-start.28) | collective-permute-done | bytes 229408 | tf_op jit(solution)/shard_map/ppermute | solution.py:24
  116.3 1.3 collective-permute-start.29
  117.8 1.2 collective-permute-start.27
  119.0 9.0 %collective-permute-done.29 = bf16[32,7168]{1,0:T(8,128)(2,1)S(1)} collective-permute-done((bf16[32,7168]{1,0:T(8,128)(2,1)S(1)}, bf16[32,7168]{1,0:T(8,128)(2,1)S(1)}, u32[]{:S(2)}, u32[]{:S(2)}) %collective-permute-start.29) | collective-permute-done | bytes 458784 | tf_op jit(solution)/shard_map/ppermute | solution.py:24
  130.3 5.3 %collective-permute-done.30 = bf16[16,7168]{1,0:T(8,128)(2,1)S(1)} collective-permute-done((bf16[16,7168]{1,0:T(8,128)(2,1)S(1)}, bf16[16,7168]{1,0:T(8,128)(2,1)S(1)}, u32[]{:S(2)}, u32[]{:S(2)}) %collective-permute-start.30) | collective-permute-done | bytes 229408 | tf_op jit(solution)/shard_map/ppermute | solution.py:24
  135.6 1.2 collective-permute-start.31
  136.8 5.8 %collective-permute-done.31 = bf16[8,7168]{1,0:T(8,128)(2,1)S(1)} collective-permute-done((bf16[8,7168]{1,0:T(8,128)(2,1)S(1)}, bf16[8,7168]{1,0:T(8,128)(2,1)S(1)}, u32[]{:S(2)}, u32[]{:S(2)}) %collective-permute-start.31) | collective-permute-done | bytes 114720 | tf_op jit(solution)/shard_map/ppermute | solution.py:24
  (114 shorter events, 25.4 us)
Async XLA Ops:
  4.3 16.2 %all-to-all-start = ((bf16[16,4,1152]{2,1,0:T(4,128)(2,1)}), bf16[16,4,1152]{2,1,0:T(4,128)(2,1)S(1)}, u32[]{:S(2)}, u32[]{:S(2)}) async-start(bf16[16,4,1152]{2,1,0:T(4,128)(2,1)} %bitcast.1), calls=%async_computation | async-start | bytes 294912 | tf_op jit(solution)/shard_map/all_to_all | solution.py:428
  21.4 11.5 %all-to-all-start.1 = ((bf16[16,4,1152]{2,1,0:T(4,128)(2,1)}), bf16[16,4,1152]{2,1,0:T(4,128)(2,1)S(1)}, u32[]{:S(2)}, u32[]{:S(2)}) async-start(bf16[16,4,1152]{2,1,0:T(4,128)(2,1)} %reshape.194), calls=%async_computation.1 | async-start | bytes 294912 | tf_op jit(solution)/shard_map/all_to_all | solution.py:432
  48.0 1.4 collective-permute-start
  49.6 6.2 %collective-permute-start.1 = (bf16[8,3584]{1,0:T(8,128)(2,1)S(1)}, bf16[8,3584]{1,0:T(8,128)(2,1)S(1)}, u32[]{:S(2)}, u32[]{:S(2)}) collective-permute-start(bf16[8,3584]{1,0:T(8,128)(2,1)S(1)} %multiply_convert_fusion.1), channel_id=1, source_target_pairs={{0,16},{2,18},{4,20},{6,22},{8,24},{10,26},{12,28},{14,30},{16,0},... | collective-permute-start | bytes 172040 | tf_op jit(solution)/shard_map/ppermute | solution.py:24
  55.7 7.7 %collective-permute-start.2 = (bf16[16,3584]{1,0:T(8,128)(2,1)S(1)}, bf16[16,3584]{1,0:T(8,128)(2,1)S(1)}, u32[]{:S(2)}, u32[]{:S(2)}) collective-permute-start(bf16[16,3584]{1,0:T(8,128)(2,1)S(1)} %pad_maximum_fusion.5), channel_id=1, source_target_pairs={{0,8},{2,10},{4,12},{6,14},{8,0},{10,2},{12,4},{14,6},{16,24},{18,... | collective-permute-start | bytes 344072 | tf_op jit(solution)/shard_map/ppermute | solution.py:24
  65.4 6.3 %collective-permute-start.4 = (bf16[8,3712]{1,0:T(8,128)(2,1)S(1)}, bf16[8,3712]{1,0:T(8,128)(2,1)S(1)}, u32[]{:S(2)}, u32[]{:S(2)}) collective-permute-start(bf16[8,3712]{1,0:T(8,128)(2,1)S(1)} %concatenate.33), channel_id=1, source_target_pairs={{0,16},{2,18},{4,20},{6,22},{8,24},{10,26},{12,28},{14,30},{16,0},... | collective-permute-start | bytes 178184 | tf_op jit(solution)/shard_map/ppermute | solution.py:24
  67.2 7.4 %collective-permute-start.6 = (bf16[32,3584]{1,0:T(8,128)(2,1)S(1)}, bf16[32,3584]{1,0:T(8,128)(2,1)S(1)}, u32[]{:S(2)}, u32[]{:S(2)}) collective-permute-start(bf16[32,3584]{1,0:T(8,128)(2,1)S(1)} %pad_maximum_fusion.3.refs_0_), channel_id=1, source_target_pairs={{0,4},{2,6},{4,0},{6,2},{8,12},{10,14},{12,8},{14,10},{16,20},{18,... | collective-permute-start | bytes 688136 | tf_op jit(solution)/shard_map/ppermute | solution.py:24
  67.9 7.1 %collective-permute-start.5 = (bf16[32,3584]{1,0:T(8,128)(2,1)S(1)}, bf16[32,3584]{1,0:T(8,128)(2,1)S(1)}, u32[]{:S(2)}, u32[]{:S(2)}) collective-permute-start(bf16[32,3584]{1,0:T(8,128)(2,1)S(1)} %pad_maximum_fusion.3.refs_0_), channel_id=1, source_target_pairs={{0,2},{2,0},{4,6},{6,4},{8,10},{10,8},{12,14},{14,12},{16,18},{18,... | collective-permute-start | bytes 688136 | tf_op jit(solution)/shard_map/ppermute | solution.py:24
  75.0 4.8 %collective-permute-start.7 = (bf16[16,3712]{1,0:T(8,128)(2,1)S(1)}, bf16[16,3712]{1,0:T(8,128)(2,1)S(1)}, u32[]{:S(2)}, u32[]{:S(2)}) collective-permute-start(bf16[16,3712]{1,0:T(8,128)(2,1)S(1)} %pad_maximum_fusion.4), channel_id=1, source_target_pairs={{0,8},{2,10},{4,12},{6,14},{8,0},{10,2},{12,4},{14,6},{16,24},{18,... | collective-permute-start | bytes 356360 | tf_op jit(solution)/shard_map/ppermute | solution.py:24
  76.3 13.6 %collective-permute-start.12 = (bf16[32,3584]{1,0:T(8,128)(2,1)S(1)}, bf16[32,3584]{1,0:T(8,128)(2,1)S(1)}, u32[]{:S(2)}, u32[]{:S(2)}) collective-permute-start(bf16[32,3584]{1,0:T(8,128)(2,1)S(1)} %pad_maximum_fusion.3.refs_0_), channel_id=1, source_target_pairs={{0,1},{1,0},{2,3},{3,2},{4,5},{5,4},{6,7},{7,6},{8,9},{9,8},{10,11... | collective-permute-start | bytes 688136 | tf_op jit(solution)/shard_map/ppermute | solution.py:24
  76.4 14.1 %collective-permute-start.14 = (bf16[32,3584]{1,0:T(8,128)(2,1)S(1)}, bf16[32,3584]{1,0:T(8,128)(2,1)S(1)}, u32[]{:S(2)}, u32[]{:S(2)}) collective-permute-start(bf16[32,3584]{1,0:T(8,128)(2,1)S(1)} %collective-permute-done.6.refs_2_), channel_id=1, source_target_pairs={{0,1},{1,0},{2,3},{3,2},{4,5},{5,4},{6,7},{7,6},{8,9},{9,8},{10,11... | collective-permute-start | bytes 688136 | tf_op jit(solution)/shard_map/ppermute | solution.py:24
  77.0 5.1 %collective-permute-start.9 = (bf16[32,1792]{1,0:T(8,128)(2,1)S(1)}, bf16[32,1792]{1,0:T(8,128)(2,1)S(1)}, u32[]{:S(2)}, u32[]{:S(2)}) collective-permute-start(bf16[32,1792]{1,0:T(8,128)(2,1)S(1)} %slice.49), channel_id=1, source_target_pairs={{0,4},{2,6},{4,0},{6,2},{8,12},{10,14},{12,8},{14,10},{16,20},{18,... | collective-permute-start | bytes 344072 | tf_op jit(solution)/shard_map/ppermute | solution.py:24
  78.3 4.8 %collective-permute-start.8 = (bf16[32,1792]{1,0:T(8,128)(2,1)S(1)}, bf16[32,1792]{1,0:T(8,128)(2,1)S(1)}, u32[]{:S(2)}, u32[]{:S(2)}) collective-permute-start(bf16[32,1792]{1,0:T(8,128)(2,1)S(1)} %slice.48), channel_id=1, source_target_pairs={{0,2},{2,0},{4,6},{6,4},{8,10},{10,8},{12,14},{14,12},{16,18},{18,... | collective-permute-start | bytes 344072 | tf_op jit(solution)/shard_map/ppermute | solution.py:24
  83.1 8.7 %collective-permute-start.11 = (bf16[32,3712]{1,0:T(8,128)(2,1)S(1)}, bf16[32,3712]{1,0:T(8,128)(2,1)S(1)}, u32[]{:S(2)}, u32[]{:S(2)}) collective-permute-start(bf16[32,3712]{1,0:T(8,128)(2,1)S(1)} %pad_maximum_fusion.2.refs_0_), channel_id=1, source_target_pairs={{0,4},{2,6},{4,0},{6,2},{8,12},{10,14},{12,8},{14,10},{16,20},{18,... | collective-permute-start | bytes 712712 | tf_op jit(solution)/shard_map/ppermute | solution.py:24
  83.9 8.0 %collective-permute-start.10 = (bf16[32,3712]{1,0:T(8,128)(2,1)S(1)}, bf16[32,3712]{1,0:T(8,128)(2,1)S(1)}, u32[]{:S(2)}, u32[]{:S(2)}) collective-permute-start(bf16[32,3712]{1,0:T(8,128)(2,1)S(1)} %pad_maximum_fusion.2.refs_0_), channel_id=1, source_target_pairs={{0,2},{2,0},{4,6},{6,4},{8,10},{10,8},{12,14},{14,12},{16,18},{18,... | collective-permute-start | bytes 712712 | tf_op jit(solution)/shard_map/ppermute | solution.py:24
  84.6 6.0 %collective-permute-start.13 = (bf16[32,3584]{1,0:T(8,128)(2,1)S(1)}, bf16[32,3584]{1,0:T(8,128)(2,1)S(1)}, u32[]{:S(2)}, u32[]{:S(2)}) collective-permute-start(bf16[32,3584]{1,0:T(8,128)(2,1)S(1)} %collective-permute-done.5.refs_1_), channel_id=1, source_target_pairs={{0,1},{1,0},{2,3},{3,2},{4,5},{5,4},{6,7},{7,6},{8,9},{9,8},{10,11... | collective-permute-start | bytes 688136 | tf_op jit(solution)/shard_map/ppermute | solution.py:24
  89.9 1.5 %collective-permute-start.15 = (bf16[32,1792]{1,0:T(8,128)(2,1)S(1)}, bf16[32,1792]{1,0:T(8,128)(2,1)S(1)}, u32[]{:S(2)}, u32[]{:S(2)}) collective-permute-start(bf16[32,1792]{1,0:T(8,128)(2,1)S(1)} %collective-permute-done.8.refs_3_), channel_id=1, source_target_pairs={{0,1},{1,0},{2,3},{3,2},{4,5},{5,4},{6,7},{7,6},{8,9},{9,8},{10,11... | collective-permute-start | bytes 344072 | tf_op jit(solution)/shard_map/ppermute | solution.py:24
  90.6 9.4 %collective-permute-start.19 = (bf16[32,3712]{1,0:T(8,128)(2,1)S(1)}, bf16[32,3712]{1,0:T(8,128)(2,1)S(1)}, u32[]{:S(2)}, u32[]{:S(2)}) collective-permute-start(bf16[32,3712]{1,0:T(8,128)(2,1)S(1)} %pad_maximum_fusion.2.refs_0_), channel_id=1, source_target_pairs={{0,1},{1,0},{2,3},{3,2},{4,5},{5,4},{6,7},{7,6},{8,9},{9,8},{10,11... | collective-permute-start | bytes 712712 | tf_op jit(solution)/shard_map/ppermute | solution.py:24
  91.9 9.1 %collective-permute-start.20 = (bf16[32,3712]{1,0:T(8,128)(2,1)S(1)}, bf16[32,3712]{1,0:T(8,128)(2,1)S(1)}, u32[]{:S(2)}, u32[]{:S(2)}) collective-permute-start(bf16[32,3712]{1,0:T(8,128)(2,1)S(1)} %collective-permute-done.10.refs_1_), channel_id=1, source_target_pairs={{0,1},{1,0},{2,3},{3,2},{4,5},{5,4},{6,7},{7,6},{8,9},{9,8},{10,11... | collective-permute-start | bytes 712712 | tf_op jit(solution)/shard_map/ppermute | solution.py:24
  92.1 8.9 %collective-permute-start.21 = (bf16[32,3712]{1,0:T(8,128)(2,1)S(1)}, bf16[32,3712]{1,0:T(8,128)(2,1)S(1)}, u32[]{:S(2)}, u32[]{:S(2)}) collective-permute-start(bf16[32,3712]{1,0:T(8,128)(2,1)S(1)} %collective-permute-done.11.refs_2_), channel_id=1, source_target_pairs={{0,1},{1,0},{2,3},{3,2},{4,5},{5,4},{6,7},{7,6},{8,9},{9,8},{10,11... | collective-permute-start | bytes 712712 | tf_op jit(solution)/shard_map/ppermute | solution.py:24
  92.5 6.8 %collective-permute-start.17 = (bf16[32,1792]{1,0:T(8,128)(2,1)S(1)}, bf16[32,1792]{1,0:T(8,128)(2,1)S(1)}, u32[]{:S(2)}, u32[]{:S(2)}) collective-permute-start(bf16[32,1792]{1,0:T(8,128)(2,1)S(1)} %slice.50), channel_id=1, source_target_pairs={{0,2},{2,0},{4,6},{6,4},{8,10},{10,8},{12,14},{14,12},{16,18},{18,... | collective-permute-start | bytes 344072 | tf_op jit(solution)/shard_map/ppermute | solution.py:24
  93.8 5.6 %collective-permute-start.18 = (bf16[32,1920]{1,0:T(8,128)(2,1)S(1)}, bf16[32,1920]{1,0:T(8,128)(2,1)S(1)}, u32[]{:S(2)}, u32[]{:S(2)}) collective-permute-start(bf16[32,1920]{1,0:T(8,128)(2,1)S(1)} %slice.51), channel_id=1, source_target_pairs={{0,4},{2,6},{4,0},{6,2},{8,12},{10,14},{12,8},{14,10},{16,20},{18,... | collective-permute-start | bytes 368648 | tf_op jit(solution)/shard_map/ppermute | solution.py:24
  99.4 1.6 %collective-permute-start.23 = (bf16[32,1920]{1,0:T(8,128)(2,1)S(1)}, bf16[32,1920]{1,0:T(8,128)(2,1)S(1)}, u32[]{:S(2)}, u32[]{:S(2)}) collective-permute-start(bf16[32,1920]{1,0:T(8,128)(2,1)S(1)} %collective-permute-done.18.refs_4_), channel_id=1, source_target_pairs={{0,1},{1,0},{2,3},{3,2},{4,5},{5,4},{6,7},{7,6},{8,9},{9,8},{10,11... | collective-permute-start | bytes 368648 | tf_op jit(solution)/shard_map/ppermute | solution.py:24
  99.5 1.5 %collective-permute-start.22 = (bf16[32,1792]{1,0:T(8,128)(2,1)S(1)}, bf16[32,1792]{1,0:T(8,128)(2,1)S(1)}, u32[]{:S(2)}, u32[]{:S(2)}) collective-permute-start(bf16[32,1792]{1,0:T(8,128)(2,1)S(1)} %collective-permute-done.17.refs_3_), channel_id=1, source_target_pairs={{0,1},{1,0},{2,3},{3,2},{4,5},{5,4},{6,7},{7,6},{8,9},{9,8},{10,11... | collective-permute-start | bytes 344072 | tf_op jit(solution)/shard_map/ppermute | solution.py:24
  104.8 2.8 %collective-permute-start.25 = (bf16[32,7168]{1,0:T(8,128)(2,1)S(1)}, bf16[32,7168]{1,0:T(8,128)(2,1)S(1)}, u32[]{:S(2)}, u32[]{:S(2)}) collective-permute-start(bf16[32,7168]{1,0:T(8,128)(2,1)S(1)} %get-tuple-element.97), channel_id=1, source_target_pairs={{0,1},{1,0},{2,3},{3,2},{4,5},{5,4},{6,7},{7,6},{8,9},{9,8},{10,11... | collective-permute-start | bytes 1376264 | tf_op jit(solution)/shard_map/ppermute | solution.py:24
  107.4 3.2 %collective-permute-start.24 = (bf16[96,7168]{1,0:T(8,128)(2,1)S(1)}, bf16[96,7168]{1,0:T(8,128)(2,1)S(1)}, u32[]{:S(2)}, u32[]{:S(2)}) collective-permute-start(bf16[96,7168]{1,0:T(8,128)(2,1)S(1)} %get-tuple-element.95), channel_id=1, source_target_pairs={{0,1},{1,0},{2,3},{3,2},{4,5},{5,4},{6,7},{7,6},{8,9},{9,8},{10,11... | collective-permute-start | bytes 4128776 | tf_op jit(solution)/shard_map/ppermute | solution.py:24
  107.8 9.8 %collective-permute-start.26 = (bf16[32,3584]{1,0:T(8,128)(2,1)S(1)}, bf16[32,3584]{1,0:T(8,128)(2,1)S(1)}, u32[]{:S(2)}, u32[]{:S(2)}) collective-permute-start(bf16[32,3584]{1,0:T(8,128)(2,1)S(1)} %get-tuple-element.104), channel_id=1, source_target_pairs={{0,4},{2,6},{4,0},{6,2},{8,12},{10,14},{12,8},{14,10},{16,20},{18,... | collective-permute-start | bytes 688136 | tf_op jit(solution)/shard_map/ppermute | solution.py:24
  108.7 7.6 %collective-permute-start.28 = (bf16[32,3584]{1,0:T(8,128)(2,1)S(1)}, bf16[32,3584]{1,0:T(8,128)(2,1)S(1)}, u32[]{:S(2)}, u32[]{:S(2)}) collective-permute-start(bf16[32,3584]{1,0:T(8,128)(2,1)S(1)} %get-tuple-element.105), channel_id=1, source_target_pairs={{0,2},{2,0},{4,6},{6,4},{8,10},{10,8},{12,14},{14,12},{16,18},{18,... | collective-permute-start | bytes 688136 | tf_op jit(solution)/shard_map/ppermute | solution.py:24
  116.3 11.7 %collective-permute-start.29 = (bf16[32,7168]{1,0:T(8,128)(2,1)S(1)}, bf16[32,7168]{1,0:T(8,128)(2,1)S(1)}, u32[]{:S(2)}, u32[]{:S(2)}) collective-permute-start(bf16[32,7168]{1,0:T(8,128)(2,1)S(1)} %pad_maximum_fusion.1), channel_id=1, source_target_pairs={{0,4},{2,6},{4,0},{6,2},{8,12},{10,14},{12,8},{14,10},{16,20},{18,... | collective-permute-start | bytes 1376264 | tf_op jit(solution)/shard_map/ppermute | solution.py:24
  117.8 11.4 %collective-permute-start.27 = (bf16[32,7168]{1,0:T(8,128)(2,1)S(1)}, bf16[32,7168]{1,0:T(8,128)(2,1)S(1)}, u32[]{:S(2)}, u32[]{:S(2)}) collective-permute-start(bf16[32,7168]{1,0:T(8,128)(2,1)S(1)} %pad_maximum_fusion), channel_id=1, source_target_pairs={{0,2},{2,0},{4,6},{6,4},{8,10},{10,8},{12,14},{14,12},{16,18},{18,... | collective-permute-start | bytes 1376264 | tf_op jit(solution)/shard_map/ppermute | solution.py:24
  129.4 6.1 %collective-permute-start.30 = (bf16[16,7168]{1,0:T(8,128)(2,1)S(1)}, bf16[16,7168]{1,0:T(8,128)(2,1)S(1)}, u32[]{:S(2)}, u32[]{:S(2)}) collective-permute-start(bf16[16,7168]{1,0:T(8,128)(2,1)S(1)} %split.63), channel_id=1, source_target_pairs={{0,8},{2,10},{4,12},{6,14},{8,0},{10,2},{12,4},{14,6},{16,24},{18,... | collective-permute-start | bytes 688136 | tf_op jit(solution)/shard_map/ppermute | solution.py:24
  135.6 7.0 %collective-permute-start.31 = (bf16[8,7168]{1,0:T(8,128)(2,1)S(1)}, bf16[8,7168]{1,0:T(8,128)(2,1)S(1)}, u32[]{:S(2)}, u32[]{:S(2)}) collective-permute-start(bf16[8,7168]{1,0:T(8,128)(2,1)S(1)} %split.64), channel_id=1, source_target_pairs={{0,16},{2,18},{4,20},{6,22},{8,24},{10,26},{12,28},{14,30},{16,0},... | collective-permute-start | bytes 344072 | tf_op jit(solution)/shard_map/ppermute | solution.py:24
  (8 other events, 68.0 us)

commit v6 on v5

--- a/solution.py
+++ b/solution.py
@@ -185,9 +185,8 @@
     )(values, w_o)
 
 
-def first_kernel(set_count, *refs):
-    flat, refs = refs[: 5 * set_count], refs[5 * set_count :]
-    sets = [flat[5 * n : 5 * n + 5] for n in range(set_count)]
+def first_kernel(piece_count, *refs):
+    pieces, refs = refs[:piece_count], refs[piece_count:]
     w_gate, w_up, gate_acc, up_acc, gate_buf, up_buf, sems = refs
     chunks, size, _ = gate_buf.shape
 
@@ -201,11 +200,8 @@
         for copy in copies_in(n):
             copy.start()
     for n in range(chunks):
-        parts = []
-        for own, near_x, near_y, low, high in sets:
-            parts += [ref[:, n * size : (n + 1) * size] for ref in (own, near_x, near_y)]
-            parts.append((low, high)[n][...])
-        rows = jnp.concatenate(parts, axis=0)
+        columns = slice(n * size, (n + 1) * size)
+        rows = jnp.concatenate([ref[:, columns] for ref in pieces], axis=0)
         for copy in copies_in(n):
             copy.wait()
         gate_part = jnp.dot(rows, gate_buf[n], preferred_element_type=jnp.float32)
@@ -222,10 +218,10 @@
     width, hidden_units = w_gate.shape[1:]
     size = width // CHUNKS
     flat = [piece for pieces in sets for piece in pieces]
-    rows = sum(piece.shape[0] for pieces in sets for piece in pieces[:4])
+    rows = sum(piece.shape[0] for piece in flat)
     sums = jax.ShapeDtypeStruct((rows, hidden_units), jnp.float32)
     return pl.pallas_call(
-        functools.partial(first_kernel, len(sets)),
+        functools.partial(first_kernel, len(flat)),
         out_shape=(sums, sums),
         in_specs=[vmem_spec()] * len(flat) + [hbm_spec()] * 2,
         out_specs=(vmem_spec(), vmem_spec()),
@@ -295,27 +291,19 @@
 
 
 def second_kernel(set_count, *refs):
-    flat, refs = refs[: 5 * set_count], refs[5 * set_count :]
-    sets = [flat[5 * n : 5 * n + 5] for n in range(set_count)]
+    pieces, refs = refs[: 4 * set_count], refs[4 * set_count :]
     mask, gate_first, up_first, w_gate, w_up, w_down = refs[:6]
     near, far, rest, gate_acc, up_acc, act = refs[6:]
     half = w_gate.shape[0]
     size = half // 2
     line = near.shape[0] * 2 // set_count
-    tails = []
-    for own, near_x, near_y, low, high in sets:
-        tails += [ref[:, half:] for ref in (own, near_x, near_y)] + [high[:, size:]]
-    terms = jnp.concatenate(tails, axis=0).astype(jnp.float32)
+    terms = jnp.concatenate([ref[:, half:] for ref in pieces], axis=0).astype(jnp.float32)
     gates = jnp.sum(terms * mask[0:1], axis=1, keepdims=True)
     factors = jnp.sum(terms * mask[1:2], axis=1, keepdims=True)
     for n in range(2):
-        parts = []
-        for own, near_x, near_y, low, high in sets:
-            parts += [ref[:, n * size : (n + 1) * size] for ref in (own, near_x, near_y)]
-            parts.append((low, high)[n][:, :size])
-        rows = jnp.concatenate(parts, axis=0)
+        depth = slice(n * size, (n + 1) * size)
+        rows = jnp.concatenate([ref[:, depth] for ref in pieces], axis=0)
         before = (gate_first, up_first) if n == 0 else (gate_acc, up_acc)
-        depth = slice(n * size, (n + 1) * size)
         gate_acc[...] = before[0][...] + jnp.dot(
             rows, w_gate[depth], preferred_element_type=jnp.float32
         )
@@ -536,7 +524,7 @@
     cached = latent_cache.reshape(replica_rows, CTX, KV)
     arrived = arrivals.reshape(MOVE_MAX, CTX, KV)
     width = residual.shape[1]
-    half, size = width // 2, width // CHUNKS
+    half = width // 2
     tokens = residual.astype(jnp.float32)
 
     part, values = attention_and_first(
@@ -546,17 +534,19 @@
     rows_a = narrow(hidden_a * norm_gain[None, :half])
     values, rows_a = lax.optimization_barrier((values, rows_a))
     inner_x, inner_y, outer = dp_bits()
-    early = half * 2 // 5 // 128 * 128
-    parts_b = [more_columns(values, w_o, half, early)]
+    third = half * 2 // 7 // 128 * 128
+    parts_b = [more_columns(values, w_o, half, third)]
     came, parts_b = lax.optimization_barrier((flip(rows_a, "dp", outer[0]), parts_b))
     held_a = jnp.concatenate([rows_a, came], axis=0)
     values, held_a = lax.optimization_barrier((values, held_a))
-    parts_b.append(more_columns(values, w_o, half + early, half - early))
+    parts_b.append(more_columns(values, w_o, half + third, third))
     for bit in outer[1:]:
         held_a = jnp.concatenate([held_a, flip(held_a, "dp", bit)], axis=0)
-    parts_b, held_a = lax.optimization_barrier((parts_b, held_a))
+    values, parts_b, held_a = lax.optimization_barrier((values, parts_b, held_a))
     x_a = flip(held_a, "dp", inner_x)
     y_a = flip(held_a, "dp", inner_y)
+    parts_b.append(more_columns(values, w_o, half + 2 * third, half - 2 * third))
+    parts_b, x_a, y_a = lax.optimization_barrier((parts_b, x_a, y_a))
 
     hidden_b = tokens[:, half:] + head_sums(jnp.concatenate(parts_b, axis=1))
     squares = jnp.sum(hidden_a * hidden_a, axis=1, keepdims=True) + jnp.sum(
@@ -569,28 +559,24 @@
     terms = three_terms(gate_sum) + three_terms(factor)
     terms.append(jnp.zeros((tokens.shape[0], GATE_COLS - 3 * replicas - 3), jnp.bfloat16))
     rows_b = jnp.concatenate([narrow(hidden_b * norm_gain[None, half:])] + terms, axis=1)
-    held_b = jnp.concatenate([rows_b, flip(rows_b, "dp", outer[0])], axis=0)
-    held_b, x_a, y_a = lax.optimization_barrier((held_b, x_a, y_a))
-    low_a = flip(y_a[:, :size], "dp", inner_x)
-    high_a = flip(x_a[:, size:], "dp", inner_y)
-    for bit in outer[1:]:
-        held_b = jnp.concatenate([held_b, flip(held_b, "dp", bit)], axis=0)
     columns = jnp.arange(GATE_COLS, dtype=jnp.int32)
     gate_mask = (columns < 3 * replicas) & (columns % replicas == own_replica)
     factor_mask = (columns >= 3 * replicas) & (columns < 3 * replicas + 3)
     mask = jnp.stack([gate_mask, factor_mask]).astype(jnp.float32)
-    held_b, low_a, high_a, mask = lax.optimization_barrier((held_b, low_a, high_a, mask))
+    corner_a = flip(y_a, "dp", inner_x)
+    rows_b, mask = lax.optimization_barrier((rows_b, mask))
+    came = flip(rows_b, "dp", outer[0])
+    gate_held, up_held, down_held, mask = hold_weights(mask, w_gate, w_up, w_down)
+    came, corner_a, mask = lax.optimization_barrier((came, corner_a, mask))
+    held_b = jnp.concatenate([rows_b, came], axis=0)
+    for bit in outer[1:]:
+        held_b = jnp.concatenate([held_b, flip(held_b, "dp", bit)], axis=0)
+    sets_a = all_sets((held_a, x_a, y_a, corner_a))
     x_b = flip(held_b, "dp", inner_x)
     y_b = flip(held_b, "dp", inner_y)
-    gate_held, up_held, down_held, mask = hold_weights(mask, w_gate, w_up, w_down)
-    low_a, high_a, mask = lax.optimization_barrier((low_a, high_a, mask))
-    sets_a = all_sets((held_a, x_a, y_a, low_a, high_a))
-    x_b, y_b, sets_a = lax.optimization_barrier((x_b, y_b, sets_a))
-    low_b = flip(y_b[:, :size], "dp", inner_x)
-    high_b = flip(x_b[:, size:], "dp", inner_y)
     sums = experts_first(sets_a, w_gate, w_up)
-    low_b, high_b, sums = lax.optimization_barrier((low_b, high_b, sums))
-    sets_b = all_sets((held_b, x_b, y_b, low_b, high_b))
+    x_b, y_b, sums = lax.optimization_barrier((x_b, y_b, sums))
+    sets_b = all_sets((held_b, x_b, y_b, flip(x_b, "dp", inner_y)))
     near, far, rest = experts_second(sets_b, mask, sums, gate_held, up_held, down_held)
     mixture = scatter_sums((near, far), experts_rest(rest, down_held))
     hidden = jnp.concatenate([hidden_a, hidden_b], axis=1)

time: 144 us -> 140 us (0.972)
  starting transfers between devices: 35.1 us -> 31.9 us
  waiting for transfers between devices: 53.1 us -> 51.1 us
    ppermute x32 -> x28, starting transfers between devices: 23.1 us -> 19.9 us  [flip(): return lax.ppermute(x, axis, pairs)]
    ppermute x32 -> x28, waiting for transfers between devices: 42.1 us -> 40 us  [flip(): return lax.ppermute(x, axis, pairs)]
    pallas_call x2 -> x3, Pallas kernels: 11.8 us -> 12.8 us  [more_columns(): pl.pallas_call(functools.partial(columns_kernel, start), out_shape=jax.Sh...]
  transfers between devices with their start and end apart: 34 -> 30, of which waited for: 20 -> 18; matrix products, arithmetic and copies ran while one was open for 4% -> 4% of each run, Pallas kernels for 16% -> 18%
where the time goes in v6:
time: 140 us
  waiting for transfers between devices  51.1 us (36%)
  Pallas kernels  40.9 us (29%)
  starting transfers between devices  31.9 us (23%)
  local copies, waits for them, and re-layouts  5.71 us (4%)
  other arithmetic  3.68 us (3%)
  matrix products  3.16 us (2%)
  blocking collectives  2.19 us (2%)
    ppermute x28, waiting for transfers between devices, flip(): return lax.ppermute(x, axis, pairs)  40 us
    ppermute x28, starting transfers between devices, flip(): return lax.ppermute(x, axis, pairs)  19.9 us
    pallas_call x3, Pallas kernels, more_columns(): pl.pallas_call(functools.partial(columns_kernel, start), out_shape=jax.Sh...  12.8 us
    pallas_call x1, Pallas kernels, attention_and_first(): pl.pallas_call(attention_kernel, out_shape=(jax.ShapeDtypeStruct((request...  12.4 us
    all_to_all x1, starting transfers between devices, migrate(): met = lax.all_to_all(outbox, 'dp', split_axis=0, concat_axis=0)  8.31 us
    all_to_all x1, waiting for transfers between devices, migrate(): met = lax.all_to_all(outbox, 'dp', split_axis=0, concat_axis=0)  6.88 us
    pallas_call x1, Pallas kernels, hold_weights(): pl.pallas_call(hold_kernel, out_shape=(pltpu.VMEM((half, hidden_units), j...  5.29 us
    pallas_call x1, Pallas kernels, experts_first(): pl.pallas_call(functools.partial(first_kernel, len(flat)), out_shape=(sum...  4.3 us
  transfers between devices with their start and end apart: 30, of which 18 were waited for; matrix products, arithmetic and copies ran while one was open for 4% of the time, Pallas kernels for 18%

profile of v6, /device:TPU:0, one launch (start us, length us, event | category | flops | bytes accessed | tf_op | source)
XLA Modules:
  0.0 139.7 jit_solution(11243360707184184579)
XLA Ops:
  2.3 2.0 %convolution_convert_fusion = bf16[4,18432]{1,0:T(4,128)(2,1)} fusion(bf16[16,36864]{1,0:T(8,128)(2,1)} %param.15, s32[]{:T(128)S(6)} %select_n.69, pred[64,256]{1,0:T(8,128)(4,1)S(1)} %iota_compare_fusion.4, s32[]{:T(128)S(6)} %select_n.67, s32[]{:T(128)S(6)} %select_n.68), kind=kOutput, calls=%fused_computation | convolution fusion | flops 2433024 | bytes 737804 | tf_op jit(solution)/shard_map/dot_general | solution.py:414
  4.3 8.3 %all-to-all-start = ((bf16[16,4,1152]{2,1,0:T(4,128)(2,1)}), bf16[16,4,1152]{2,1,0:T(4,128)(2,1)S(1)}, u32[]{:S(2)}, u32[]{:S(2)}) async-start(bf16[16,4,1152]{2,1,0:T(4,128)(2,1)} %bitcast.1), calls=%async_computation | async-start | bytes 294912 | tf_op jit(solution)/shard_map/all_to_all | solution.py:416
  13.6 6.9 %all-to-all-done = bf16[16,4,1152]{2,1,0:T(4,128)(2,1)S(1)} async-done(((bf16[16,4,1152]{2,1,0:T(4,128)(2,1)}), bf16[16,4,1152]{2,1,0:T(4,128)(2,1)S(1)}, u32[]{:S(2)}, u32[]{:S(2)}) %all-to-all-start) | async-done | bytes 147488 | tf_op jit(solution)/shard_map/all_to_all | solution.py:416
  21.4 3.6 %all-to-all-start.1 = ((bf16[16,4,1152]{2,1,0:T(4,128)(2,1)}), bf16[16,4,1152]{2,1,0:T(4,128)(2,1)S(1)}, u32[]{:S(2)}, u32[]{:S(2)}) async-start(bf16[16,4,1152]{2,1,0:T(4,128)(2,1)} %reshape.194), calls=%async_computation.1 | async-start | bytes 294912 | tf_op jit(solution)/shard_map/all_to_all | solution.py:420
  25.2 1.6 %reshape.191.cached = bf16[16,64,576]{2,1,0:T(8,128)(2,1)S(1)} reshape(bf16[16,36864]{1,0:T(8,128)(2,1)S(1)} %copy-done.1) | data formatting | bytes 2359296 | tf_op jit(solution)/shard_map/reshape | solution.py:524
  26.9 1.8 %reshape.190.queries = bf16[16,32,576]{2,1,0:T(8,128)(2,1)S(1)} reshape(bf16[16,18432]{1,0:T(8,128)(2,1)} %param.14) | data formatting | bytes 1179648 | tf_op jit(solution)/shard_map/reshape | solution.py:523
  28.7 4.2 %all-to-all-done.1 = bf16[16,4,1152]{2,1,0:T(4,128)(2,1)S(1)} async-done(((bf16[16,4,1152]{2,1,0:T(4,128)(2,1)}), bf16[16,4,1152]{2,1,0:T(4,128)(2,1)S(1)}, u32[]{:S(2)}, u32[]{:S(2)}) %all-to-all-start.1) | async-done | bytes 147488 | tf_op jit(solution)/shard_map/all_to_all | solution.py:420
  32.9 2.2 %all_gather.3 = bf16[4,36864]{1,0:T(4,128)(2,1)S(1)} all-gather(bf16[4,18432]{1,0:T(4,128)(2,1)S(1)} %bitcast.10), channel_id=1, replica_groups=mesh['dp'=16,'ep'=2] {'ep'}, dimensions={1}, use_global_device_ids=true | all-gather | bytes 442368 | tf_op jit(solution)/shard_map/all_gather | solution.py:424
  35.5 12.4 %attention_and_first.1 = (f32[16,3584]{1,0:T(8,128)S(1)}, bf16[16,4096]{1,0:T(8,128)(2,1)S(1)}) custom-call(s32[16]{0:T(128)S(1)} %convert_add_fusion.3.moved, s32[16]{0:T(128)S(1)} %copy-done, bf16[16,32,576]{2,1,0:T(8,128)(2,1)S(1)} %reshape.190.queries, bf16[16,64,576]{2,1,0:T(8,128)(2,1)S(1)} %reshape.191.cached, ...), custom_call_target="tpu_custom_call" | custom-call | flops 536870912 | bytes 33554432 | tf_op jit(solution)/shard_map/attention_and_first/pallas_call | solution.py:119
  48.2 1.2 collective-permute-done
  50.6 3.8 %more_columns.3 = f32[16,1024]{1,0:T(8,128)S(1)} custom-call(bf16[16,4096]{1,0:T(8,128)(2,1)S(1)} %get-tuple-element.49.values, bf16[4096,7168]{1,0:T(8,128)(2,1)} %w_o.7), custom_call_target="tpu_custom_call" | custom-call | flops 134217728 | bytes 8388608 | tf_op jit(solution)/shard_map/more_columns/pallas_call | solution.py:171
  54.3 1.4 collective-permute-done.1
  55.9 3.8 %more_columns.4 = f32[16,1024]{1,0:T(8,128)S(1)} custom-call(bf16[16,4096]{1,0:T(8,128)(2,1)S(1)} %get-tuple-element.49.values, bf16[4096,7168]{1,0:T(8,128)(2,1)} %w_o.7), custom_call_target="tpu_custom_call" | custom-call | flops 134217728 | bytes 8388608 | tf_op jit(solution)/shard_map/more_columns/pallas_call | solution.py:171
  62.1 5.3 %more_columns.5 = f32[16,1536]{1,0:T(8,128)S(1)} custom-call(bf16[16,4096]{1,0:T(8,128)(2,1)S(1)} %get-tuple-element.49.values, bf16[4096,7168]{1,0:T(8,128)(2,1)} %w_o.7), custom_call_target="tpu_custom_call" | custom-call | flops 201326592 | bytes 12582912 | tf_op jit(solution)/shard_map/more_columns/pallas_call | solution.py:171
  68.4 1.2 collective-permute-start.7
  71.1 5.3 %hold_weights.1 = (bf16[3584,512]{1,0:T(8,128)(2,1)S(1)}, bf16[3584,512]{1,0:T(8,128)(2,1)S(1)}, bf16[512,7168]{1,0:T(8,128)(2,1)S(1)}, f32[2,128]{1,0:T(2,128)S(1)}) custom-call(f32[2,128]{1,0:T(2,128)S(1)} %add_convert_fusion.1.after, bf16[1,7168,512]{2,1,0:T(8,128)(2,1)} %refs_8_.1, bf16[1,7168,512]{2,1,0:T(8,128)(2,1)} %refs_9_.1, ...), custom_call_target="tpu_custom_call" | custom-call | bytes 14680064 | tf_op jit(solution)/shard_map/hold_weights/pallas_call | solution.py:270
  76.6 1.5 %collective-permute-start.8 = (bf16[16,3712]{1,0:T(8,128)(2,1)S(1)}, bf16[16,3712]{1,0:T(8,128)(2,1)S(1)}, u32[]{:S(2)}, u32[]{:S(2)}) collective-permute-start(bf16[16,3712]{1,0:T(8,128)(2,1)S(1)} %pad_maximum_fusion.3), channel_id=1, source_target_pairs={{0,8},{2,10},{4,12},{6,14},{8,0},{10,2},{12,4},{14,6},{16,24},{18,... | collective-permute-start | bytes 356360 | tf_op jit(solution)/shard_map/ppermute | solution.py:24
  78.1 3.5 %collective-permute-done.8 = bf16[16,3712]{1,0:T(8,128)(2,1)S(1)} collective-permute-done((bf16[16,3712]{1,0:T(8,128)(2,1)S(1)}, bf16[16,3712]{1,0:T(8,128)(2,1)S(1)}, u32[]{:S(2)}, u32[]{:S(2)}) %collective-permute-start.8) | collective-permute-done | bytes 118816 | tf_op jit(solution)/shard_map/ppermute | solution.py:24
  81.7 1.3 collective-permute-start.10
  84.1 4.3 %experts_first.1 = (f32[256,512]{1,0:T(8,128)S(1)}, f32[256,512]{1,0:T(8,128)S(1)}) custom-call(bf16[32,3584]{1,0:T(8,128)(2,1)S(1)} %pad_maximum_fusion.2.refs_0_, bf16[32,3584]{1,0:T(8,128)(2,1)S(1)} %collective-permute-done.3.refs_1_, bf16[32,3584]{1,0:T(8,128)(2,1)S(1)} %collective-permute-done.4.refs_2_, ...), custom_call_target="tpu_custom_call" | custom-call | flops 1879048192 | bytes 9175040 | tf_op jit(solution)/shard_map/experts_first/pallas_call | solution.py:223
  90.8 4.8 %collective-permute-done.15.refs_3_ = bf16[32,3712]{1,0:T(8,128)(2,1)S(1)} collective-permute-done((bf16[32,3712]{1,0:T(8,128)(2,1)S(1)}, bf16[32,3712]{1,0:T(8,128)(2,1)S(1)}, u32[]{:S(2)}, u32[]{:S(2)}) %collective-permute-start.15) | collective-permute-done | bytes 237600 | tf_op jit(solution)/shard_map/ppermute | solution.py:24
  95.6 1.5 %collective-permute-done.19.refs_7_ = bf16[32,3712]{1,0:T(8,128)(2,1)S(1)} collective-permute-done((bf16[32,3712]{1,0:T(8,128)(2,1)S(1)}, bf16[32,3712]{1,0:T(8,128)(2,1)S(1)}, u32[]{:S(2)}, u32[]{:S(2)}) %collective-permute-start.19) | collective-permute-done | bytes 237600 | tf_op jit(solution)/shard_map/ppermute | solution.py:24
  97.1 3.9 %experts_second.1 = (bf16[32,7168]{1,0:T(8,128)(2,1)S(1)}, bf16[32,7168]{1,0:T(8,128)(2,1)S(1)}, bf16[192,512]{1,0:T(8,128)(2,1)S(1)}) custom-call(bf16[32,3712]{1,0:T(8,128)(2,1)S(1)} %constant_dynamic-update-slice_fusion.3.refs_0_, bf16[32,3712]{1,0:T(8,128)(2,1)S(1)} %collective-permute-done.9.refs_1_, ...), custom_call_target="tpu_custom_call" | custom-call | flops 2818572288 | bytes 3670016 | tf_op jit(solution)/shard_map/experts_second/pallas_call | solution.py:336
  101.2 2.2 %experts_rest.1 = (bf16[96,7168]{1,0:T(8,128)(2,1)S(1)}, bf16[96,7168]{1,0:T(8,128)(2,1)S(1)}) custom-call(bf16[192,512]{1,0:T(8,128)(2,1)S(1)} %get-tuple-element.71.rest, bf16[512,7168]{1,0:T(8,128)(2,1)S(1)} %get-tuple-element.70.refs_13_.w_down), custom_call_target="tpu_custom_call" | custom-call | flops 1409286144 | bytes 2752512 | tf_op jit(solution)/shard_map/experts_rest/pallas_call | solution.py:376
  106.8 5.4 %collective-permute-done.24 = bf16[32,3584]{1,0:T(8,128)(2,1)S(1)} collective-permute-done((bf16[32,3584]{1,0:T(8,128)(2,1)S(1)}, bf16[32,3584]{1,0:T(8,128)(2,1)S(1)}, u32[]{:S(2)}, u32[]{:S(2)}) %collective-permute-start.24) | collective-permute-done | bytes 229408 | tf_op jit(solution)/shard_map/ppermute | solution.py:24
  112.3 1.3 collective-permute-start.25
  114.8 9.0 %collective-permute-done.25 = bf16[32,7168]{1,0:T(8,128)(2,1)S(1)} collective-permute-done((bf16[32,7168]{1,0:T(8,128)(2,1)S(1)}, bf16[32,7168]{1,0:T(8,128)(2,1)S(1)}, u32[]{:S(2)}, u32[]{:S(2)}) %collective-permute-start.25) | collective-permute-done | bytes 458784 | tf_op jit(solution)/shard_map/ppermute | solution.py:24
  123.8 1.1 collective-permute-done.23
  125.1 1.4 collective-permute-start.26
  126.5 4.7 %collective-permute-done.26 = bf16[16,7168]{1,0:T(8,128)(2,1)S(1)} collective-permute-done((bf16[16,7168]{1,0:T(8,128)(2,1)S(1)}, bf16[16,7168]{1,0:T(8,128)(2,1)S(1)}, u32[]{:S(2)}, u32[]{:S(2)}) %collective-permute-start.26) | collective-permute-done | bytes 229408 | tf_op jit(solution)/shard_map/ppermute | solution.py:24
  131.3 3.0 %collective-permute-start.27 = (bf16[8,7168]{1,0:T(8,128)(2,1)S(1)}, bf16[8,7168]{1,0:T(8,128)(2,1)S(1)}, u32[]{:S(2)}, u32[]{:S(2)}) collective-permute-start(bf16[8,7168]{1,0:T(8,128)(2,1)S(1)} %split.64), channel_id=1, source_target_pairs={{0,16},{2,18},{4,20},{6,22},{8,24},{10,26},{12,28},{14,30},{16,0},... | collective-permute-start | bytes 344072 | tf_op jit(solution)/shard_map/ppermute | solution.py:24
  134.3 4.0 %collective-permute-done.27 = bf16[8,7168]{1,0:T(8,128)(2,1)S(1)} collective-permute-done((bf16[8,7168]{1,0:T(8,128)(2,1)S(1)}, bf16[8,7168]{1,0:T(8,128)(2,1)S(1)}, u32[]{:S(2)}, u32[]{:S(2)}) %collective-permute-start.27) | collective-permute-done | bytes 114720 | tf_op jit(solution)/shard_map/ppermute | solution.py:24
  (106 shorter events, 20.7 us)
Async XLA Ops:
  0.6 24.6 %copy-start.1 = (bf16[16,36864]{1,0:T(8,128)(2,1)S(1)}, bf16[16,36864]{1,0:T(8,128)(2,1)}, u32[]{:S(2)}) copy-start(bf16[16,36864]{1,0:T(8,128)(2,1)} %param.15) | copy-start | bytes 3538948
  4.3 16.2 %all-to-all-start = ((bf16[16,4,1152]{2,1,0:T(4,128)(2,1)}), bf16[16,4,1152]{2,1,0:T(4,128)(2,1)S(1)}, u32[]{:S(2)}, u32[]{:S(2)}) async-start(bf16[16,4,1152]{2,1,0:T(4,128)(2,1)} %bitcast.1), calls=%async_computation | async-start | bytes 294912 | tf_op jit(solution)/shard_map/all_to_all | solution.py:416
  21.4 11.5 %all-to-all-start.1 = ((bf16[16,4,1152]{2,1,0:T(4,128)(2,1)}), bf16[16,4,1152]{2,1,0:T(4,128)(2,1)S(1)}, u32[]{:S(2)}, u32[]{:S(2)}) async-start(bf16[16,4,1152]{2,1,0:T(4,128)(2,1)} %reshape.194), calls=%async_computation.1 | async-start | bytes 294912 | tf_op jit(solution)/shard_map/all_to_all | solution.py:420
  35.5 12.7 %copy-start.3 = (f32[7168]{0:T(1024)S(1)}, f32[7168]{0:T(1024)}, u32[]{:S(2)}) copy-start(f32[7168]{0:T(1024)} %param.20) | copy-start | bytes 86020
  48.0 1.4 collective-permute-start
  49.5 6.2 %collective-permute-start.1 = (bf16[8,3584]{1,0:T(8,128)(2,1)S(1)}, bf16[8,3584]{1,0:T(8,128)(2,1)S(1)}, u32[]{:S(2)}, u32[]{:S(2)}) collective-permute-start(bf16[8,3584]{1,0:T(8,128)(2,1)S(1)} %multiply_convert_fusion.1), channel_id=1, source_target_pairs={{0,16},{2,18},{4,20},{6,22},{8,24},{10,26},{12,28},{14,30},{16,0},... | collective-permute-start | bytes 172040 | tf_op jit(solution)/shard_map/ppermute | solution.py:24
  55.7 4.9 %collective-permute-start.2 = (bf16[16,3584]{1,0:T(8,128)(2,1)S(1)}, bf16[16,3584]{1,0:T(8,128)(2,1)S(1)}, u32[]{:S(2)}, u32[]{:S(2)}) collective-permute-start(bf16[16,3584]{1,0:T(8,128)(2,1)S(1)} %pad_maximum_fusion.4), channel_id=1, source_target_pairs={{0,8},{2,10},{4,12},{6,14},{8,0},{10,2},{12,4},{14,6},{16,24},{18,... | collective-permute-start | bytes 344072 | tf_op jit(solution)/shard_map/ppermute | solution.py:24
  60.7 6.7 %collective-permute-start.4 = (bf16[32,3584]{1,0:T(8,128)(2,1)S(1)}, bf16[32,3584]{1,0:T(8,128)(2,1)S(1)}, u32[]{:S(2)}, u32[]{:S(2)}) collective-permute-start(bf16[32,3584]{1,0:T(8,128)(2,1)S(1)} %pad_maximum_fusion.2.refs_0_), channel_id=1, source_target_pairs={{0,4},{2,6},{4,0},{6,2},{8,12},{10,14},{12,8},{14,10},{16,20},{18,... | collective-permute-start | bytes 688136 | tf_op jit(solution)/shard_map/ppermute | solution.py:24
  61.5 6.2 %collective-permute-start.3 = (bf16[32,3584]{1,0:T(8,128)(2,1)S(1)}, bf16[32,3584]{1,0:T(8,128)(2,1)S(1)}, u32[]{:S(2)}, u32[]{:S(2)}) collective-permute-start(bf16[32,3584]{1,0:T(8,128)(2,1)S(1)} %pad_maximum_fusion.2.refs_0_), channel_id=1, source_target_pairs={{0,2},{2,0},{4,6},{6,4},{8,10},{10,8},{12,14},{14,12},{16,18},{18,... | collective-permute-start | bytes 688136 | tf_op jit(solution)/shard_map/ppermute | solution.py:24
  67.7 2.1 %collective-permute-start.5 = (f32[8,3584]{1,0:T(8,128)S(1)}, f32[8,3584]{1,0:T(8,128)S(1)}, u32[]{:S(2)}, u32[]{:S(2)}) collective-permute-start(f32[8,3584]{1,0:T(8,128)S(1)} %constant_dynamic-slice_fusion), channel_id=1, source_target_pairs={{0,1},{1,0},{2,3},{3,2},{4,5},{5,4},{6,7},{7,6},{8,9},{9,8},{10,11... | collective-permute-start | bytes 344072 | tf_op jit(solution)/shard_map/ppermute | solution.py:24
  67.8 15.2 %collective-permute-start.11 = (bf16[32,3584]{1,0:T(8,128)(2,1)S(1)}, bf16[32,3584]{1,0:T(8,128)(2,1)S(1)}, u32[]{:S(2)}, u32[]{:S(2)}) collective-permute-start(bf16[32,3584]{1,0:T(8,128)(2,1)S(1)} %pad_maximum_fusion.2.refs_0_), channel_id=1, source_target_pairs={{0,1},{1,0},{2,3},{3,2},{4,5},{5,4},{6,7},{7,6},{8,9},{9,8},{10,11... | collective-permute-start | bytes 688136 | tf_op jit(solution)/shard_map/ppermute | solution.py:24
  68.4 15.7 %collective-permute-start.13 = (bf16[32,3584]{1,0:T(8,128)(2,1)S(1)}, bf16[32,3584]{1,0:T(8,128)(2,1)S(1)}, u32[]{:S(2)}, u32[]{:S(2)}) collective-permute-start(bf16[32,3584]{1,0:T(8,128)(2,1)S(1)} %collective-permute-done.4.refs_2_), channel_id=1, source_target_pairs={{0,1},{1,0},{2,3},{3,2},{4,5},{5,4},{6,7},{7,6},{8,9},{9,8},{10,11... | collective-permute-start | bytes 688136 | tf_op jit(solution)/shard_map/ppermute | solution.py:24
  68.4 8.1 %collective-permute-start.7 = (bf16[32,3584]{1,0:T(8,128)(2,1)S(1)}, bf16[32,3584]{1,0:T(8,128)(2,1)S(1)}, u32[]{:S(2)}, u32[]{:S(2)}) collective-permute-start(bf16[32,3584]{1,0:T(8,128)(2,1)S(1)} %collective-permute-done.4.refs_2_), channel_id=1, source_target_pairs={{0,2},{2,0},{4,6},{6,4},{8,10},{10,8},{12,14},{14,12},{16,18},{18,... | collective-permute-start | bytes 688136 | tf_op jit(solution)/shard_map/ppermute | solution.py:24
  69.6 14.4 %collective-permute-start.12 = (bf16[32,3584]{1,0:T(8,128)(2,1)S(1)}, bf16[32,3584]{1,0:T(8,128)(2,1)S(1)}, u32[]{:S(2)}, u32[]{:S(2)}) collective-permute-start(bf16[32,3584]{1,0:T(8,128)(2,1)S(1)} %collective-permute-done.3.refs_1_), channel_id=1, source_target_pairs={{0,1},{1,0},{2,3},{3,2},{4,5},{5,4},{6,7},{7,6},{8,9},{9,8},{10,11... | collective-permute-start | bytes 688136 | tf_op jit(solution)/shard_map/ppermute | solution.py:24
  70.2 6.4 %collective-permute-start.6 = (bf16[8,3712]{1,0:T(8,128)(2,1)S(1)}, bf16[8,3712]{1,0:T(8,128)(2,1)S(1)}, u32[]{:S(2)}, u32[]{:S(2)}) collective-permute-start(bf16[8,3712]{1,0:T(8,128)(2,1)S(1)} %concatenate.34), channel_id=1, source_target_pairs={{0,16},{2,18},{4,20},{6,22},{8,24},{10,26},{12,28},{14,30},{16,0},... | collective-permute-start | bytes 178184 | tf_op jit(solution)/shard_map/ppermute | solution.py:24
  76.6 5.1 %collective-permute-start.8 = (bf16[16,3712]{1,0:T(8,128)(2,1)S(1)}, bf16[16,3712]{1,0:T(8,128)(2,1)S(1)}, u32[]{:S(2)}, u32[]{:S(2)}) collective-permute-start(bf16[16,3712]{1,0:T(8,128)(2,1)S(1)} %pad_maximum_fusion.3), channel_id=1, source_target_pairs={{0,8},{2,10},{4,12},{6,14},{8,0},{10,2},{12,4},{14,6},{16,24},{18,... | collective-permute-start | bytes 356360 | tf_op jit(solution)/shard_map/ppermute | solution.py:24
  78.1 5.9 %collective-permute-start.14 = (bf16[32,3584]{1,0:T(8,128)(2,1)S(1)}, bf16[32,3584]{1,0:T(8,128)(2,1)S(1)}, u32[]{:S(2)}, u32[]{:S(2)}) collective-permute-start(bf16[32,3584]{1,0:T(8,128)(2,1)S(1)} %collective-permute-done.7.refs_3_), channel_id=1, source_target_pairs={{0,1},{1,0},{2,3},{3,2},{4,5},{5,4},{6,7},{7,6},{8,9},{9,8},{10,11... | collective-permute-start | bytes 688136 | tf_op jit(solution)/shard_map/ppermute | solution.py:24
  81.7 6.8 %collective-permute-start.10 = (bf16[32,3712]{1,0:T(8,128)(2,1)S(1)}, bf16[32,3712]{1,0:T(8,128)(2,1)S(1)}, u32[]{:S(2)}, u32[]{:S(2)}) collective-permute-start(bf16[32,3712]{1,0:T(8,128)(2,1)S(1)} %constant_dynamic-update-slice_fusion.3.refs_0_), channel_id=1, source_target_pairs={{0,4},{2,6},{4,0},{6,2},{8,12},{10,14},{12,8},{14,10},{16,20},{18,... | collective-permute-start | bytes 712712 | tf_op jit(solution)/shard_map/ppermute | solution.py:24
  83.0 6.4 %collective-permute-start.9 = (bf16[32,3712]{1,0:T(8,128)(2,1)S(1)}, bf16[32,3712]{1,0:T(8,128)(2,1)S(1)}, u32[]{:S(2)}, u32[]{:S(2)}) collective-permute-start(bf16[32,3712]{1,0:T(8,128)(2,1)S(1)} %constant_dynamic-update-slice_fusion.3.refs_0_), channel_id=1, source_target_pairs={{0,2},{2,0},{4,6},{6,4},{8,10},{10,8},{12,14},{14,12},{16,18},{18,... | collective-permute-start | bytes 712712 | tf_op jit(solution)/shard_map/ppermute | solution.py:24
  89.5 6.1 %collective-permute-start.15 = (bf16[32,3712]{1,0:T(8,128)(2,1)S(1)}, bf16[32,3712]{1,0:T(8,128)(2,1)S(1)}, u32[]{:S(2)}, u32[]{:S(2)}) collective-permute-start(bf16[32,3712]{1,0:T(8,128)(2,1)S(1)} %collective-permute-done.9.refs_1_), channel_id=1, source_target_pairs={{0,4},{2,6},{4,0},{6,2},{8,12},{10,14},{12,8},{14,10},{16,20},{18,... | collective-permute-start | bytes 712712 | tf_op jit(solution)/shard_map/ppermute | solution.py:24
  90.2 5.4 %collective-permute-start.16 = (bf16[32,3712]{1,0:T(8,128)(2,1)S(1)}, bf16[32,3712]{1,0:T(8,128)(2,1)S(1)}, u32[]{:S(2)}, u32[]{:S(2)}) collective-permute-start(bf16[32,3712]{1,0:T(8,128)(2,1)S(1)} %constant_dynamic-update-slice_fusion.3.refs_0_), channel_id=1, source_target_pairs={{0,1},{1,0},{2,3},{3,2},{4,5},{5,4},{6,7},{7,6},{8,9},{9,8},{10,11... | collective-permute-start | bytes 712712 | tf_op jit(solution)/shard_map/ppermute | solution.py:24
  90.2 5.4 %collective-permute-start.17 = (bf16[32,3712]{1,0:T(8,128)(2,1)S(1)}, bf16[32,3712]{1,0:T(8,128)(2,1)S(1)}, u32[]{:S(2)}, u32[]{:S(2)}) collective-permute-start(bf16[32,3712]{1,0:T(8,128)(2,1)S(1)} %collective-permute-done.9.refs_1_), channel_id=1, source_target_pairs={{0,1},{1,0},{2,3},{3,2},{4,5},{5,4},{6,7},{7,6},{8,9},{9,8},{10,11... | collective-permute-start | bytes 712712 | tf_op jit(solution)/shard_map/ppermute | solution.py:24
  90.7 4.8 %collective-permute-start.18 = (bf16[32,3712]{1,0:T(8,128)(2,1)S(1)}, bf16[32,3712]{1,0:T(8,128)(2,1)S(1)}, u32[]{:S(2)}, u32[]{:S(2)}) collective-permute-start(bf16[32,3712]{1,0:T(8,128)(2,1)S(1)} %collective-permute-done.10.refs_2_), channel_id=1, source_target_pairs={{0,1},{1,0},{2,3},{3,2},{4,5},{5,4},{6,7},{7,6},{8,9},{9,8},{10,11... | collective-permute-start | bytes 712712 | tf_op jit(solution)/shard_map/ppermute | solution.py:24
  95.6 1.5 %collective-permute-start.19 = (bf16[32,3712]{1,0:T(8,128)(2,1)S(1)}, bf16[32,3712]{1,0:T(8,128)(2,1)S(1)}, u32[]{:S(2)}, u32[]{:S(2)}) collective-permute-start(bf16[32,3712]{1,0:T(8,128)(2,1)S(1)} %collective-permute-done.15.refs_3_), channel_id=1, source_target_pairs={{0,1},{1,0},{2,3},{3,2},{4,5},{5,4},{6,7},{7,6},{8,9},{9,8},{10,11... | collective-permute-start | bytes 712712 | tf_op jit(solution)/shard_map/ppermute | solution.py:24
  101.0 2.8 %collective-permute-start.21 = (bf16[32,7168]{1,0:T(8,128)(2,1)S(1)}, bf16[32,7168]{1,0:T(8,128)(2,1)S(1)}, u32[]{:S(2)}, u32[]{:S(2)}) collective-permute-start(bf16[32,7168]{1,0:T(8,128)(2,1)S(1)} %get-tuple-element.75), channel_id=1, source_target_pairs={{0,1},{1,0},{2,3},{3,2},{4,5},{5,4},{6,7},{7,6},{8,9},{9,8},{10,11... | collective-permute-start | bytes 1376264 | tf_op jit(solution)/shard_map/ppermute | solution.py:24
  103.4 3.2 %collective-permute-start.20 = (bf16[96,7168]{1,0:T(8,128)(2,1)S(1)}, bf16[96,7168]{1,0:T(8,128)(2,1)S(1)}, u32[]{:S(2)}, u32[]{:S(2)}) collective-permute-start(bf16[96,7168]{1,0:T(8,128)(2,1)S(1)} %get-tuple-element.73), channel_id=1, source_target_pairs={{0,1},{1,0},{2,3},{3,2},{4,5},{5,4},{6,7},{7,6},{8,9},{9,8},{10,11... | collective-permute-start | bytes 4128776 | tf_op jit(solution)/shard_map/ppermute | solution.py:24
  104.0 9.6 %collective-permute-start.22 = (bf16[32,3584]{1,0:T(8,128)(2,1)S(1)}, bf16[32,3584]{1,0:T(8,128)(2,1)S(1)}, u32[]{:S(2)}, u32[]{:S(2)}) collective-permute-start(bf16[32,3584]{1,0:T(8,128)(2,1)S(1)} %get-tuple-element.82), channel_id=1, source_target_pairs={{0,4},{2,6},{4,0},{6,2},{8,12},{10,14},{12,8},{14,10},{16,20},{18,... | collective-permute-start | bytes 688136 | tf_op jit(solution)/shard_map/ppermute | solution.py:24
  104.8 7.4 %collective-permute-start.24 = (bf16[32,3584]{1,0:T(8,128)(2,1)S(1)}, bf16[32,3584]{1,0:T(8,128)(2,1)S(1)}, u32[]{:S(2)}, u32[]{:S(2)}) collective-permute-start(bf16[32,3584]{1,0:T(8,128)(2,1)S(1)} %get-tuple-element.83), channel_id=1, source_target_pairs={{0,2},{2,0},{4,6},{6,4},{8,10},{10,8},{12,14},{14,12},{16,18},{18,... | collective-permute-start | bytes 688136 | tf_op jit(solution)/shard_map/ppermute | solution.py:24
  112.3 11.5 %collective-permute-start.25 = (bf16[32,7168]{1,0:T(8,128)(2,1)S(1)}, bf16[32,7168]{1,0:T(8,128)(2,1)S(1)}, u32[]{:S(2)}, u32[]{:S(2)}) collective-permute-start(bf16[32,7168]{1,0:T(8,128)(2,1)S(1)} %pad_maximum_fusion.1), channel_id=1, source_target_pairs={{0,4},{2,6},{4,0},{6,2},{8,12},{10,14},{12,8},{14,10},{16,20},{18,... | collective-permute-start | bytes 1376264 | tf_op jit(solution)/shard_map/ppermute | solution.py:24
  113.7 11.2 %collective-permute-start.23 = (bf16[32,7168]{1,0:T(8,128)(2,1)S(1)}, bf16[32,7168]{1,0:T(8,128)(2,1)S(1)}, u32[]{:S(2)}, u32[]{:S(2)}) collective-permute-start(bf16[32,7168]{1,0:T(8,128)(2,1)S(1)} %pad_maximum_fusion), channel_id=1, source_target_pairs={{0,2},{2,0},{4,6},{6,4},{8,10},{10,8},{12,14},{14,12},{16,18},{18,... | collective-permute-start | bytes 1376264 | tf_op jit(solution)/shard_map/ppermute | solution.py:24
  125.1 6.1 %collective-permute-start.26 = (bf16[16,7168]{1,0:T(8,128)(2,1)S(1)}, bf16[16,7168]{1,0:T(8,128)(2,1)S(1)}, u32[]{:S(2)}, u32[]{:S(2)}) collective-permute-start(bf16[16,7168]{1,0:T(8,128)(2,1)S(1)} %split.63), channel_id=1, source_target_pairs={{0,8},{2,10},{4,12},{6,14},{8,0},{10,2},{12,4},{14,6},{16,24},{18,... | collective-permute-start | bytes 688136 | tf_op jit(solution)/shard_map/ppermute | solution.py:24
  131.3 7.0 %collective-permute-start.27 = (bf16[8,7168]{1,0:T(8,128)(2,1)S(1)}, bf16[8,7168]{1,0:T(8,128)(2,1)S(1)}, u32[]{:S(2)}, u32[]{:S(2)}) collective-permute-start(bf16[8,7168]{1,0:T(8,128)(2,1)S(1)} %split.64), channel_id=1, source_target_pairs={{0,16},{2,18},{4,20},{6,22},{8,24},{10,26},{12,28},{14,30},{16,0},... | collective-permute-start | bytes 344072 | tf_op jit(solution)/shard_map/ppermute | solution.py:24
  (4 other events, 26.6 us)

commit v7 on v6

--- a/solution.py
+++ b/solution.py
@@ -30,6 +30,7 @@
 
 
 CHUNKS = 4
+OUTER_FIRST = 0.125
 IN_FLIGHT = 10 << 20
 
 
@@ -402,7 +403,7 @@
     picker = lax.dot_general(
         target, to_box, (((1,), (1,)), ((), ())), preferred_element_type=jnp.float32
     ).astype(jnp.bfloat16)
-    return to_box, picker
+    return picker
 
 
 def migrate(packing, picker, latent_cache):
@@ -453,23 +454,43 @@
     return near, came
 
 
+def outer_sums(lines, bits):
+    for bit in bits:
+        mine, other = jnp.split(lines, 2, axis=1)
+        lines = mine + plus(flip(narrow(other), "dp", bit))
+    return lines
+
+
 def scatter_sums(corner, rest):
     inner_x, inner_y, outer = dp_bits()
-    half = corner[0].shape[1] // 2
-    diagonal = narrow(plus(*ep_sums(*corner)))
+    longest, *nearer = outer
+    nearer = nearer[::-1]
+    width = corner[0].shape[1]
+    main = width - int(width * OUTER_FIRST) // 128 * 128
+    half = main // 2 // 128 * 128
+    corner = ep_sums(*corner)
+    diagonal = narrow(plus(*(term[:, :main] for term in corner)))
     low = flip(diagonal[:, :half], "dp", inner_x)
     high = flip(diagonal[:, half:], "dp", inner_y)
-    own, to_x, to_y = zip(*(jnp.split(term, 3, axis=0) for term in ep_sums(*rest)))
-    to_x, to_y = plus(*to_x), plus(*to_y)
+    rest = [jnp.split(term, 3, axis=0) for term in ep_sums(*rest)]
+
+    lines = [plus(*(term[n][:, main:] for term in rest)) for n in range(3)]
+    lines.append(plus(*(term[:, main:] for term in corner)))
+    lines = outer_sums(jnp.stack(lines), nearer)
+
+    own, to_x, to_y = (plus(*(term[n][:, :main] for term in rest)) for n in range(3))
     to_x = narrow(jnp.concatenate([to_x[:, :half], to_x[:, half:] + plus(high)], axis=1))
     to_y = narrow(jnp.concatenate([to_y[:, :half] + plus(low), to_y[:, half:]], axis=1))
     from_x = flip(to_x, "dp", inner_x)
     from_y = flip(to_y, "dp", inner_y)
-    total = plus(*own, from_x, from_y)
-    for bit in outer[::-1]:
-        mine, other = jnp.split(total, 2, axis=0)
-        total = mine + plus(flip(narrow(other), "dp", bit))
-    return total
+    first = outer_sums(plus(own, from_x, from_y)[None], nearer)[0]
+
+    own, to_x, to_y, far = lines
+    to_y = to_y + plus(flip(narrow(far), "dp", inner_x))
+    from_x = flip(narrow(to_x), "dp", inner_x)
+    from_y = flip(narrow(to_y), "dp", inner_y)
+    last = own + plus(from_x, from_y)
+    return outer_sums(jnp.concatenate([first, last], axis=1)[None], [longest])[0]
 
 
 def head_sums(part):
@@ -512,10 +533,14 @@
     replica_rows = latent_cache.shape[0]
     replicas = destination.shape[0] // replica_rows
     own_replica = lax.axis_index("dp")
-    to_box, picker = moves(destination, replica_rows)
-    packing = lax.dynamic_slice(
-        to_box, (own_replica * MOVE_MAX, own_replica * replica_rows), (MOVE_MAX, replica_rows)
-    )
+    picker = moves(destination, replica_rows)
+    own_slots = lax.dynamic_slice_in_dim(destination, own_replica * replica_rows, replica_rows)
+    leaving = own_slots // replica_rows != own_replica
+    places = jnp.arange(replica_rows, dtype=jnp.int32)
+    earlier = (places[:, None] < places[None, :]) & leaving[:, None]
+    rank = jnp.sum(earlier.astype(jnp.int32), axis=0)
+    box_ids = jnp.arange(MOVE_MAX, dtype=jnp.int32)
+    packing = narrow((rank[None, :] == box_ids[:, None]) & leaving[None, :])
     arrivals = migrate(packing, picker, latent_cache)
     boxes = jnp.arange(1, MOVE_MAX + 1, dtype=jnp.float32)[:, None]
     moved = jnp.sum(packing.astype(jnp.float32) * boxes, axis=0).astype(jnp.int32) - 1

time: 140 us -> 139 us (level)
  waiting for transfers between devices: 51.1 us -> 44.6 us
  starting transfers between devices: 31.9 us -> 36.1 us
  other arithmetic: 3.68 us -> 5.52 us
    ppermute x28 -> x32, waiting for transfers between devices: 40 us -> 34.9 us  [flip(): return lax.ppermute(x, axis, pairs)]
    ppermute x28 -> x32, starting transfers between devices: 19.9 us -> 24.3 us  [flip(): return lax.ppermute(x, axis, pairs)]
    all_to_all x1, waiting for transfers between devices: 6.88 us -> 5.34 us  [migrate(): met = lax.all_to_all(outbox, 'dp', split_axis=0, concat_axis=0)]
  transfers between devices with their start and end apart: 30 -> 34, of which waited for: 18 -> 18; matrix products, arithmetic and copies ran while one was open for 4% -> 5% of each run, Pallas kernels for 18% -> 18%
where the time goes in v7:
time: 139 us; the launch traced here: 138 us
  waiting for transfers between devices  44.6 us (32%)
  Pallas kernels  41.1 us (30%)
  starting transfers between devices  36.1 us (26%)
  other arithmetic  5.52 us (4%)
  local copies, waits for them, and re-layouts  4.67 us (3%)
  matrix products  3.08 us (2%)
  blocking collectives  2.19 us (2%)
    ppermute x32, waiting for transfers between devices, flip(): return lax.ppermute(x, axis, pairs)  34.9 us
    ppermute x32, starting transfers between devices, flip(): return lax.ppermute(x, axis, pairs)  24.3 us
    pallas_call x3, Pallas kernels, more_columns(): pl.pallas_call(functools.partial(columns_kernel, start), out_shape=jax.Sh...  12.8 us
    pallas_call x1, Pallas kernels, attention_and_first(): pl.pallas_call(attention_kernel, out_shape=(jax.ShapeDtypeStruct((request...  12.4 us
    all_to_all x1, starting transfers between devices, migrate(): met = lax.all_to_all(outbox, 'dp', split_axis=0, concat_axis=0)  8.31 us
    all_to_all x1, waiting for transfers between devices, migrate(): met = lax.all_to_all(outbox, 'dp', split_axis=0, concat_axis=0)  5.34 us
    pallas_call x1, Pallas kernels, hold_weights(): pl.pallas_call(hold_kernel, out_shape=(pltpu.VMEM((half, hidden_units), j...  5.29 us
    all_to_all x1, waiting for transfers between devices, migrate(): lax.all_to_all(sorted_rows.reshape(replicas, MOVE_MAX, share), 'dp', spli...  4.34 us
  transfers between devices with their start and end apart: 34, of which 18 were waited for; matrix products, arithmetic and copies ran while one was open for 5% of the time, Pallas kernels for 18%

profile of v7, /device:TPU:0, one launch (start us, length us, event | category | flops | bytes accessed | tf_op | source)
XLA Modules:
  0.0 138.4 jit_solution(10962588490086876860)
XLA Ops:
  1.6 1.9 %convolution_convert_fusion = bf16[4,18432]{1,0:T(4,128)(2,1)} fusion(bf16[16,36864]{1,0:T(8,128)(2,1)} %param.15, s32[]{:T(128)S(6)} %select_n.71, s32[16]{0:T(128)S(1)} %convert_reduce_fusion, pred[16]{0:T(512)(128)(4,1)S(1)} %fusion.30), kind=kOutput, calls=%fused_computation | convolution fusion | flops 2433152 | bytes 737364 | tf_op jit(solution)/shard_map/dot_general | solution.py:415
  3.5 8.3 %all-to-all-start = ((bf16[16,4,1152]{2,1,0:T(4,128)(2,1)}), bf16[16,4,1152]{2,1,0:T(4,128)(2,1)S(1)}, u32[]{:S(2)}, u32[]{:S(2)}) async-start(bf16[16,4,1152]{2,1,0:T(4,128)(2,1)} %bitcast.1), calls=%async_computation | async-start | bytes 294912 | tf_op jit(solution)/shard_map/all_to_all | solution.py:417
  14.4 5.3 %all-to-all-done = bf16[16,4,1152]{2,1,0:T(4,128)(2,1)S(1)} async-done(((bf16[16,4,1152]{2,1,0:T(4,128)(2,1)}), bf16[16,4,1152]{2,1,0:T(4,128)(2,1)S(1)}, u32[]{:S(2)}, u32[]{:S(2)}) %all-to-all-start) | async-done | bytes 147488 | tf_op jit(solution)/shard_map/all_to_all | solution.py:417
  20.7 3.5 %all-to-all-start.1 = ((bf16[16,4,1152]{2,1,0:T(4,128)(2,1)}), bf16[16,4,1152]{2,1,0:T(4,128)(2,1)S(1)}, u32[]{:S(2)}, u32[]{:S(2)}) async-start(bf16[16,4,1152]{2,1,0:T(4,128)(2,1)} %reshape.199), calls=%async_computation.1 | async-start | bytes 294912 | tf_op jit(solution)/shard_map/all_to_all | solution.py:421
  24.3 1.6 %reshape.196.cached = bf16[16,64,576]{2,1,0:T(8,128)(2,1)S(1)} reshape(bf16[16,36864]{1,0:T(8,128)(2,1)S(1)} %copy-done.1) | data formatting | bytes 2359296 | tf_op jit(solution)/shard_map/reshape | solution.py:549
  27.7 4.3 %all-to-all-done.1 = bf16[16,4,1152]{2,1,0:T(4,128)(2,1)S(1)} async-done(((bf16[16,4,1152]{2,1,0:T(4,128)(2,1)}), bf16[16,4,1152]{2,1,0:T(4,128)(2,1)S(1)}, u32[]{:S(2)}, u32[]{:S(2)}) %all-to-all-start.1) | async-done | bytes 147488 | tf_op jit(solution)/shard_map/all_to_all | solution.py:421
  32.0 2.2 %all_gather.3 = bf16[4,36864]{1,0:T(4,128)(2,1)S(1)} all-gather(bf16[4,18432]{1,0:T(4,128)(2,1)S(1)} %bitcast.44), channel_id=1, replica_groups=mesh['dp'=16,'ep'=2] {'ep'}, dimensions={1}, use_global_device_ids=true | all-gather | bytes 442368 | tf_op jit(solution)/shard_map/all_gather | solution.py:425
  34.6 12.4 %attention_and_first.1 = (f32[16,3584]{1,0:T(8,128)S(1)}, bf16[16,4096]{1,0:T(8,128)(2,1)S(1)}) custom-call(s32[16]{0:T(128)S(1)} %convert_add_fusion.2.moved, s32[16]{0:T(128)S(1)} %copy-done, bf16[16,32,576]{2,1,0:T(8,128)(2,1)S(1)} %reshape.195.queries, bf16[16,64,576]{2,1,0:T(8,128)(2,1)S(1)} %reshape.196.cached, ...), custom_call_target="tpu_custom_call" | custom-call | flops 536870912 | bytes 33554432 | tf_op jit(solution)/shard_map/attention_and_first/pallas_call | solution.py:120
  47.3 1.2 collective-permute-done
  49.7 3.8 %more_columns.3 = f32[16,1024]{1,0:T(8,128)S(1)} custom-call(bf16[16,4096]{1,0:T(8,128)(2,1)S(1)} %get-tuple-element.49.values, bf16[4096,7168]{1,0:T(8,128)(2,1)} %w_o.7), custom_call_target="tpu_custom_call" | custom-call | flops 134217728 | bytes 8388608 | tf_op jit(solution)/shard_map/more_columns/pallas_call | solution.py:172
  53.4 1.4 collective-permute-done.1
  55.0 3.8 %more_columns.4 = f32[16,1024]{1,0:T(8,128)S(1)} custom-call(bf16[16,4096]{1,0:T(8,128)(2,1)S(1)} %get-tuple-element.49.values, bf16[4096,7168]{1,0:T(8,128)(2,1)} %w_o.7), custom_call_target="tpu_custom_call" | custom-call | flops 134217728 | bytes 8388608 | tf_op jit(solution)/shard_map/more_columns/pallas_call | solution.py:172
  61.1 5.3 %more_columns.5 = f32[16,1536]{1,0:T(8,128)S(1)} custom-call(bf16[16,4096]{1,0:T(8,128)(2,1)S(1)} %get-tuple-element.49.values, bf16[4096,7168]{1,0:T(8,128)(2,1)} %w_o.7), custom_call_target="tpu_custom_call" | custom-call | flops 201326592 | bytes 12582912 | tf_op jit(solution)/shard_map/more_columns/pallas_call | solution.py:172
  67.5 1.2 collective-permute-start.7
  70.2 5.3 %hold_weights.1 = (bf16[3584,512]{1,0:T(8,128)(2,1)S(1)}, bf16[3584,512]{1,0:T(8,128)(2,1)S(1)}, bf16[512,7168]{1,0:T(8,128)(2,1)S(1)}, f32[2,128]{1,0:T(2,128)S(1)}) custom-call(f32[2,128]{1,0:T(2,128)S(1)} %add_convert_fusion.1.after, bf16[1,7168,512]{2,1,0:T(8,128)(2,1)} %refs_8_.1, bf16[1,7168,512]{2,1,0:T(8,128)(2,1)} %refs_9_.1, ...), custom_call_target="tpu_custom_call" | custom-call | bytes 14680064 | tf_op jit(solution)/shard_map/hold_weights/pallas_call | solution.py:271
  75.7 1.5 %collective-permute-start.8 = (bf16[16,3712]{1,0:T(8,128)(2,1)S(1)}, bf16[16,3712]{1,0:T(8,128)(2,1)S(1)}, u32[]{:S(2)}, u32[]{:S(2)}) collective-permute-start(bf16[16,3712]{1,0:T(8,128)(2,1)S(1)} %pad_maximum_fusion.4), channel_id=1, source_target_pairs={{0,8},{2,10},{4,12},{6,14},{8,0},{10,2},{12,4},{14,6},{16,24},{18,... | collective-permute-start | bytes 356360 | tf_op jit(solution)/shard_map/ppermute | solution.py:24
  77.2 3.6 %collective-permute-done.8 = bf16[16,3712]{1,0:T(8,128)(2,1)S(1)} collective-permute-done((bf16[16,3712]{1,0:T(8,128)(2,1)S(1)}, bf16[16,3712]{1,0:T(8,128)(2,1)S(1)}, u32[]{:S(2)}, u32[]{:S(2)}) %collective-permute-start.8) | collective-permute-done | bytes 118816 | tf_op jit(solution)/shard_map/ppermute | solution.py:24
  80.8 1.3 collective-permute-start.10
  83.2 4.3 %experts_first.1 = (f32[256,512]{1,0:T(8,128)S(1)}, f32[256,512]{1,0:T(8,128)S(1)}) custom-call(bf16[32,3584]{1,0:T(8,128)(2,1)S(1)} %pad_maximum_fusion.3.refs_0_, bf16[32,3584]{1,0:T(8,128)(2,1)S(1)} %collective-permute-done.3.refs_1_, bf16[32,3584]{1,0:T(8,128)(2,1)S(1)} %collective-permute-done.4.refs_2_, ...), custom_call_target="tpu_custom_call" | custom-call | flops 1879048192 | bytes 9175040 | tf_op jit(solution)/shard_map/experts_first/pallas_call | solution.py:224
  89.9 4.8 %collective-permute-done.15.refs_3_ = bf16[32,3712]{1,0:T(8,128)(2,1)S(1)} collective-permute-done((bf16[32,3712]{1,0:T(8,128)(2,1)S(1)}, bf16[32,3712]{1,0:T(8,128)(2,1)S(1)}, u32[]{:S(2)}, u32[]{:S(2)}) %collective-permute-start.15) | collective-permute-done | bytes 237600 | tf_op jit(solution)/shard_map/ppermute | solution.py:24
  94.7 1.5 %collective-permute-done.19.refs_7_ = bf16[32,3712]{1,0:T(8,128)(2,1)S(1)} collective-permute-done((bf16[32,3712]{1,0:T(8,128)(2,1)S(1)}, bf16[32,3712]{1,0:T(8,128)(2,1)S(1)}, u32[]{:S(2)}, u32[]{:S(2)}) %collective-permute-start.19) | collective-permute-done | bytes 237600 | tf_op jit(solution)/shard_map/ppermute | solution.py:24
  96.2 4.1 %experts_second.1 = (bf16[32,7168]{1,0:T(8,128)(2,1)S(1)}, bf16[32,7168]{1,0:T(8,128)(2,1)S(1)}, bf16[192,512]{1,0:T(8,128)(2,1)S(1)}) custom-call(bf16[32,3712]{1,0:T(8,128)(2,1)S(1)} %constant_dynamic-update-slice_fusion.3.refs_0_, bf16[32,3712]{1,0:T(8,128)(2,1)S(1)} %collective-permute-done.9.refs_1_, ...), custom_call_target="tpu_custom_call" | custom-call | flops 2818572288 | bytes 3670016 | tf_op jit(solution)/shard_map/experts_second/pallas_call | solution.py:337
  100.5 2.2 %experts_rest.1 = (bf16[96,7168]{1,0:T(8,128)(2,1)S(1)}, bf16[96,7168]{1,0:T(8,128)(2,1)S(1)}) custom-call(bf16[192,512]{1,0:T(8,128)(2,1)S(1)} %get-tuple-element.71.rest, bf16[512,7168]{1,0:T(8,128)(2,1)S(1)} %get-tuple-element.70.refs_13_.w_down), custom_call_target="tpu_custom_call" | custom-call | flops 1409286144 | bytes 2752512 | tf_op jit(solution)/shard_map/experts_rest/pallas_call | solution.py:377
  106.0 1.4 collective-permute-start.27
  107.6 2.7 %collective-permute-done.24 = bf16[32,3072]{1,0:T(8,128)(2,1)S(1)} collective-permute-done((bf16[32,3072]{1,0:T(8,128)(2,1)S(1)}, bf16[32,3072]{1,0:T(8,128)(2,1)S(1)}, u32[]{:S(2)}, u32[]{:S(2)}) %collective-permute-start.24) | collective-permute-done | bytes 196640 | tf_op jit(solution)/shard_map/ppermute | solution.py:24
  112.4 1.1 collective-permute-start.29
  114.5 8.0 %collective-permute-done.29 = bf16[16,896]{1,0:T(8,128)(2,1)S(1)} collective-permute-done((bf16[16,896]{1,0:T(8,128)(2,1)S(1)}, bf16[16,896]{1,0:T(8,128)(2,1)S(1)}, u32[]{:S(2)}, u32[]{:S(2)}) %collective-permute-start.29) | collective-permute-done | bytes 28704 | tf_op jit(solution)/shard_map/ppermute | solution.py:24
  122.5 1.3 collective-permute-start.30
  124.1 1.4 %collective-permute-start.26 = (bf16[1,16,6272]{2,1,0:T(8,128)(2,1)S(1)}, bf16[1,16,6272]{2,1,0:T(8,128)(2,1)S(1)}, u32[]{:S(2)}, u32[]{:S(2)}) collective-permute-start(bf16[1,16,6272]{2,1,0:T(8,128)(2,1)S(1)} %split.53), channel_id=1, source_target_pairs={{0,8},{2,10},{4,12},{6,14},{8,0},{10,2},{12,4},{14,6},{16,24},{18,... | collective-permute-start | bytes 602120 | tf_op jit(solution)/shard_map/ppermute | solution.py:24
  126.5 3.4 %collective-permute-done.26 = bf16[1,16,6272]{2,1,0:T(8,128)(2,1)S(1)} collective-permute-done((bf16[1,16,6272]{2,1,0:T(8,128)(2,1)S(1)}, bf16[1,16,6272]{2,1,0:T(8,128)(2,1)S(1)}, u32[]{:S(2)}, u32[]{:S(2)}) %collective-permute-start.26) | collective-permute-done | bytes 200736 | tf_op jit(solution)/shard_map/ppermute | solution.py:24
  130.0 3.0 %collective-permute-start.31 = (bf16[1,8,7168]{2,1,0:T(8,128)(2,1)S(1)}, bf16[1,8,7168]{2,1,0:T(8,128)(2,1)S(1)}, u32[]{:S(2)}, u32[]{:S(2)}) collective-permute-start(bf16[1,8,7168]{2,1,0:T(8,128)(2,1)S(1)} %split.54), channel_id=1, source_target_pairs={{0,16},{2,18},{4,20},{6,22},{8,24},{10,26},{12,28},{14,30},{16,0},... | collective-permute-start | bytes 344072 | tf_op jit(solution)/shard_map/ppermute | solution.py:24
  133.0 4.0 %collective-permute-done.31 = bf16[1,8,7168]{2,1,0:T(8,128)(2,1)S(1)} collective-permute-done((bf16[1,8,7168]{2,1,0:T(8,128)(2,1)S(1)}, bf16[1,8,7168]{2,1,0:T(8,128)(2,1)S(1)}, u32[]{:S(2)}, u32[]{:S(2)}) %collective-permute-start.31) | collective-permute-done | bytes 114720 | tf_op jit(solution)/shard_map/ppermute | solution.py:24
  (125 shorter events, 26.1 us)
Async XLA Ops:
  3.5 16.2 %all-to-all-start = ((bf16[16,4,1152]{2,1,0:T(4,128)(2,1)}), bf16[16,4,1152]{2,1,0:T(4,128)(2,1)S(1)}, u32[]{:S(2)}, u32[]{:S(2)}) async-start(bf16[16,4,1152]{2,1,0:T(4,128)(2,1)} %bitcast.1), calls=%async_computation | async-start | bytes 294912 | tf_op jit(solution)/shard_map/all_to_all | solution.py:417
  20.7 11.4 %all-to-all-start.1 = ((bf16[16,4,1152]{2,1,0:T(4,128)(2,1)}), bf16[16,4,1152]{2,1,0:T(4,128)(2,1)S(1)}, u32[]{:S(2)}, u32[]{:S(2)}) async-start(bf16[16,4,1152]{2,1,0:T(4,128)(2,1)} %reshape.199), calls=%async_computation.1 | async-start | bytes 294912 | tf_op jit(solution)/shard_map/all_to_all | solution.py:421
  48.6 6.2 %collective-permute-start.1 = (bf16[8,3584]{1,0:T(8,128)(2,1)S(1)}, bf16[8,3584]{1,0:T(8,128)(2,1)S(1)}, u32[]{:S(2)}, u32[]{:S(2)}) collective-permute-start(bf16[8,3584]{1,0:T(8,128)(2,1)S(1)} %multiply_convert_fusion.1), channel_id=1, source_target_pairs={{0,16},{2,18},{4,20},{6,22},{8,24},{10,26},{12,28},{14,30},{16,0},... | collective-permute-start | bytes 172040 | tf_op jit(solution)/shard_map/ppermute | solution.py:24
  54.8 4.9 %collective-permute-start.2 = (bf16[16,3584]{1,0:T(8,128)(2,1)S(1)}, bf16[16,3584]{1,0:T(8,128)(2,1)S(1)}, u32[]{:S(2)}, u32[]{:S(2)}) collective-permute-start(bf16[16,3584]{1,0:T(8,128)(2,1)S(1)} %pad_maximum_fusion.5), channel_id=1, source_target_pairs={{0,8},{2,10},{4,12},{6,14},{8,0},{10,2},{12,4},{14,6},{16,24},{18,... | collective-permute-start | bytes 344072 | tf_op jit(solution)/shard_map/ppermute | solution.py:24
  59.8 6.7 %collective-permute-start.4 = (bf16[32,3584]{1,0:T(8,128)(2,1)S(1)}, bf16[32,3584]{1,0:T(8,128)(2,1)S(1)}, u32[]{:S(2)}, u32[]{:S(2)}) collective-permute-start(bf16[32,3584]{1,0:T(8,128)(2,1)S(1)} %pad_maximum_fusion.3.refs_0_), channel_id=1, source_target_pairs={{0,4},{2,6},{4,0},{6,2},{8,12},{10,14},{12,8},{14,10},{16,20},{18,... | collective-permute-start | bytes 688136 | tf_op jit(solution)/shard_map/ppermute | solution.py:24
  60.6 6.2 %collective-permute-start.3 = (bf16[32,3584]{1,0:T(8,128)(2,1)S(1)}, bf16[32,3584]{1,0:T(8,128)(2,1)S(1)}, u32[]{:S(2)}, u32[]{:S(2)}) collective-permute-start(bf16[32,3584]{1,0:T(8,128)(2,1)S(1)} %pad_maximum_fusion.3.refs_0_), channel_id=1, source_target_pairs={{0,2},{2,0},{4,6},{6,4},{8,10},{10,8},{12,14},{14,12},{16,18},{18,... | collective-permute-start | bytes 688136 | tf_op jit(solution)/shard_map/ppermute | solution.py:24
  66.8 2.1 %collective-permute-start.5 = (f32[8,3584]{1,0:T(8,128)S(1)}, f32[8,3584]{1,0:T(8,128)S(1)}, u32[]{:S(2)}, u32[]{:S(2)}) collective-permute-start(f32[8,3584]{1,0:T(8,128)S(1)} %constant_dynamic-slice_fusion), channel_id=1, source_target_pairs={{0,1},{1,0},{2,3},{3,2},{4,5},{5,4},{6,7},{7,6},{8,9},{9,8},{10,11... | collective-permute-start | bytes 344072 | tf_op jit(solution)/shard_map/ppermute | solution.py:24
  66.9 15.2 %collective-permute-start.11 = (bf16[32,3584]{1,0:T(8,128)(2,1)S(1)}, bf16[32,3584]{1,0:T(8,128)(2,1)S(1)}, u32[]{:S(2)}, u32[]{:S(2)}) collective-permute-start(bf16[32,3584]{1,0:T(8,128)(2,1)S(1)} %pad_maximum_fusion.3.refs_0_), channel_id=1, source_target_pairs={{0,1},{1,0},{2,3},{3,2},{4,5},{5,4},{6,7},{7,6},{8,9},{9,8},{10,11... | collective-permute-start | bytes 688136 | tf_op jit(solution)/shard_map/ppermute | solution.py:24
  67.5 15.7 %collective-permute-start.13 = (bf16[32,3584]{1,0:T(8,128)(2,1)S(1)}, bf16[32,3584]{1,0:T(8,128)(2,1)S(1)}, u32[]{:S(2)}, u32[]{:S(2)}) collective-permute-start(bf16[32,3584]{1,0:T(8,128)(2,1)S(1)} %collective-permute-done.4.refs_2_), channel_id=1, source_target_pairs={{0,1},{1,0},{2,3},{3,2},{4,5},{5,4},{6,7},{7,6},{8,9},{9,8},{10,11... | collective-permute-start | bytes 688136 | tf_op jit(solution)/shard_map/ppermute | solution.py:24
  67.5 8.1 %collective-permute-start.7 = (bf16[32,3584]{1,0:T(8,128)(2,1)S(1)}, bf16[32,3584]{1,0:T(8,128)(2,1)S(1)}, u32[]{:S(2)}, u32[]{:S(2)}) collective-permute-start(bf16[32,3584]{1,0:T(8,128)(2,1)S(1)} %collective-permute-done.4.refs_2_), channel_id=1, source_target_pairs={{0,2},{2,0},{4,6},{6,4},{8,10},{10,8},{12,14},{14,12},{16,18},{18,... | collective-permute-start | bytes 688136 | tf_op jit(solution)/shard_map/ppermute | solution.py:24
  68.7 14.4 %collective-permute-start.12 = (bf16[32,3584]{1,0:T(8,128)(2,1)S(1)}, bf16[32,3584]{1,0:T(8,128)(2,1)S(1)}, u32[]{:S(2)}, u32[]{:S(2)}) collective-permute-start(bf16[32,3584]{1,0:T(8,128)(2,1)S(1)} %collective-permute-done.3.refs_1_), channel_id=1, source_target_pairs={{0,1},{1,0},{2,3},{3,2},{4,5},{5,4},{6,7},{7,6},{8,9},{9,8},{10,11... | collective-permute-start | bytes 688136 | tf_op jit(solution)/shard_map/ppermute | solution.py:24
  69.3 6.4 %collective-permute-start.6 = (bf16[8,3712]{1,0:T(8,128)(2,1)S(1)}, bf16[8,3712]{1,0:T(8,128)(2,1)S(1)}, u32[]{:S(2)}, u32[]{:S(2)}) collective-permute-start(bf16[8,3712]{1,0:T(8,128)(2,1)S(1)} %concatenate.37), channel_id=1, source_target_pairs={{0,16},{2,18},{4,20},{6,22},{8,24},{10,26},{12,28},{14,30},{16,0},... | collective-permute-start | bytes 178184 | tf_op jit(solution)/shard_map/ppermute | solution.py:24
  75.7 5.1 %collective-permute-start.8 = (bf16[16,3712]{1,0:T(8,128)(2,1)S(1)}, bf16[16,3712]{1,0:T(8,128)(2,1)S(1)}, u32[]{:S(2)}, u32[]{:S(2)}) collective-permute-start(bf16[16,3712]{1,0:T(8,128)(2,1)S(1)} %pad_maximum_fusion.4), channel_id=1, source_target_pairs={{0,8},{2,10},{4,12},{6,14},{8,0},{10,2},{12,4},{14,6},{16,24},{18,... | collective-permute-start | bytes 356360 | tf_op jit(solution)/shard_map/ppermute | solution.py:24
  77.2 5.9 %collective-permute-start.14 = (bf16[32,3584]{1,0:T(8,128)(2,1)S(1)}, bf16[32,3584]{1,0:T(8,128)(2,1)S(1)}, u32[]{:S(2)}, u32[]{:S(2)}) collective-permute-start(bf16[32,3584]{1,0:T(8,128)(2,1)S(1)} %collective-permute-done.7.refs_3_), channel_id=1, source_target_pairs={{0,1},{1,0},{2,3},{3,2},{4,5},{5,4},{6,7},{7,6},{8,9},{9,8},{10,11... | collective-permute-start | bytes 688136 | tf_op jit(solution)/shard_map/ppermute | solution.py:24
  80.8 6.8 %collective-permute-start.10 = (bf16[32,3712]{1,0:T(8,128)(2,1)S(1)}, bf16[32,3712]{1,0:T(8,128)(2,1)S(1)}, u32[]{:S(2)}, u32[]{:S(2)}) collective-permute-start(bf16[32,3712]{1,0:T(8,128)(2,1)S(1)} %constant_dynamic-update-slice_fusion.3.refs_0_), channel_id=1, source_target_pairs={{0,4},{2,6},{4,0},{6,2},{8,12},{10,14},{12,8},{14,10},{16,20},{18,... | collective-permute-start | bytes 712712 | tf_op jit(solution)/shard_map/ppermute | solution.py:24
  82.1 6.4 %collective-permute-start.9 = (bf16[32,3712]{1,0:T(8,128)(2,1)S(1)}, bf16[32,3712]{1,0:T(8,128)(2,1)S(1)}, u32[]{:S(2)}, u32[]{:S(2)}) collective-permute-start(bf16[32,3712]{1,0:T(8,128)(2,1)S(1)} %constant_dynamic-update-slice_fusion.3.refs_0_), channel_id=1, source_target_pairs={{0,2},{2,0},{4,6},{6,4},{8,10},{10,8},{12,14},{14,12},{16,18},{18,... | collective-permute-start | bytes 712712 | tf_op jit(solution)/shard_map/ppermute | solution.py:24
  88.6 6.1 %collective-permute-start.15 = (bf16[32,3712]{1,0:T(8,128)(2,1)S(1)}, bf16[32,3712]{1,0:T(8,128)(2,1)S(1)}, u32[]{:S(2)}, u32[]{:S(2)}) collective-permute-start(bf16[32,3712]{1,0:T(8,128)(2,1)S(1)} %collective-permute-done.9.refs_1_), channel_id=1, source_target_pairs={{0,4},{2,6},{4,0},{6,2},{8,12},{10,14},{12,8},{14,10},{16,20},{18,... | collective-permute-start | bytes 712712 | tf_op jit(solution)/shard_map/ppermute | solution.py:24
  89.3 5.4 %collective-permute-start.16 = (bf16[32,3712]{1,0:T(8,128)(2,1)S(1)}, bf16[32,3712]{1,0:T(8,128)(2,1)S(1)}, u32[]{:S(2)}, u32[]{:S(2)}) collective-permute-start(bf16[32,3712]{1,0:T(8,128)(2,1)S(1)} %constant_dynamic-update-slice_fusion.3.refs_0_), channel_id=1, source_target_pairs={{0,1},{1,0},{2,3},{3,2},{4,5},{5,4},{6,7},{7,6},{8,9},{9,8},{10,11... | collective-permute-start | bytes 712712 | tf_op jit(solution)/shard_map/ppermute | solution.py:24
  89.3 5.4 %collective-permute-start.17 = (bf16[32,3712]{1,0:T(8,128)(2,1)S(1)}, bf16[32,3712]{1,0:T(8,128)(2,1)S(1)}, u32[]{:S(2)}, u32[]{:S(2)}) collective-permute-start(bf16[32,3712]{1,0:T(8,128)(2,1)S(1)} %collective-permute-done.9.refs_1_), channel_id=1, source_target_pairs={{0,1},{1,0},{2,3},{3,2},{4,5},{5,4},{6,7},{7,6},{8,9},{9,8},{10,11... | collective-permute-start | bytes 712712 | tf_op jit(solution)/shard_map/ppermute | solution.py:24
  89.8 4.8 %collective-permute-start.18 = (bf16[32,3712]{1,0:T(8,128)(2,1)S(1)}, bf16[32,3712]{1,0:T(8,128)(2,1)S(1)}, u32[]{:S(2)}, u32[]{:S(2)}) collective-permute-start(bf16[32,3712]{1,0:T(8,128)(2,1)S(1)} %collective-permute-done.10.refs_2_), channel_id=1, source_target_pairs={{0,1},{1,0},{2,3},{3,2},{4,5},{5,4},{6,7},{7,6},{8,9},{9,8},{10,11... | collective-permute-start | bytes 712712 | tf_op jit(solution)/shard_map/ppermute | solution.py:24
  100.3 2.8 %collective-permute-start.21 = (bf16[32,7168]{1,0:T(8,128)(2,1)S(1)}, bf16[32,7168]{1,0:T(8,128)(2,1)S(1)}, u32[]{:S(2)}, u32[]{:S(2)}) collective-permute-start(bf16[32,7168]{1,0:T(8,128)(2,1)S(1)} %get-tuple-element.75), channel_id=1, source_target_pairs={{0,1},{1,0},{2,3},{3,2},{4,5},{5,4},{6,7},{7,6},{8,9},{9,8},{10,11... | collective-permute-start | bytes 1376264 | tf_op jit(solution)/shard_map/ppermute | solution.py:24
  102.7 3.2 %collective-permute-start.20 = (bf16[96,7168]{1,0:T(8,128)(2,1)S(1)}, bf16[96,7168]{1,0:T(8,128)(2,1)S(1)}, u32[]{:S(2)}, u32[]{:S(2)}) collective-permute-start(bf16[96,7168]{1,0:T(8,128)(2,1)S(1)} %get-tuple-element.73), channel_id=1, source_target_pairs={{0,1},{1,0},{2,3},{3,2},{4,5},{5,4},{6,7},{7,6},{8,9},{9,8},{10,11... | collective-permute-start | bytes 4128776 | tf_op jit(solution)/shard_map/ppermute | solution.py:24
  103.3 7.0 %collective-permute-start.24 = (bf16[32,3072]{1,0:T(8,128)(2,1)S(1)}, bf16[32,3072]{1,0:T(8,128)(2,1)S(1)}, u32[]{:S(2)}, u32[]{:S(2)}) collective-permute-start(bf16[32,3072]{1,0:T(8,128)(2,1)S(1)} %slice.128), channel_id=1, source_target_pairs={{0,2},{2,0},{4,6},{6,4},{8,10},{10,8},{12,14},{14,12},{16,18},{18,... | collective-permute-start | bytes 589832 | tf_op jit(solution)/shard_map/ppermute | solution.py:24
  104.4 6.9 %collective-permute-start.22 = (bf16[32,3200]{1,0:T(8,128)(2,1)S(1)}, bf16[32,3200]{1,0:T(8,128)(2,1)S(1)}, u32[]{:S(2)}, u32[]{:S(2)}) collective-permute-start(bf16[32,3200]{1,0:T(8,128)(2,1)S(1)} %slice.125), channel_id=1, source_target_pairs={{0,4},{2,6},{4,0},{6,2},{8,12},{10,14},{12,8},{14,10},{16,20},{18,... | collective-permute-start | bytes 614408 | tf_op jit(solution)/shard_map/ppermute | solution.py:24
  106.0 6.4 %collective-permute-start.27 = (bf16[4,16,896]{2,1,0:T(8,128)(2,1)S(1)}, bf16[4,16,896]{2,1,0:T(8,128)(2,1)S(1)}, u32[]{:S(2)}, u32[]{:S(2)}) collective-permute-start(bf16[4,16,896]{2,1,0:T(8,128)(2,1)S(1)} %split.55), channel_id=1, source_target_pairs={{0,8},{2,10},{4,12},{6,14},{8,0},{10,2},{12,4},{14,6},{16,24},{18,... | collective-permute-start | bytes 344072 | tf_op jit(solution)/shard_map/ppermute | solution.py:24
  110.4 13.5 %collective-permute-start.25 = (bf16[32,6272]{1,0:T(8,128)(2,1)S(1)}, bf16[32,6272]{1,0:T(8,128)(2,1)S(1)}, u32[]{:S(2)}, u32[]{:S(2)}) collective-permute-start(bf16[32,6272]{1,0:T(8,128)(2,1)S(1)} %pad_maximum_fusion.2), channel_id=1, source_target_pairs={{0,4},{2,6},{4,0},{6,2},{8,12},{10,14},{12,8},{14,10},{16,20},{18,... | collective-permute-start | bytes 1204232 | tf_op jit(solution)/shard_map/ppermute | solution.py:24
  111.3 12.5 %collective-permute-start.23 = (bf16[32,6272]{1,0:T(8,128)(2,1)S(1)}, bf16[32,6272]{1,0:T(8,128)(2,1)S(1)}, u32[]{:S(2)}, u32[]{:S(2)}) collective-permute-start(bf16[32,6272]{1,0:T(8,128)(2,1)S(1)} %pad_maximum_fusion.1), channel_id=1, source_target_pairs={{0,2},{2,0},{4,6},{6,4},{8,10},{10,8},{12,14},{14,12},{16,18},{18,... | collective-permute-start | bytes 1204232 | tf_op jit(solution)/shard_map/ppermute | solution.py:24
  112.4 10.1 %collective-permute-start.29 = (bf16[16,896]{1,0:T(8,128)(2,1)S(1)}, bf16[16,896]{1,0:T(8,128)(2,1)S(1)}, u32[]{:S(2)}, u32[]{:S(2)}) collective-permute-start(bf16[16,896]{1,0:T(8,128)(2,1)S(1)} %get-tuple-element.88), channel_id=1, source_target_pairs={{0,2},{2,0},{4,6},{6,4},{8,10},{10,8},{12,14},{14,12},{16,18},{18,... | collective-permute-start | bytes 86024 | tf_op jit(solution)/shard_map/ppermute | solution.py:24
  113.5 11.9 %collective-permute-start.28 = (bf16[16,896]{1,0:T(8,128)(2,1)S(1)}, bf16[16,896]{1,0:T(8,128)(2,1)S(1)}, u32[]{:S(2)}, u32[]{:S(2)}) collective-permute-start(bf16[16,896]{1,0:T(8,128)(2,1)S(1)} %get-tuple-element.87), channel_id=1, source_target_pairs={{0,2},{2,0},{4,6},{6,4},{8,10},{10,8},{12,14},{14,12},{16,18},{18,... | collective-permute-start | bytes 86024 | tf_op jit(solution)/shard_map/ppermute | solution.py:24
  122.5 3.9 %collective-permute-start.30 = (bf16[16,896]{1,0:T(8,128)(2,1)S(1)}, bf16[16,896]{1,0:T(8,128)(2,1)S(1)}, u32[]{:S(2)}, u32[]{:S(2)}) collective-permute-start(bf16[16,896]{1,0:T(8,128)(2,1)S(1)} %fusion.14), channel_id=1, source_target_pairs={{0,4},{2,6},{4,0},{6,2},{8,12},{10,14},{12,8},{14,10},{16,20},{18,... | collective-permute-start | bytes 86024 | tf_op jit(solution)/shard_map/ppermute | solution.py:24
  124.1 5.8 %collective-permute-start.26 = (bf16[1,16,6272]{2,1,0:T(8,128)(2,1)S(1)}, bf16[1,16,6272]{2,1,0:T(8,128)(2,1)S(1)}, u32[]{:S(2)}, u32[]{:S(2)}) collective-permute-start(bf16[1,16,6272]{2,1,0:T(8,128)(2,1)S(1)} %split.53), channel_id=1, source_target_pairs={{0,8},{2,10},{4,12},{6,14},{8,0},{10,2},{12,4},{14,6},{16,24},{18,... | collective-permute-start | bytes 602120 | tf_op jit(solution)/shard_map/ppermute | solution.py:24
  130.0 7.0 %collective-permute-start.31 = (bf16[1,8,7168]{2,1,0:T(8,128)(2,1)S(1)}, bf16[1,8,7168]{2,1,0:T(8,128)(2,1)S(1)}, u32[]{:S(2)}, u32[]{:S(2)}) collective-permute-start(bf16[1,8,7168]{2,1,0:T(8,128)(2,1)S(1)} %split.54), channel_id=1, source_target_pairs={{0,16},{2,18},{4,20},{6,22},{8,24},{10,26},{12,28},{14,30},{16,0},... | collective-permute-start | bytes 344072 | tf_op jit(solution)/shard_map/ppermute | solution.py:24
  (8 other events, 63.0 us)

commit v8 on v7

--- a/solution.py
+++ b/solution.py
@@ -31,7 +31,7 @@
 
 CHUNKS = 4
 OUTER_FIRST = 0.125
-IN_FLIGHT = 10 << 20
+IN_FLIGHT = 6 << 20
 
 
 def vmem_spec():
@@ -483,10 +483,12 @@
     to_y = narrow(jnp.concatenate([to_y[:, :half] + plus(low), to_y[:, half:]], axis=1))
     from_x = flip(to_x, "dp", inner_x)
     from_y = flip(to_y, "dp", inner_y)
+    far = flip(narrow(lines[3]), "dp", inner_x)
+    from_x, from_y, far = lax.optimization_barrier((from_x, from_y, far))
     first = outer_sums(plus(own, from_x, from_y)[None], nearer)[0]
 
-    own, to_x, to_y, far = lines
-    to_y = to_y + plus(flip(narrow(far), "dp", inner_x))
+    own, to_x, to_y, _ = lines
+    to_y = to_y + plus(far)
     from_x = flip(narrow(to_x), "dp", inner_x)
     from_y = flip(narrow(to_y), "dp", inner_y)
     last = own + plus(from_x, from_y)

time: 139 us -> 137 us (0.986)
  transfers between devices with their start and end apart: 34 -> 34, of which waited for: 18 -> 16; matrix products, arithmetic and copies ran while one was open for 5% -> 5% of each run, Pallas kernels for 18% -> 18%
where the time goes in v8:
time: 137 us
  waiting for transfers between devices  43.8 us (32%)
  Pallas kernels  41.3 us (30%)
  starting transfers between devices  35.3 us (26%)
  other arithmetic  5.5 us (4%)
  local copies, waits for them, and re-layouts  4.67 us (3%)
  matrix products  3.08 us (2%)
  blocking collectives  2.19 us (2%)
    ppermute x32, waiting for transfers between devices, flip(): return lax.ppermute(x, axis, pairs)  34.1 us
    ppermute x32, starting transfers between devices, flip(): return lax.ppermute(x, axis, pairs)  23.4 us
    pallas_call x3, Pallas kernels, more_columns(): pl.pallas_call(functools.partial(columns_kernel, start), out_shape=jax.Sh...  13.2 us
    pallas_call x1, Pallas kernels, attention_and_first(): pl.pallas_call(attention_kernel, out_shape=(jax.ShapeDtypeStruct((request...  12.2 us
    all_to_all x1, starting transfers between devices, migrate(): met = lax.all_to_all(outbox, 'dp', split_axis=0, concat_axis=0)  8.31 us
    all_to_all x1, waiting for transfers between devices, migrate(): met = lax.all_to_all(outbox, 'dp', split_axis=0, concat_axis=0)  5.34 us
    pallas_call x1, Pallas kernels, hold_weights(): pl.pallas_call(hold_kernel, out_shape=(pltpu.VMEM((half, hidden_units), j...  5.29 us
    all_to_all x1, waiting for transfers between devices, migrate(): lax.all_to_all(sorted_rows.reshape(replicas, MOVE_MAX, share), 'dp', spli...  4.34 us
  transfers between devices with their start and end apart: 34, of which 16 were waited for; matrix products, arithmetic and copies ran while one was open for 5% of the time, Pallas kernels for 18%

profile of v8, /device:TPU:0, one launch (start us, length us, event | category | flops | bytes accessed | tf_op | source)
XLA Modules:
  0.0 137.0 jit_solution(8201014753523334766)
XLA Ops:
  1.6 1.9 %convolution_convert_fusion = bf16[4,18432]{1,0:T(4,128)(2,1)} fusion(bf16[16,36864]{1,0:T(8,128)(2,1)} %param.15, s32[]{:T(128)S(6)} %select_n.71, s32[16]{0:T(128)S(1)} %convert_reduce_fusion, pred[16]{0:T(512)(128)(4,1)S(1)} %fusion.30), kind=kOutput, calls=%fused_computation | convolution fusion | flops 2433152 | bytes 737364 | tf_op jit(solution)/shard_map/dot_general | solution.py:415
  3.5 8.3 %all-to-all-start = ((bf16[16,4,1152]{2,1,0:T(4,128)(2,1)}), bf16[16,4,1152]{2,1,0:T(4,128)(2,1)S(1)}, u32[]{:S(2)}, u32[]{:S(2)}) async-start(bf16[16,4,1152]{2,1,0:T(4,128)(2,1)} %bitcast.1), calls=%async_computation | async-start | bytes 294912 | tf_op jit(solution)/shard_map/all_to_all | solution.py:417
  14.4 5.3 %all-to-all-done = bf16[16,4,1152]{2,1,0:T(4,128)(2,1)S(1)} async-done(((bf16[16,4,1152]{2,1,0:T(4,128)(2,1)}), bf16[16,4,1152]{2,1,0:T(4,128)(2,1)S(1)}, u32[]{:S(2)}, u32[]{:S(2)}) %all-to-all-start) | async-done | bytes 147488 | tf_op jit(solution)/shard_map/all_to_all | solution.py:417
  20.7 3.5 %all-to-all-start.1 = ((bf16[16,4,1152]{2,1,0:T(4,128)(2,1)}), bf16[16,4,1152]{2,1,0:T(4,128)(2,1)S(1)}, u32[]{:S(2)}, u32[]{:S(2)}) async-start(bf16[16,4,1152]{2,1,0:T(4,128)(2,1)} %reshape.199), calls=%async_computation.1 | async-start | bytes 294912 | tf_op jit(solution)/shard_map/all_to_all | solution.py:421
  24.3 1.6 %reshape.196.cached = bf16[16,64,576]{2,1,0:T(8,128)(2,1)S(1)} reshape(bf16[16,36864]{1,0:T(8,128)(2,1)S(1)} %copy-done.1) | data formatting | bytes 2359296 | tf_op jit(solution)/shard_map/reshape | solution.py:551
  27.7 4.3 %all-to-all-done.1 = bf16[16,4,1152]{2,1,0:T(4,128)(2,1)S(1)} async-done(((bf16[16,4,1152]{2,1,0:T(4,128)(2,1)}), bf16[16,4,1152]{2,1,0:T(4,128)(2,1)S(1)}, u32[]{:S(2)}, u32[]{:S(2)}) %all-to-all-start.1) | async-done | bytes 147488 | tf_op jit(solution)/shard_map/all_to_all | solution.py:421
  32.0 2.2 %all_gather.3 = bf16[4,36864]{1,0:T(4,128)(2,1)S(1)} all-gather(bf16[4,18432]{1,0:T(4,128)(2,1)S(1)} %bitcast.44), channel_id=1, replica_groups=mesh['dp'=16,'ep'=2] {'ep'}, dimensions={1}, use_global_device_ids=true | all-gather | bytes 442368 | tf_op jit(solution)/shard_map/all_gather | solution.py:425
  34.6 12.2 %attention_and_first.1 = (f32[16,3584]{1,0:T(8,128)S(1)}, bf16[16,4096]{1,0:T(8,128)(2,1)S(1)}) custom-call(s32[16]{0:T(128)S(1)} %convert_add_fusion.2.moved, s32[16]{0:T(128)S(1)} %copy-done, bf16[16,32,576]{2,1,0:T(8,128)(2,1)S(1)} %reshape.195.queries, bf16[16,64,576]{2,1,0:T(8,128)(2,1)S(1)} %reshape.196.cached, ...), custom_call_target="tpu_custom_call" | custom-call | flops 536870912 | bytes 33554432 | tf_op jit(solution)/shard_map/attention_and_first/pallas_call | solution.py:120
  47.0 1.2 collective-permute-done
  49.4 4.0 %more_columns.3 = f32[16,1024]{1,0:T(8,128)S(1)} custom-call(bf16[16,4096]{1,0:T(8,128)(2,1)S(1)} %get-tuple-element.52.values, bf16[4096,7168]{1,0:T(8,128)(2,1)} %w_o.7), custom_call_target="tpu_custom_call" | custom-call | flops 134217728 | bytes 8388608 | tf_op jit(solution)/shard_map/more_columns/pallas_call | solution.py:172
  54.8 4.0 %more_columns.4 = f32[16,1024]{1,0:T(8,128)S(1)} custom-call(bf16[16,4096]{1,0:T(8,128)(2,1)S(1)} %get-tuple-element.52.values, bf16[4096,7168]{1,0:T(8,128)(2,1)} %w_o.7), custom_call_target="tpu_custom_call" | custom-call | flops 134217728 | bytes 8388608 | tf_op jit(solution)/shard_map/more_columns/pallas_call | solution.py:172
  60.9 5.2 %more_columns.5 = f32[16,1536]{1,0:T(8,128)S(1)} custom-call(bf16[16,4096]{1,0:T(8,128)(2,1)S(1)} %get-tuple-element.52.values, bf16[4096,7168]{1,0:T(8,128)(2,1)} %w_o.7), custom_call_target="tpu_custom_call" | custom-call | flops 201326592 | bytes 12582912 | tf_op jit(solution)/shard_map/more_columns/pallas_call | solution.py:172
  70.1 5.3 %hold_weights.1 = (bf16[3584,512]{1,0:T(8,128)(2,1)S(1)}, bf16[3584,512]{1,0:T(8,128)(2,1)S(1)}, bf16[512,7168]{1,0:T(8,128)(2,1)S(1)}, f32[2,128]{1,0:T(2,128)S(1)}) custom-call(f32[2,128]{1,0:T(2,128)S(1)} %add_convert_fusion.1.after, bf16[1,7168,512]{2,1,0:T(8,128)(2,1)} %refs_8_.1, bf16[1,7168,512]{2,1,0:T(8,128)(2,1)} %refs_9_.1, ...), custom_call_target="tpu_custom_call" | custom-call | bytes 14680064 | tf_op jit(solution)/shard_map/hold_weights/pallas_call | solution.py:271
  75.5 1.7 %collective-permute-start.8 = (bf16[16,3712]{1,0:T(8,128)(2,1)S(1)}, bf16[16,3712]{1,0:T(8,128)(2,1)S(1)}, u32[]{:S(2)}, u32[]{:S(2)}) collective-permute-start(bf16[16,3712]{1,0:T(8,128)(2,1)S(1)} %pad_maximum_fusion.4), channel_id=1, source_target_pairs={{0,8},{2,10},{4,12},{6,14},{8,0},{10,2},{12,4},{14,6},{16,24},{18,... | collective-permute-start | bytes 356360 | tf_op jit(solution)/shard_map/ppermute | solution.py:24
  77.2 3.5 %collective-permute-done.8 = bf16[16,3712]{1,0:T(8,128)(2,1)S(1)} collective-permute-done((bf16[16,3712]{1,0:T(8,128)(2,1)S(1)}, bf16[16,3712]{1,0:T(8,128)(2,1)S(1)}, u32[]{:S(2)}, u32[]{:S(2)}) %collective-permute-start.8) | collective-permute-done | bytes 118816 | tf_op jit(solution)/shard_map/ppermute | solution.py:24
  80.7 1.3 collective-permute-start.10
  82.1 1.3 collective-permute-start.9
  83.4 4.3 %experts_first.1 = (f32[256,512]{1,0:T(8,128)S(1)}, f32[256,512]{1,0:T(8,128)S(1)}) custom-call(bf16[32,3584]{1,0:T(8,128)(2,1)S(1)} %pad_maximum_fusion.3.refs_0_, bf16[32,3584]{1,0:T(8,128)(2,1)S(1)} %collective-permute-done.3.refs_1_, bf16[32,3584]{1,0:T(8,128)(2,1)S(1)} %collective-permute-done.4.refs_2_, ...), custom_call_target="tpu_custom_call" | custom-call | flops 1879048192 | bytes 9175040 | tf_op jit(solution)/shard_map/experts_first/pallas_call | solution.py:224
  90.0 4.8 %collective-permute-done.15.refs_3_ = bf16[32,3712]{1,0:T(8,128)(2,1)S(1)} collective-permute-done((bf16[32,3712]{1,0:T(8,128)(2,1)S(1)}, bf16[32,3712]{1,0:T(8,128)(2,1)S(1)}, u32[]{:S(2)}, u32[]{:S(2)}) %collective-permute-start.15) | collective-permute-done | bytes 237600 | tf_op jit(solution)/shard_map/ppermute | solution.py:24
  94.8 1.5 %collective-permute-done.19.refs_7_ = bf16[32,3712]{1,0:T(8,128)(2,1)S(1)} collective-permute-done((bf16[32,3712]{1,0:T(8,128)(2,1)S(1)}, bf16[32,3712]{1,0:T(8,128)(2,1)S(1)}, u32[]{:S(2)}, u32[]{:S(2)}) %collective-permute-start.19) | collective-permute-done | bytes 237600 | tf_op jit(solution)/shard_map/ppermute | solution.py:24
  96.3 4.1 %experts_second.1 = (bf16[32,7168]{1,0:T(8,128)(2,1)S(1)}, bf16[32,7168]{1,0:T(8,128)(2,1)S(1)}, bf16[192,512]{1,0:T(8,128)(2,1)S(1)}) custom-call(bf16[32,3712]{1,0:T(8,128)(2,1)S(1)} %constant_dynamic-update-slice_fusion.3.refs_0_, bf16[32,3712]{1,0:T(8,128)(2,1)S(1)} %collective-permute-done.9.refs_1_, ...), custom_call_target="tpu_custom_call" | custom-call | flops 2818572288 | bytes 3670016 | tf_op jit(solution)/shard_map/experts_second/pallas_call | solution.py:337
  100.7 2.2 %experts_rest.1 = (bf16[96,7168]{1,0:T(8,128)(2,1)S(1)}, bf16[96,7168]{1,0:T(8,128)(2,1)S(1)}) custom-call(bf16[192,512]{1,0:T(8,128)(2,1)S(1)} %get-tuple-element.74.rest, bf16[512,7168]{1,0:T(8,128)(2,1)S(1)} %get-tuple-element.73.refs_13_.w_down), custom_call_target="tpu_custom_call" | custom-call | flops 1409286144 | bytes 2752512 | tf_op jit(solution)/shard_map/experts_rest/pallas_call | solution.py:377
  103.4 1.3 collective-permute-start.24
  106.1 1.7 %collective-permute-start.26 = (bf16[4,16,896]{2,1,0:T(8,128)(2,1)S(1)}, bf16[4,16,896]{2,1,0:T(8,128)(2,1)S(1)}, u32[]{:S(2)}, u32[]{:S(2)}) collective-permute-start(bf16[4,16,896]{2,1,0:T(8,128)(2,1)S(1)} %split.55), channel_id=1, source_target_pairs={{0,8},{2,10},{4,12},{6,14},{8,0},{10,2},{12,4},{14,6},{16,24},{18,... | collective-permute-start | bytes 344072 | tf_op jit(solution)/shard_map/ppermute | solution.py:24
  108.0 3.5 %collective-permute-done.22 = bf16[32,3200]{1,0:T(8,128)(2,1)S(1)} collective-permute-done((bf16[32,3200]{1,0:T(8,128)(2,1)S(1)}, bf16[32,3200]{1,0:T(8,128)(2,1)S(1)}, u32[]{:S(2)}, u32[]{:S(2)}) %collective-permute-start.22) | collective-permute-done | bytes 204832 | tf_op jit(solution)/shard_map/ppermute | solution.py:24
  113.5 1.3 collective-permute-start.27
  115.6 7.3 %collective-permute-done.27 = bf16[16,896]{1,0:T(8,128)(2,1)S(1)} collective-permute-done((bf16[16,896]{1,0:T(8,128)(2,1)S(1)}, bf16[16,896]{1,0:T(8,128)(2,1)S(1)}, u32[]{:S(2)}, u32[]{:S(2)}) %collective-permute-start.27) | collective-permute-done | bytes 28704 | tf_op jit(solution)/shard_map/ppermute | solution.py:24
  123.9 1.3 collective-permute-start.28
  125.2 1.6 %collective-permute-done.30 = bf16[16,896]{1,0:T(8,128)(2,1)S(1)} collective-permute-done((bf16[16,896]{1,0:T(8,128)(2,1)S(1)}, bf16[16,896]{1,0:T(8,128)(2,1)S(1)}, u32[]{:S(2)}, u32[]{:S(2)}) %collective-permute-start.30) | collective-permute-done | bytes 28704 | tf_op jit(solution)/shard_map/ppermute | solution.py:24
  126.8 2.9 %collective-permute-done.28 = bf16[1,16,6272]{2,1,0:T(8,128)(2,1)S(1)} collective-permute-done((bf16[1,16,6272]{2,1,0:T(8,128)(2,1)S(1)}, bf16[1,16,6272]{2,1,0:T(8,128)(2,1)S(1)}, u32[]{:S(2)}, u32[]{:S(2)}) %collective-permute-start.28) | collective-permute-done | bytes 200736 | tf_op jit(solution)/shard_map/ppermute | solution.py:24
  129.8 1.9 %collective-permute-start.31 = (bf16[1,8,7168]{2,1,0:T(8,128)(2,1)S(1)}, bf16[1,8,7168]{2,1,0:T(8,128)(2,1)S(1)}, u32[]{:S(2)}, u32[]{:S(2)}) collective-permute-start(bf16[1,8,7168]{2,1,0:T(8,128)(2,1)S(1)} %split.54), channel_id=1, source_target_pairs={{0,16},{2,18},{4,20},{6,22},{8,24},{10,26},{12,28},{14,30},{16,0},... | collective-permute-start | bytes 344072 | tf_op jit(solution)/shard_map/ppermute | solution.py:24
  131.7 3.8 %collective-permute-done.31 = bf16[1,8,7168]{2,1,0:T(8,128)(2,1)S(1)} collective-permute-done((bf16[1,8,7168]{2,1,0:T(8,128)(2,1)S(1)}, bf16[1,8,7168]{2,1,0:T(8,128)(2,1)S(1)}, u32[]{:S(2)}, u32[]{:S(2)}) %collective-permute-start.31) | collective-permute-done | bytes 114720 | tf_op jit(solution)/shard_map/ppermute | solution.py:24
  (125 shorter events, 25.2 us)
Async XLA Ops:
  3.5 16.2 %all-to-all-start = ((bf16[16,4,1152]{2,1,0:T(4,128)(2,1)}), bf16[16,4,1152]{2,1,0:T(4,128)(2,1)S(1)}, u32[]{:S(2)}, u32[]{:S(2)}) async-start(bf16[16,4,1152]{2,1,0:T(4,128)(2,1)} %bitcast.1), calls=%async_computation | async-start | bytes 294912 | tf_op jit(solution)/shard_map/all_to_all | solution.py:417
  20.7 11.4 %all-to-all-start.1 = ((bf16[16,4,1152]{2,1,0:T(4,128)(2,1)}), bf16[16,4,1152]{2,1,0:T(4,128)(2,1)S(1)}, u32[]{:S(2)}, u32[]{:S(2)}) async-start(bf16[16,4,1152]{2,1,0:T(4,128)(2,1)} %reshape.199), calls=%async_computation.1 | async-start | bytes 294912 | tf_op jit(solution)/shard_map/all_to_all | solution.py:421
  48.4 6.2 %collective-permute-start.1 = (bf16[8,3584]{1,0:T(8,128)(2,1)S(1)}, bf16[8,3584]{1,0:T(8,128)(2,1)S(1)}, u32[]{:S(2)}, u32[]{:S(2)}) collective-permute-start(bf16[8,3584]{1,0:T(8,128)(2,1)S(1)} %multiply_convert_fusion.1), channel_id=1, source_target_pairs={{0,16},{2,18},{4,20},{6,22},{8,24},{10,26},{12,28},{14,30},{16,0},... | collective-permute-start | bytes 172040 | tf_op jit(solution)/shard_map/ppermute | solution.py:24
  54.6 4.9 %collective-permute-start.2 = (bf16[16,3584]{1,0:T(8,128)(2,1)S(1)}, bf16[16,3584]{1,0:T(8,128)(2,1)S(1)}, u32[]{:S(2)}, u32[]{:S(2)}) collective-permute-start(bf16[16,3584]{1,0:T(8,128)(2,1)S(1)} %pad_maximum_fusion.5), channel_id=1, source_target_pairs={{0,8},{2,10},{4,12},{6,14},{8,0},{10,2},{12,4},{14,6},{16,24},{18,... | collective-permute-start | bytes 344072 | tf_op jit(solution)/shard_map/ppermute | solution.py:24
  59.5 6.7 %collective-permute-start.4 = (bf16[32,3584]{1,0:T(8,128)(2,1)S(1)}, bf16[32,3584]{1,0:T(8,128)(2,1)S(1)}, u32[]{:S(2)}, u32[]{:S(2)}) collective-permute-start(bf16[32,3584]{1,0:T(8,128)(2,1)S(1)} %pad_maximum_fusion.3.refs_0_), channel_id=1, source_target_pairs={{0,4},{2,6},{4,0},{6,2},{8,12},{10,14},{12,8},{14,10},{16,20},{18,... | collective-permute-start | bytes 688136 | tf_op jit(solution)/shard_map/ppermute | solution.py:24
  60.3 6.3 %collective-permute-start.3 = (bf16[32,3584]{1,0:T(8,128)(2,1)S(1)}, bf16[32,3584]{1,0:T(8,128)(2,1)S(1)}, u32[]{:S(2)}, u32[]{:S(2)}) collective-permute-start(bf16[32,3584]{1,0:T(8,128)(2,1)S(1)} %pad_maximum_fusion.3.refs_0_), channel_id=1, source_target_pairs={{0,2},{2,0},{4,6},{6,4},{8,10},{10,8},{12,14},{14,12},{16,18},{18,... | collective-permute-start | bytes 688136 | tf_op jit(solution)/shard_map/ppermute | solution.py:24
  66.7 1.9 %collective-permute-start.5 = (f32[8,3584]{1,0:T(8,128)S(1)}, f32[8,3584]{1,0:T(8,128)S(1)}, u32[]{:S(2)}, u32[]{:S(2)}) collective-permute-start(f32[8,3584]{1,0:T(8,128)S(1)} %constant_dynamic-slice_fusion), channel_id=1, source_target_pairs={{0,1},{1,0},{2,3},{3,2},{4,5},{5,4},{6,7},{7,6},{8,9},{9,8},{10,11... | collective-permute-start | bytes 344072 | tf_op jit(solution)/shard_map/ppermute | solution.py:24
  66.8 15.3 %collective-permute-start.11 = (bf16[32,3584]{1,0:T(8,128)(2,1)S(1)}, bf16[32,3584]{1,0:T(8,128)(2,1)S(1)}, u32[]{:S(2)}, u32[]{:S(2)}) collective-permute-start(bf16[32,3584]{1,0:T(8,128)(2,1)S(1)} %pad_maximum_fusion.3.refs_0_), channel_id=1, source_target_pairs={{0,1},{1,0},{2,3},{3,2},{4,5},{5,4},{6,7},{7,6},{8,9},{9,8},{10,11... | collective-permute-start | bytes 688136 | tf_op jit(solution)/shard_map/ppermute | solution.py:24
  67.4 16.0 %collective-permute-start.13 = (bf16[32,3584]{1,0:T(8,128)(2,1)S(1)}, bf16[32,3584]{1,0:T(8,128)(2,1)S(1)}, u32[]{:S(2)}, u32[]{:S(2)}) collective-permute-start(bf16[32,3584]{1,0:T(8,128)(2,1)S(1)} %collective-permute-done.4.refs_2_), channel_id=1, source_target_pairs={{0,1},{1,0},{2,3},{3,2},{4,5},{5,4},{6,7},{7,6},{8,9},{9,8},{10,11... | collective-permute-start | bytes 688136 | tf_op jit(solution)/shard_map/ppermute | solution.py:24
  67.4 8.0 %collective-permute-start.7 = (bf16[32,3584]{1,0:T(8,128)(2,1)S(1)}, bf16[32,3584]{1,0:T(8,128)(2,1)S(1)}, u32[]{:S(2)}, u32[]{:S(2)}) collective-permute-start(bf16[32,3584]{1,0:T(8,128)(2,1)S(1)} %collective-permute-done.4.refs_2_), channel_id=1, source_target_pairs={{0,2},{2,0},{4,6},{6,4},{8,10},{10,8},{12,14},{14,12},{16,18},{18,... | collective-permute-start | bytes 688136 | tf_op jit(solution)/shard_map/ppermute | solution.py:24
  68.4 14.9 %collective-permute-start.12 = (bf16[32,3584]{1,0:T(8,128)(2,1)S(1)}, bf16[32,3584]{1,0:T(8,128)(2,1)S(1)}, u32[]{:S(2)}, u32[]{:S(2)}) collective-permute-start(bf16[32,3584]{1,0:T(8,128)(2,1)S(1)} %collective-permute-done.3.refs_1_), channel_id=1, source_target_pairs={{0,1},{1,0},{2,3},{3,2},{4,5},{5,4},{6,7},{7,6},{8,9},{9,8},{10,11... | collective-permute-start | bytes 688136 | tf_op jit(solution)/shard_map/ppermute | solution.py:24
  69.0 6.4 %collective-permute-start.6 = (bf16[8,3712]{1,0:T(8,128)(2,1)S(1)}, bf16[8,3712]{1,0:T(8,128)(2,1)S(1)}, u32[]{:S(2)}, u32[]{:S(2)}) collective-permute-start(bf16[8,3712]{1,0:T(8,128)(2,1)S(1)} %concatenate.37), channel_id=1, source_target_pairs={{0,16},{2,18},{4,20},{6,22},{8,24},{10,26},{12,28},{14,30},{16,0},... | collective-permute-start | bytes 178184 | tf_op jit(solution)/shard_map/ppermute | solution.py:24
  75.5 5.3 %collective-permute-start.8 = (bf16[16,3712]{1,0:T(8,128)(2,1)S(1)}, bf16[16,3712]{1,0:T(8,128)(2,1)S(1)}, u32[]{:S(2)}, u32[]{:S(2)}) collective-permute-start(bf16[16,3712]{1,0:T(8,128)(2,1)S(1)} %pad_maximum_fusion.4), channel_id=1, source_target_pairs={{0,8},{2,10},{4,12},{6,14},{8,0},{10,2},{12,4},{14,6},{16,24},{18,... | collective-permute-start | bytes 356360 | tf_op jit(solution)/shard_map/ppermute | solution.py:24
  77.2 6.1 %collective-permute-start.14 = (bf16[32,3584]{1,0:T(8,128)(2,1)S(1)}, bf16[32,3584]{1,0:T(8,128)(2,1)S(1)}, u32[]{:S(2)}, u32[]{:S(2)}) collective-permute-start(bf16[32,3584]{1,0:T(8,128)(2,1)S(1)} %collective-permute-done.7.refs_3_), channel_id=1, source_target_pairs={{0,1},{1,0},{2,3},{3,2},{4,5},{5,4},{6,7},{7,6},{8,9},{9,8},{10,11... | collective-permute-start | bytes 688136 | tf_op jit(solution)/shard_map/ppermute | solution.py:24
  80.7 7.0 %collective-permute-start.10 = (bf16[32,3712]{1,0:T(8,128)(2,1)S(1)}, bf16[32,3712]{1,0:T(8,128)(2,1)S(1)}, u32[]{:S(2)}, u32[]{:S(2)}) collective-permute-start(bf16[32,3712]{1,0:T(8,128)(2,1)S(1)} %constant_dynamic-update-slice_fusion.3.refs_0_), channel_id=1, source_target_pairs={{0,4},{2,6},{4,0},{6,2},{8,12},{10,14},{12,8},{14,10},{16,20},{18,... | collective-permute-start | bytes 712712 | tf_op jit(solution)/shard_map/ppermute | solution.py:24
  82.1 6.6 %collective-permute-start.9 = (bf16[32,3712]{1,0:T(8,128)(2,1)S(1)}, bf16[32,3712]{1,0:T(8,128)(2,1)S(1)}, u32[]{:S(2)}, u32[]{:S(2)}) collective-permute-start(bf16[32,3712]{1,0:T(8,128)(2,1)S(1)} %constant_dynamic-update-slice_fusion.3.refs_0_), channel_id=1, source_target_pairs={{0,2},{2,0},{4,6},{6,4},{8,10},{10,8},{12,14},{14,12},{16,18},{18,... | collective-permute-start | bytes 712712 | tf_op jit(solution)/shard_map/ppermute | solution.py:24
  88.7 6.1 %collective-permute-start.15 = (bf16[32,3712]{1,0:T(8,128)(2,1)S(1)}, bf16[32,3712]{1,0:T(8,128)(2,1)S(1)}, u32[]{:S(2)}, u32[]{:S(2)}) collective-permute-start(bf16[32,3712]{1,0:T(8,128)(2,1)S(1)} %collective-permute-done.9.refs_1_), channel_id=1, source_target_pairs={{0,4},{2,6},{4,0},{6,2},{8,12},{10,14},{12,8},{14,10},{16,20},{18,... | collective-permute-start | bytes 712712 | tf_op jit(solution)/shard_map/ppermute | solution.py:24
  89.5 5.4 %collective-permute-start.16 = (bf16[32,3712]{1,0:T(8,128)(2,1)S(1)}, bf16[32,3712]{1,0:T(8,128)(2,1)S(1)}, u32[]{:S(2)}, u32[]{:S(2)}) collective-permute-start(bf16[32,3712]{1,0:T(8,128)(2,1)S(1)} %constant_dynamic-update-slice_fusion.3.refs_0_), channel_id=1, source_target_pairs={{0,1},{1,0},{2,3},{3,2},{4,5},{5,4},{6,7},{7,6},{8,9},{9,8},{10,11... | collective-permute-start | bytes 712712 | tf_op jit(solution)/shard_map/ppermute | solution.py:24
  89.5 5.4 %collective-permute-start.17 = (bf16[32,3712]{1,0:T(8,128)(2,1)S(1)}, bf16[32,3712]{1,0:T(8,128)(2,1)S(1)}, u32[]{:S(2)}, u32[]{:S(2)}) collective-permute-start(bf16[32,3712]{1,0:T(8,128)(2,1)S(1)} %collective-permute-done.9.refs_1_), channel_id=1, source_target_pairs={{0,1},{1,0},{2,3},{3,2},{4,5},{5,4},{6,7},{7,6},{8,9},{9,8},{10,11... | collective-permute-start | bytes 712712 | tf_op jit(solution)/shard_map/ppermute | solution.py:24
  90.0 4.9 %collective-permute-start.18 = (bf16[32,3712]{1,0:T(8,128)(2,1)S(1)}, bf16[32,3712]{1,0:T(8,128)(2,1)S(1)}, u32[]{:S(2)}, u32[]{:S(2)}) collective-permute-start(bf16[32,3712]{1,0:T(8,128)(2,1)S(1)} %collective-permute-done.10.refs_2_), channel_id=1, source_target_pairs={{0,1},{1,0},{2,3},{3,2},{4,5},{5,4},{6,7},{7,6},{8,9},{9,8},{10,11... | collective-permute-start | bytes 712712 | tf_op jit(solution)/shard_map/ppermute | solution.py:24
  100.5 2.8 %collective-permute-start.21 = (bf16[32,7168]{1,0:T(8,128)(2,1)S(1)}, bf16[32,7168]{1,0:T(8,128)(2,1)S(1)}, u32[]{:S(2)}, u32[]{:S(2)}) collective-permute-start(bf16[32,7168]{1,0:T(8,128)(2,1)S(1)} %get-tuple-element.78), channel_id=1, source_target_pairs={{0,1},{1,0},{2,3},{3,2},{4,5},{5,4},{6,7},{7,6},{8,9},{9,8},{10,11... | collective-permute-start | bytes 1376264 | tf_op jit(solution)/shard_map/ppermute | solution.py:24
  102.8 3.2 %collective-permute-start.20 = (bf16[96,7168]{1,0:T(8,128)(2,1)S(1)}, bf16[96,7168]{1,0:T(8,128)(2,1)S(1)}, u32[]{:S(2)}, u32[]{:S(2)}) collective-permute-start(bf16[96,7168]{1,0:T(8,128)(2,1)S(1)} %get-tuple-element.76), channel_id=1, source_target_pairs={{0,1},{1,0},{2,3},{3,2},{4,5},{5,4},{6,7},{7,6},{8,9},{9,8},{10,11... | collective-permute-start | bytes 4128776 | tf_op jit(solution)/shard_map/ppermute | solution.py:24
  103.4 9.1 %collective-permute-start.24 = (bf16[32,3072]{1,0:T(8,128)(2,1)S(1)}, bf16[32,3072]{1,0:T(8,128)(2,1)S(1)}, u32[]{:S(2)}, u32[]{:S(2)}) collective-permute-start(bf16[32,3072]{1,0:T(8,128)(2,1)S(1)} %slice.133), channel_id=1, source_target_pairs={{0,2},{2,0},{4,6},{6,4},{8,10},{10,8},{12,14},{14,12},{16,18},{18,... | collective-permute-start | bytes 589832 | tf_op jit(solution)/shard_map/ppermute | solution.py:24
  104.7 6.8 %collective-permute-start.22 = (bf16[32,3200]{1,0:T(8,128)(2,1)S(1)}, bf16[32,3200]{1,0:T(8,128)(2,1)S(1)}, u32[]{:S(2)}, u32[]{:S(2)}) collective-permute-start(bf16[32,3200]{1,0:T(8,128)(2,1)S(1)} %slice.130), channel_id=1, source_target_pairs={{0,4},{2,6},{4,0},{6,2},{8,12},{10,14},{12,8},{14,10},{16,20},{18,... | collective-permute-start | bytes 614408 | tf_op jit(solution)/shard_map/ppermute | solution.py:24
  106.1 7.3 %collective-permute-start.26 = (bf16[4,16,896]{2,1,0:T(8,128)(2,1)S(1)}, bf16[4,16,896]{2,1,0:T(8,128)(2,1)S(1)}, u32[]{:S(2)}, u32[]{:S(2)}) collective-permute-start(bf16[4,16,896]{2,1,0:T(8,128)(2,1)S(1)} %split.55), channel_id=1, source_target_pairs={{0,8},{2,10},{4,12},{6,14},{8,0},{10,2},{12,4},{14,6},{16,24},{18,... | collective-permute-start | bytes 344072 | tf_op jit(solution)/shard_map/ppermute | solution.py:24
  111.7 11.2 %collective-permute-start.23 = (bf16[32,6272]{1,0:T(8,128)(2,1)S(1)}, bf16[32,6272]{1,0:T(8,128)(2,1)S(1)}, u32[]{:S(2)}, u32[]{:S(2)}) collective-permute-start(bf16[32,6272]{1,0:T(8,128)(2,1)S(1)} %pad_maximum_fusion.1), channel_id=1, source_target_pairs={{0,2},{2,0},{4,6},{6,4},{8,10},{10,8},{12,14},{14,12},{16,18},{18,... | collective-permute-start | bytes 1204232 | tf_op jit(solution)/shard_map/ppermute | solution.py:24
  112.6 10.3 %collective-permute-start.25 = (bf16[32,6272]{1,0:T(8,128)(2,1)S(1)}, bf16[32,6272]{1,0:T(8,128)(2,1)S(1)}, u32[]{:S(2)}, u32[]{:S(2)}) collective-permute-start(bf16[32,6272]{1,0:T(8,128)(2,1)S(1)} %pad_maximum_fusion.2), channel_id=1, source_target_pairs={{0,4},{2,6},{4,0},{6,2},{8,12},{10,14},{12,8},{14,10},{16,20},{18,... | collective-permute-start | bytes 1204232 | tf_op jit(solution)/shard_map/ppermute | solution.py:24
  113.5 9.4 %collective-permute-start.27 = (bf16[16,896]{1,0:T(8,128)(2,1)S(1)}, bf16[16,896]{1,0:T(8,128)(2,1)S(1)}, u32[]{:S(2)}, u32[]{:S(2)}) collective-permute-start(bf16[16,896]{1,0:T(8,128)(2,1)S(1)} %get-tuple-element.94), channel_id=1, source_target_pairs={{0,2},{2,0},{4,6},{6,4},{8,10},{10,8},{12,14},{14,12},{16,18},{18,... | collective-permute-start | bytes 86024 | tf_op jit(solution)/shard_map/ppermute | solution.py:24
  114.8 10.5 %collective-permute-start.29 = (bf16[16,896]{1,0:T(8,128)(2,1)S(1)}, bf16[16,896]{1,0:T(8,128)(2,1)S(1)}, u32[]{:S(2)}, u32[]{:S(2)}) collective-permute-start(bf16[16,896]{1,0:T(8,128)(2,1)S(1)} %get-tuple-element.93), channel_id=1, source_target_pairs={{0,2},{2,0},{4,6},{6,4},{8,10},{10,8},{12,14},{14,12},{16,18},{18,... | collective-permute-start | bytes 86024 | tf_op jit(solution)/shard_map/ppermute | solution.py:24
  122.9 3.9 %collective-permute-start.30 = (bf16[16,896]{1,0:T(8,128)(2,1)S(1)}, bf16[16,896]{1,0:T(8,128)(2,1)S(1)}, u32[]{:S(2)}, u32[]{:S(2)}) collective-permute-start(bf16[16,896]{1,0:T(8,128)(2,1)S(1)} %fusion.14), channel_id=1, source_target_pairs={{0,4},{2,6},{4,0},{6,2},{8,12},{10,14},{12,8},{14,10},{16,20},{18,... | collective-permute-start | bytes 86024 | tf_op jit(solution)/shard_map/ppermute | solution.py:24
  123.9 5.8 %collective-permute-start.28 = (bf16[1,16,6272]{2,1,0:T(8,128)(2,1)S(1)}, bf16[1,16,6272]{2,1,0:T(8,128)(2,1)S(1)}, u32[]{:S(2)}, u32[]{:S(2)}) collective-permute-start(bf16[1,16,6272]{2,1,0:T(8,128)(2,1)S(1)} %split.53), channel_id=1, source_target_pairs={{0,8},{2,10},{4,12},{6,14},{8,0},{10,2},{12,4},{14,6},{16,24},{18,... | collective-permute-start | bytes 602120 | tf_op jit(solution)/shard_map/ppermute | solution.py:24
  129.8 5.8 %collective-permute-start.31 = (bf16[1,8,7168]{2,1,0:T(8,128)(2,1)S(1)}, bf16[1,8,7168]{2,1,0:T(8,128)(2,1)S(1)}, u32[]{:S(2)}, u32[]{:S(2)}) collective-permute-start(bf16[1,8,7168]{2,1,0:T(8,128)(2,1)S(1)} %split.54), channel_id=1, source_target_pairs={{0,16},{2,18},{4,20},{6,22},{8,24},{10,26},{12,28},{14,30},{16,0},... | collective-permute-start | bytes 344072 | tf_op jit(solution)/shard_map/ppermute | solution.py:24
  (8 other events, 62.8 us)
